TPU v7x, 32 devices: a whole 2x2x4 slice. The times are simulated.
32 devices in a mesh: dp: 8 (over y, x, core), seq: 4 (over z).
Axes of the slice: x: 2, y: 2, z: 4, core: 2. Of those that a mesh axis runs over, the one named last changes fastest.
Arguments:
- tokens: bfloat16 [8, 1024, 1152], P('dp', 'seq'), may hold values from -4 to 4, as said below
- conditions: bfloat16 [8, 4, 1152], P('dp'), may hold values from -4 to 4, as said below
- segment_ids: int32 [8, 1024], P('dp'), may hold values from 0 to 3, never falling along the last dimension, each value on 1 to 770 neighbouring positions
- padding: int32 [8, 1024], P('dp'), may hold values 0 or 1
- targets: bfloat16 [8, 1024, 768], P('dp', 'seq'), may hold values from -6 to 6
- cotangent: float32 [8, 1024, 1152], P('dp', 'seq'), may hold values from -0.01953125 to 0.01953125
- tile_counts: int32 [32], replicated, may hold values from 1 to 612, as said below
- master: float32 [19584, 2048], P(('dp', 'seq')), may hold values from -2 to 2, as said below
- first_moment: float32 [19584, 2048], P(('dp', 'seq')), may hold values from -1.75 to 1.75
- second_moment: float32 [19584, 2048], P(('dp', 'seq')), may hold values from 0.013888889 to 0.055555556
Outputs:
- output: bfloat16 [8, 1024, 1152], P('dp', 'seq')
- grad_tokens: float32 [8, 1024, 1152], P('dp', 'seq')
- grad_conditions: float32 [8, 4, 1152], P('dp')
- new_master: float32 [19584, 2048], P(('dp', 'seq'))
- new_first: float32 [19584, 2048], P(('dp', 'seq'))
- new_second: float32 [19584, 2048], P(('dp', 'seq'))
Inputs may be any that keep to these rules, and one draw needn't show every extreme that they name: `tile_counts`: the counts sum to 15643 and one device owns exactly 612 tiles. `master`: each weight's entries of order its fan-in to the minus one half. `segment_ids`: in each row the ids never fall, each of the 4 images has 1 to 770 tokens, and one has exactly that many. `tokens`: entries of order one. `conditions`: entries of order one.
All inputs are finite; a program needn't handle non-finite values. No bound on the sum of `padding` on one device may be relied on, other than what follows from the above.
Results may differ from a plain program's by a relative error of at most 0.017.
Values may be sent and summed in bfloat16 or wider, within the bound.
A program may use at most 512 MiB of HBM per device.

v0:
```python
from functools import partial
import math

import jax
import jax.numpy as jnp
from jax import lax
from jax.sharding import PartitionSpec as P

HEADS = 16
HEAD_DIM = 72
D = 1152
FF = 4608
PROJ = 2048
TARGET = 768
SEGS = 4
STEP = 10
TILES = 15643


ln_eps = 1e-06
cos_eps = 1e-06
repa_weight = 0.5
beta_one = 0.5
beta_two = 0.5
learn_rate = 0.02
weight_decay = 0.01
adam_eps = 1e-08
highest = lax.Precision.HIGHEST


def param_shapes():
    return [
        (D, 6 * D),
        (6 * D,),
        (D, 3 * D),
        (D,),
        (D,),
        (D, D),
        (D,),
        (D, FF),
        (FF,),
        (FF, D),
        (D,),
        (D, PROJ),
        (PROJ,),
        (PROJ, PROJ),
        (PROJ,),
        (PROJ, TARGET),
        (TARGET,),
    ]


def param_offsets():
    starts = []
    offset = 0
    for dims in param_shapes():
        starts.append(offset)
        offset = offset + math.prod(dims)
    return starts


def unpack(flat):
    pieces = []
    offset = 0
    for dims in param_shapes():
        extent = math.prod(dims)
        pieces.append(flat[offset : offset + extent].reshape(dims))
        offset = offset + extent
    return pieces


def place(buffer, piece, index):
    return lax.dynamic_update_slice_in_dim(buffer, piece.reshape(-1), param_offsets()[index], 0)


def normalize(values):
    centred = values - jnp.mean(values, axis=-1, keepdims=True)
    spread = jnp.mean(centred * centred, axis=-1, keepdims=True)
    return centred * lax.rsqrt(spread + ln_eps)


def cosine_of(target, projected):
    inner_mean = jnp.mean(projected * target, axis=-1)
    return (
        inner_mean
        * lax.rsqrt(jnp.mean(projected * projected, axis=-1) + cos_eps)
        * lax.rsqrt(jnp.mean(target * target, axis=-1) + cos_eps)
    )


def gelu_tanh(values):
    return jax.nn.gelu(values, approximate=True)


def block_mask(seg_row, pad_row, start_row, block_len):
    full_len = seg_row.shape[0]
    query_seg = seg_row[start_row : start_row + block_len]
    query_pos = start_row + jnp.arange(block_len, dtype=jnp.int32)
    key_pos = jnp.arange(full_len, dtype=jnp.int32)
    same_image = query_seg[:, None] == seg_row[None, :]
    usable = (pad_row[None, :] == 1) | (query_pos[:, None] == key_pos[None, :])
    return same_image & usable


def attend_forward(queries, key_rows, values, seg_row, pad_row, block_len, scaling):
    out_parts = []
    lse_parts = []
    for start_row in range(0, queries.shape[0], block_len):
        allowed = block_mask(seg_row, pad_row, start_row, block_len)
        scores = (
            jnp.einsum(
                "qhe,khe->hqk",
                queries[start_row : start_row + block_len],
                key_rows,
                preferred_element_type=jnp.float32,
            )
            * scaling
        )
        scores = jnp.where(allowed[None], scores, -1e30)
        row_max = jnp.max(scores, axis=-1, keepdims=True)
        shifted = jnp.exp(scores - row_max)
        row_sum = jnp.sum(shifted, axis=-1, keepdims=True)
        probs_low = (shifted / row_sum).astype(jnp.bfloat16)
        out_parts.append(
            jnp.einsum("hqk,khe->qhe", probs_low, values, preferred_element_type=jnp.float32)
        )
        lse_parts.append(row_max[..., 0] + jnp.log(row_sum[..., 0]))
    return (jnp.concatenate(out_parts, 0), jnp.concatenate(lse_parts, 1))


def attend_backward(
    queries, key_rows, values, grad_out, row_lse, seg_row, pad_row, block_len, scaling
):
    grad_keys = jnp.zeros(key_rows.shape, jnp.float32)
    grad_values = jnp.zeros(values.shape, jnp.float32)
    query_parts = []
    for start_row in range(0, queries.shape[0], block_len):
        allowed = block_mask(seg_row, pad_row, start_row, block_len)
        query_block = queries[start_row : start_row + block_len]
        grad_block = grad_out[start_row : start_row + block_len]
        scores = (
            jnp.einsum("qhe,khe->hqk", query_block, key_rows, preferred_element_type=jnp.float32)
            * scaling
        )
        scores = jnp.where(allowed[None], scores, -1e30)
        probs = jnp.exp(scores - row_lse[:, start_row : start_row + block_len, None])
        probs_low = probs.astype(jnp.bfloat16)
        grad_probs = jnp.einsum(
            "qhe,khe->hqk", grad_block, values, preferred_element_type=jnp.float32
        )
        inner_sum = jnp.sum(probs * grad_probs, axis=-1, keepdims=True)
        grad_scores = (probs * (grad_probs - inner_sum)).astype(jnp.bfloat16)
        query_parts.append(
            jnp.einsum("hqk,khe->qhe", grad_scores, key_rows, preferred_element_type=jnp.float32)
            * scaling
        )
        grad_keys = (
            grad_keys
            + jnp.einsum(
                "hqk,qhe->khe", grad_scores, query_block, preferred_element_type=jnp.float32
            )
            * scaling
        )
        grad_values = grad_values + jnp.einsum(
            "hqk,qhe->khe", probs_low, grad_block, preferred_element_type=jnp.float32
        )
    return (jnp.concatenate(query_parts, 0), grad_keys, grad_values)


def shards(
    tokens,
    conditions,
    segment_ids,
    padding,
    targets,
    cotangent,
    tile_counts,
    master,
    first_moment,
    second_moment,
):
    seq_count = lax.axis_size("seq")
    data_count = lax.axis_size("dp")
    seq_place = lax.axis_index("seq")
    slot_count, tile_len = master.shape
    tile_ends = jnp.cumsum(tile_counts)
    tile_starts = tile_ends - tile_counts
    tile_ids = jnp.arange(TILES, dtype=jnp.int32)
    owner_of = jnp.sum((tile_ids[:, None] >= tile_ends[None, :]).astype(jnp.int32), axis=1)
    start_of = jnp.max(
        jnp.where(tile_ids[:, None] >= tile_starts[None, :], tile_starts[None, :], 0), axis=1
    )
    own_low = master.astype(jnp.bfloat16)
    gathered = lax.all_gather(own_low, ("dp", "seq"), axis=0, tiled=True)
    rows_for = owner_of * slot_count + tile_ids - start_of
    natural = jnp.take(gathered, rows_for, axis=0).reshape(-1)
    (
        mod_weight,
        mod_bias,
        attend_weight,
        query_bias,
        value_bias,
        output_weight,
        output_bias,
        hidden_weight,
        hidden_bias,
        return_weight,
        return_bias,
        proj_one,
        proj_bias_one,
        proj_two,
        proj_bias_two,
        proj_three,
        proj_bias_three,
    ) = unpack(natural)
    rows_dev, local_len, model_width = tokens.shape
    full_len = segment_ids.shape[1]
    heads_local = HEADS // seq_count
    group_width = model_width // seq_count
    scaling = HEAD_DIM ** (-0.5)
    block_len = min(512, full_len)
    own_start = seq_place * local_len
    local_seg = lax.dynamic_slice_in_dim(segment_ids, own_start, local_len, 1)
    local_pad = lax.dynamic_slice_in_dim(padding, own_start, local_len, 1).astype(jnp.float32)
    onehot = (local_seg[:, :, None] == jnp.arange(SEGS, dtype=jnp.int32)).astype(jnp.float32)
    cond_f = conditions.astype(jnp.float32)
    cond_act, silu_cond_back = jax.vjp(jax.nn.silu, cond_f)
    cond_low = cond_act.astype(jnp.bfloat16)
    modulation = (
        jnp.einsum("rsd,dc->rsc", cond_low, mod_weight, preferred_element_type=jnp.float32)
        + mod_bias
    )
    per_token = jnp.einsum("rts,rsc->rtc", onehot, modulation, precision=highest)
    shift_one, scale_one, gate_one, shift_two, scale_two, gate_two = jnp.split(
        per_token, 6, axis=-1
    )
    token_f = tokens.astype(jnp.float32)
    normed_one, norm_back_one = jax.vjp(normalize, token_f)
    attend_in = (normed_one * (1.0 + scale_one) + shift_one).astype(jnp.bfloat16)
    triple_bias = jnp.concatenate([query_bias, jnp.zeros_like(query_bias), value_bias])
    triple = (
        jnp.einsum("rtd,dc->rtc", attend_in, attend_weight, preferred_element_type=jnp.float32)
        + triple_bias
    )
    triple_low = triple.astype(jnp.bfloat16).reshape(rows_dev, local_len, 3, model_width)
    head_rows = lax.all_to_all(triple_low, "seq", split_axis=3, concat_axis=1, tiled=True)
    head_view = head_rows.reshape(rows_dev, full_len, 3, heads_local, HEAD_DIM)
    row_index = 0
    head_out, head_lse = attend_forward(
        head_view[row_index, :, 0],
        head_view[row_index, :, 1],
        head_view[row_index, :, 2],
        segment_ids[row_index],
        padding[row_index],
        block_len,
        scaling,
    )
    attended_parts = [head_out.astype(jnp.bfloat16).reshape(full_len, group_width)]
    lse_rows = [head_lse]
    head_attended = jnp.stack(attended_parts)
    attended = lax.all_to_all(head_attended, "seq", split_axis=1, concat_axis=2, tiled=True)
    branch_one = (
        jnp.einsum("rtd,dc->rtc", attended, output_weight, preferred_element_type=jnp.float32)
        + output_bias
    )
    middle = token_f + gate_one * branch_one
    normed_two, norm_back_two = jax.vjp(normalize, middle)
    mlp_in = (normed_two * (1.0 + scale_two) + shift_two).astype(jnp.bfloat16)
    hidden = (
        jnp.einsum("rtd,df->rtf", mlp_in, hidden_weight, preferred_element_type=jnp.float32)
        + hidden_bias
    )
    activated_f, gelu_back = jax.vjp(gelu_tanh, hidden)
    activated = activated_f.astype(jnp.bfloat16)
    branch_two = (
        jnp.einsum("rtf,fd->rtd", activated, return_weight, preferred_element_type=jnp.float32)
        + return_bias
    )
    result = middle + gate_two * branch_two
    feature = result.astype(jnp.bfloat16)
    first_pre = (
        jnp.einsum("rtd,dp->rtp", feature, proj_one, preferred_element_type=jnp.float32)
        + proj_bias_one
    )
    first_act, first_back = jax.vjp(jax.nn.silu, first_pre)
    first_low = first_act.astype(jnp.bfloat16)
    second_pre = (
        jnp.einsum("rtp,pc->rtc", first_low, proj_two, preferred_element_type=jnp.float32)
        + proj_bias_two
    )
    second_act, second_back = jax.vjp(jax.nn.silu, second_pre)
    second_low = second_act.astype(jnp.bfloat16)
    projected = (
        jnp.einsum("rtc,co->rto", second_low, proj_three, preferred_element_type=jnp.float32)
        + proj_bias_three
    )
    target_f = targets.astype(jnp.float32)
    cosine, cosine_back = jax.vjp(partial(cosine_of, target_f), projected)
    grad_buffer = jnp.zeros((TILES * tile_len,), jnp.float32)
    (grad_projected,) = cosine_back(local_pad * -repa_weight)
    grad_projected = grad_projected.astype(jnp.bfloat16)
    grad_buffer = place(
        grad_buffer,
        jnp.einsum("rtc,rto->co", second_low, grad_projected, preferred_element_type=jnp.float32),
        15,
    )
    grad_buffer = place(grad_buffer, jnp.sum(grad_projected.astype(jnp.float32), axis=(0, 1)), 16)
    (grad_second,) = second_back(
        jnp.einsum("rto,co->rtc", grad_projected, proj_three, preferred_element_type=jnp.float32)
    )
    grad_second = grad_second.astype(jnp.bfloat16)
    grad_buffer = place(
        grad_buffer,
        jnp.einsum("rtp,rtc->pc", first_low, grad_second, preferred_element_type=jnp.float32),
        13,
    )
    grad_buffer = place(grad_buffer, jnp.sum(grad_second.astype(jnp.float32), axis=(0, 1)), 14)
    (grad_first,) = first_back(
        jnp.einsum("rtc,pc->rtp", grad_second, proj_two, preferred_element_type=jnp.float32)
    )
    grad_first = grad_first.astype(jnp.bfloat16)
    grad_buffer = place(
        grad_buffer,
        jnp.einsum("rtd,rtp->dp", feature, grad_first, preferred_element_type=jnp.float32),
        11,
    )
    grad_buffer = place(grad_buffer, jnp.sum(grad_first.astype(jnp.float32), axis=(0, 1)), 12)
    grad_result = cotangent + jnp.einsum(
        "rtp,dp->rtd", grad_first, proj_one, preferred_element_type=jnp.float32
    )
    grad_gate_two = grad_result * branch_two
    grad_branch_two = (grad_result * gate_two).astype(jnp.bfloat16)
    grad_buffer = place(
        grad_buffer,
        jnp.einsum("rtf,rtd->fd", activated, grad_branch_two, preferred_element_type=jnp.float32),
        9,
    )
    grad_buffer = place(grad_buffer, jnp.sum(grad_branch_two.astype(jnp.float32), axis=(0, 1)), 10)
    (grad_hidden,) = gelu_back(
        jnp.einsum(
            "rtd,fd->rtf", grad_branch_two, return_weight, preferred_element_type=jnp.float32
        )
    )
    grad_hidden = grad_hidden.astype(jnp.bfloat16)
    grad_buffer = place(
        grad_buffer,
        jnp.einsum("rtd,rtf->df", mlp_in, grad_hidden, preferred_element_type=jnp.float32),
        7,
    )
    grad_buffer = place(grad_buffer, jnp.sum(grad_hidden.astype(jnp.float32), axis=(0, 1)), 8)
    grad_mlp_in = jnp.einsum(
        "rtf,df->rtd", grad_hidden, hidden_weight, preferred_element_type=jnp.float32
    )
    grad_scale_two = grad_mlp_in * normed_two
    (grad_through_two,) = norm_back_two(grad_mlp_in * (1.0 + scale_two))
    grad_middle = grad_result + grad_through_two
    grad_gate_one = grad_middle * branch_one
    grad_branch_one = (grad_middle * gate_one).astype(jnp.bfloat16)
    grad_buffer = place(
        grad_buffer,
        jnp.einsum("rtd,rtc->dc", attended, grad_branch_one, preferred_element_type=jnp.float32),
        5,
    )
    grad_buffer = place(grad_buffer, jnp.sum(grad_branch_one.astype(jnp.float32), axis=(0, 1)), 6)
    grad_attended = jnp.einsum(
        "rtc,dc->rtd", grad_branch_one, output_weight, preferred_element_type=jnp.float32
    ).astype(jnp.bfloat16)
    head_grad = lax.all_to_all(grad_attended, "seq", split_axis=2, concat_axis=1, tiled=True)
    row_index = 0
    grad_query, grad_key, grad_value = attend_backward(
        head_view[row_index, :, 0],
        head_view[row_index, :, 1],
        head_view[row_index, :, 2],
        head_grad[row_index].reshape(full_len, heads_local, HEAD_DIM),
        lse_rows[row_index],
        segment_ids[row_index],
        padding[row_index],
        block_len,
        scaling,
    )
    triple_parts = [
        jnp.stack([grad_query, grad_key, grad_value], 1).reshape(full_len, 3, group_width)
    ]
    grad_triple_heads = jnp.stack(triple_parts).astype(jnp.bfloat16)
    grad_triple = lax.all_to_all(
        grad_triple_heads, "seq", split_axis=1, concat_axis=3, tiled=True
    ).reshape(rows_dev, local_len, 3 * model_width)
    grad_buffer = place(
        grad_buffer,
        jnp.einsum("rtd,rtc->dc", attend_in, grad_triple, preferred_element_type=jnp.float32),
        2,
    )
    triple_sums = jnp.sum(grad_triple.astype(jnp.float32), axis=(0, 1))
    grad_buffer = place(grad_buffer, triple_sums[:model_width], 3)
    grad_buffer = place(grad_buffer, triple_sums[2 * model_width :], 4)
    grad_attend_in = jnp.einsum(
        "rtc,dc->rtd", grad_triple, attend_weight, preferred_element_type=jnp.float32
    )
    grad_scale_one = grad_attend_in * normed_one
    (grad_through_one,) = norm_back_one(grad_attend_in * (1.0 + scale_one))
    grad_tokens = grad_middle + grad_through_one
    token_mod_grad = jnp.concatenate(
        [grad_attend_in, grad_scale_one, grad_gate_one, grad_mlp_in, grad_scale_two, grad_gate_two],
        axis=-1,
    )
    mod_part = jnp.einsum("rts,rtc->rsc", onehot, token_mod_grad, precision=highest)
    mod_grad = lax.psum(mod_part.astype(jnp.bfloat16), "seq")
    first_share = (seq_place == 0).astype(jnp.float32)
    grad_buffer = place(
        grad_buffer,
        jnp.einsum("rsd,rsc->dc", cond_low, mod_grad, preferred_element_type=jnp.float32)
        * first_share,
        0,
    )
    grad_buffer = place(
        grad_buffer, jnp.sum(mod_grad.astype(jnp.float32), axis=(0, 1)) * first_share, 1
    )
    (grad_conditions,) = silu_cond_back(
        jnp.einsum("rsc,dc->rsd", mod_grad, mod_weight, preferred_element_type=jnp.float32)
    )
    grad_tiles = grad_buffer.reshape(TILES, tile_len)
    seq_ids = jnp.arange(seq_count, dtype=jnp.int32)[:, None, None]
    data_ids = jnp.arange(data_count, dtype=jnp.int32)[None, :, None]
    within_ids = jnp.arange(slot_count, dtype=jnp.int32)[None, None, :]
    device_ids = data_ids * seq_count + seq_ids
    slot_valid = within_ids < jnp.take(tile_counts, device_ids)
    slot_tile = jnp.where(slot_valid, jnp.take(tile_starts, device_ids) + within_ids, 0).reshape(-1)
    slot_valid = slot_valid.reshape(-1)
    width_part = tile_len // 4
    columns = []
    for piece_index in range(4):
        block = grad_tiles[:, piece_index * width_part : (piece_index + 1) * width_part]
        terms = jnp.where(slot_valid[:, None], jnp.take(block, slot_tile, axis=0), 0.0)
        terms = terms.reshape(seq_count, data_count * slot_count, width_part)
        arrived = lax.all_to_all(
            terms.astype(jnp.bfloat16), "seq", split_axis=0, concat_axis=0, tiled=True
        ).astype(terms.dtype)
        seq_summed = jnp.sum(arrived, axis=0)
        columns.append(
            lax.psum_scatter(
                seq_summed.astype(jnp.bfloat16), "dp", scatter_dimension=0, tiled=True
            ).astype(jnp.float32)
        )
    reduced = jnp.concatenate(columns, 1)
    new_first = beta_one * first_moment + (1.0 - beta_one) * reduced
    new_second = beta_two * second_moment + (1.0 - beta_two) * reduced * reduced
    corr_one = 1.0 - beta_one**STEP
    corr_two = 1.0 - beta_two**STEP
    new_master = master - learn_rate * (
        new_first / corr_one / (jnp.sqrt(new_second / corr_two) + adam_eps) + weight_decay * master
    )
    return (
        result.astype(jnp.bfloat16),
        grad_tokens,
        grad_conditions,
        new_master,
        new_first,
        new_second,
    )


def solution(mesh):
    return jax.shard_map(
        shards,
        mesh=mesh,
        in_specs=(
            P("dp", "seq", None),
            P("dp", None, None),
            P("dp", None),
            P("dp", None),
            P("dp", "seq", None),
            P("dp", "seq", None),
            P(),
            P(("dp", "seq"), None),
            P(("dp", "seq"), None),
            P(("dp", "seq"), None),
        ),
        out_specs=(
            P("dp", "seq", None),
            P("dp", "seq", None),
            P("dp", None, None),
            P(("dp", "seq"), None),
            P(("dp", "seq"), None),
            P(("dp", "seq"), None),
        ),
        check_vma=False,
    )
```

profile of v0, /device:TPU:1, one launch (start us, length us, event | category | flops | bytes accessed | tf_op | source)
XLA Modules:
  0.0 4807.7 jit_solution(14605227109396578208)
XLA Ops:
  20.9 414.8 %all-gather.3.cloned.1.call-done = bf16[32,612,2048]{2,1,0:T(8,128)(2,1)} async-done(((bf16[1,612,2048]{2,1,0:T(8,128)(2,1)}), bf16[32,612,2048]{2,1,0:T(8,128)(2,1)}) %all-gather.3.cloned.1.call-update) | async-done | bytes 80216080 | tf_op jit(solution)/shard_map/all_gather | solution.py:194
  435.7 90.2 %reshape.1016 = bf16[19584,2048]{1,0:T(8,128)(2,1)} reshape(bf16[32,612,2048]{2,1,0:T(8,128)(2,1)} %all-gather.3.cloned.1.call-done) | data formatting | bytes 160432128
  526.0 163.9 %gather_fusion = bf16[15643,2048]{1,0:T(8,128)(2,1)} fusion(bf16[19584,2048]{1,0:T(8,128)(2,1)} %reshape.1016, s32[16384]{0:T(1024)S(1)} %pad_clamp_fusion.1), kind=kCustom, calls=%fused_computation.6 | custom fusion | bytes 128210032 | tf_op jit(solution)/shard_map/jit(_take)/gather | solution.py:196
  689.8 42.1 broadcast_select_fusion
  731.9 13.4 slice.175
  745.3 94.9 %select_n.80 = bf16[32036864]{0:T(1024)(128)(2,1)} reshape(bf16[15643,2048]{1,0:T(8,128)(2,1)} %broadcast_select_fusion) | data formatting | bytes 128147456 | tf_op jit(solution)/shard_map/jit(_take)/select_n | solution.py:196
  841.6 7.6 slice.177
  849.2 25.9 reshape.920
  875.1 15.4 reshape.922
  890.5 7.7 convolution_add_fusion
  911.7 10.1 copy.90
  926.8 16.5 fusion.131
  949.1 7.6 slice.192
  964.4 20.4 reshape.929
  984.8 19.1 reshape.928
  1003.9 8.2 reshape.931
  1012.1 13.4 reshape.932
  1070.6 12.8 all-to-all-done.1
  1106.0 10.5 add_convert_fusion
  1136.9 10.3 convolution_bitcast_fusion.1
  1154.4 9.3 convert_reduce_fusion
  1163.6 9.4 fusion.82
  1173.1 8.3 multiply_reduce_fusion.2
  1181.4 8.7 fusion.137
  1206.8 7.0 reshape.940
  1213.8 15.0 copy.108
  1234.7 21.9 reshape.943
  1256.7 20.9 reshape.944
  1280.9 6.6 reshape.945
  1287.4 42.3 dynamic_update_slice.51
  1331.0 142.0 %dynamic_update_slice.53 = f32[32036864]{0:T(1024)} dynamic-update-slice(f32[32036864]{0:T(1024)} %constant_dynamic-update-slice_fusion.11, f32[4194304]{0:T(1024)} %bitcast.238, s32[]{:T(128)} %constant.50.clone.1) | dynamic-update-slice | bytes 33554436 | tf_op jit(solution)/shard_map/dynamic_update_slice | solution.py:73
  1474.4 80.6 %dynamic_update_slice.55 = f32[32036864]{0:T(1024)} dynamic-update-slice(f32[32036864]{0:T(1024)} %constant_dynamic-update-slice_fusion.10, f32[2359296]{0:T(1024)} %bitcast.243, s32[]{:T(128)} %constant.53.clone.1) | dynamic-update-slice | bytes 18874372 | tf_op jit(solution)/shard_map/dynamic_update_slice | solution.py:73
  1556.3 179.4 %dynamic_update_slice.57 = f32[32036864]{0:T(1024)} dynamic-update-slice(f32[32036864]{0:T(1024)} %constant_dynamic-update-slice_fusion.9, f32[5308416]{0:T(1024)} %reshape.943, s32[]{:T(128)} %constant.144.clone.1) | dynamic-update-slice | bytes 42467332 | tf_op jit(solution)/shard_map/dynamic_update_slice | solution.py:73
  1737.0 179.2 %dynamic_update_slice.59 = f32[32036864]{0:T(1024)} dynamic-update-slice(f32[32036864]{0:T(1024)} %constant_dynamic-update-slice_fusion.8, f32[5308416]{0:T(1024)} %reshape.944, s32[]{:T(128)} %constant.146.clone.1) | dynamic-update-slice | bytes 42467332 | tf_op jit(solution)/shard_map/dynamic_update_slice | solution.py:73
  1924.9 7.1 multiply_reduce_fusion
  1952.2 6.7 multiply_convert_fusion
  1973.3 8.5 pad_maximum_fusion
  1992.3 64.6 %all-to-all-done.3 = bf16[1,1024,3,288]{3,2,0,1:T(4,128)(2,1)} async-done(((bf16[1,1024,3,288]{3,2,0,1:T(4,128)(2,1)}), bf16[1,1024,3,288]{3,2,0,1:T(4,128)(2,1)}, u32[]{:S(2)}, u32[]{:S(2)}) %all-to-all-start.3) | async-done | bytes 1769504 | tf_op jit(solution)/shard_map/all_to_all | solution.py:385
  2069.1 8.0 fusion.138
  2085.0 13.4 psum.7
  2098.4 16.7 reshape.946
  2115.6 12.5 convolution_multiply_fusion
  2128.2 32.7 reshape.947
  2160.9 134.8 %dynamic_update_slice.63 = f32[32036864]{0:T(1024)} dynamic-update-slice(f32[32036864]{0:T(1024)} %constant_dynamic-update-slice_fusion.5, f32[3981312]{0:T(1024)} %reshape.946, s32[]{:T(128)} %constant.150.clone.1) | dynamic-update-slice | bytes 31850500 | tf_op jit(solution)/shard_map/dynamic_update_slice | solution.py:73
  2298.3 21.7 constant_dynamic-update-slice_fusion.2
  2321.4 104.0 %reshape.948 = bf16[15643,2048]{1,0:T(8,128)(2,1)} reshape(f32[32036864]{0:T(1024)} %multiply_dynamic-update-slice_fusion.3) | data formatting | bytes 192221184 | tf_op jit(solution)/shard_map/reshape | solution.py:421
  2425.4 43.0 fusion.130
  2468.4 63.6 %gather_fusion.3 = bf16[19584,512]{1,0:T(8,128)(2,1)} fusion(bf16[15643,512]{1,0:T(8,128)(2,1)} %get-tuple-element.38, s32[20480]{0:T(1024)S(1)} %copy-done.31), kind=kCustom, calls=%fused_computation.1.clone | custom fusion | bytes 40186368 | tf_op jit(solution)/shard_map/jit(_take)/gather | solution.py:433
  2532.0 63.7 %gather_fusion.4 = bf16[19584,512]{1,0:T(8,128)(2,1)} fusion(bf16[15643,512]{1,0:T(8,128)(2,1)} %get-tuple-element.41, s32[20480]{0:T(1024)S(1)} %copy-done.31), kind=kCustom, calls=%fused_computation.3.clone | custom fusion | bytes 40186368 | tf_op jit(solution)/shard_map/jit(_take)/gather | solution.py:433
  2595.7 63.6 %gather_fusion.5 = bf16[19584,512]{1,0:T(8,128)(2,1)} fusion(bf16[15643,512]{1,0:T(8,128)(2,1)} %get-tuple-element.40, s32[20480]{0:T(1024)S(1)} %copy-done.31), kind=kCustom, calls=%fused_computation.4.clone | custom fusion | bytes 40186368 | tf_op jit(solution)/shard_map/jit(_take)/gather | solution.py:433
  2659.3 63.6 %gather_fusion.6 = bf16[19584,512]{1,0:T(8,128)(2,1)} fusion(bf16[15643,512]{1,0:T(8,128)(2,1)} %get-tuple-element.39, s32[20480]{0:T(1024)S(1)} %copy-done.31), kind=kCustom, calls=%fused_computation.5.clone | custom fusion | bytes 40186368 | tf_op jit(solution)/shard_map/jit(_take)/gather | solution.py:433
  2722.9 63.1 %fusion.7 = (bf16[19584,512]{1,0:T(8,128)(2,1)}, bf16[19584,512]{1,0:T(8,128)(2,1)}, bf16[19584,512]{1,0:T(8,128)(2,1)}, bf16[19584,512]{1,0:T(8,128)(2,1)}) fusion(bf16[19584,512]{1,0:T(8,128)(2,1)} %gather_fusion.3, pred[19584]{0:T(1024)(128)(4,1)S(1)} %copy-done.48, pred[19584]{0:T(1024)(128)(4,1)S(1)} %copy-done.42, bf16[19584,512]{1,0:T(8,128)(2,1)} %gather_fusion.4, ...), kind=kLoop, calls=%fused_computation.15 | loop fusion | flops 80216064 | bytes 160471296 | tf_op jit(solution)/shard_map/convert_element_type | solution.py:436
  2786.0 445.4 %all_to_all.80 = bf16[4,4896,512]{2,1,0:T(8,128)(2,1)} all-to-all(bf16[4,4896,512]{2,1,0:T(8,128)(2,1)} %bitcast.237), channel_id=1, replica_groups=mesh['dp'=8,'seq'=4] {'seq'}, dimensions={0} | all-to-all | bytes 40108032 | tf_op jit(solution)/shard_map/all_to_all | solution.py:435
  3231.4 436.9 %all_to_all.81 = bf16[4,4896,512]{2,1,0:T(8,128)(2,1)} all-to-all(bf16[4,4896,512]{2,1,0:T(8,128)(2,1)S(1)} %bitcast.236), channel_id=1, replica_groups=mesh['dp'=8,'seq'=4] {'seq'}, dimensions={0} | all-to-all | bytes 40108032 | tf_op jit(solution)/shard_map/all_to_all | solution.py:435
  3668.4 436.5 %all_to_all.82 = bf16[4,4896,512]{2,1,0:T(8,128)(2,1)} all-to-all(bf16[4,4896,512]{2,1,0:T(8,128)(2,1)S(1)} %bitcast.233), channel_id=1, replica_groups=mesh['dp'=8,'seq'=4] {'seq'}, dimensions={0} | all-to-all | bytes 40108032 | tf_op jit(solution)/shard_map/all_to_all | solution.py:435
  4104.9 7.9 all-to-all-start.4
  4114.0 17.4 reduce_sum.307
  4131.4 17.4 reduce_sum.306
  4148.8 17.4 reduce_sum.305
  4166.2 379.2 %all-to-all-done.4 = bf16[4,4896,512]{2,1,0:T(8,128)(2,1)} async-done(((bf16[4,4896,512]{2,1,0:T(8,128)(2,1)}), bf16[4,4896,512]{2,1,0:T(8,128)(2,1)}, u32[]{:S(2)}, u32[]{:S(2)}) %all-to-all-start.4) | async-done | bytes 20054048 | tf_op jit(solution)/shard_map/all_to_all | solution.py:435
  4545.4 17.4 reduce_sum.304
  4562.7 196.0 %fusion.123 = (bf16[616,512]{1,0:T(8,128)(2,1)S(1)}, bf16[616,512]{1,0:T(8,128)(2,1)S(1)}, bf16[616,512]{1,0:T(8,128)(2,1)S(1)}, bf16[616,512]{1,0:T(8,128)(2,1)S(1)}) fusion(bf16[4896,512]{1,0:T(8,128)(2,1)} %reduce_sum.307, bf16[4896,512]{1,0:T(8,128)(2,1)} %reduce_sum.306, bf16[4896,512]{1,0:T(8,128)(2,1)} %reduce_sum.305, bf16[4896,512]{1,0:T(8,128)(2,1)} %reduce_sum.304), kind=kCustom, calls=%all-reduce-scatter.4 | all-reduce-scatter fusion | flops 10092545 | bytes 22577664
  4763.2 10.4 fusion.108
  4789.3 11.1 multiply_subtract_fusion
  (375 shorter events, 271.5 us)
Async XLA Ops:
  7.2 428.6 %all-gather.3.cloned.1.call-start = ((), (), s32[]{:S(2)}) async-start(), calls=%async_computation.8 | async-start | bytes 83263488 | tf_op jit(solution)/shard_map/all_gather | solution.py:194
  13.8 512.2 %copy-start.41 = (pred[19584]{0:T(1024)(128)(4,1)}, pred[19584]{0:T(1024)(128)(4,1)S(1)}, u32[]{:S(2)}) copy-start(pred[19584]{0:T(1024)(128)(4,1)S(1)} %lt.71) | copy-start | bytes 58756
  15.9 510.0 %copy-start.57 = (f32[256]{0:T(256)}, f32[256]{0:T(256)S(1)}, u32[]{:S(2)}) copy-start(f32[256]{0:T(256)S(1)} %broadcast_multiply_fusion.3) | copy-start | bytes 3076
  16.2 509.7 %copy-start.65 = (f32[256]{0:T(256)}, f32[256]{0:T(256)S(1)}, u32[]{:S(2)}) copy-start(f32[256]{0:T(256)S(1)} %fusion.66) | copy-start | bytes 3076
  526.0 163.9 %copy-start.49 = (pred[15643]{0:T(1024)(128)(4,1)S(1)}, pred[15643]{0:T(1024)(128)(4,1)}, u32[]{:S(2)}) copy-start(pred[15643]{0:T(1024)(128)(4,1)} %compare_and_fusion.1) | copy-start | bytes 46933
  875.1 15.4 copy-start.45
  921.8 111.3 %all-to-all-start = ((bf16[1,256,3,1152]{1,2,0,3:T(4,128)(2,1)}), bf16[1,256,3,1152]{1,2,0,3:T(4,128)(2,1)}, u32[]{:S(2)}, u32[]{:S(2)}) async-start(bf16[1,256,3,1152]{1,2,0,3:T(4,128)(2,1)} %copy.90), calls=%async_computation | async-start | bytes 4718592 | tf_op jit(solution)/shard_map/all_to_all | solution.py:246
  1033.1 7.9 copy-start.40
  1041.0 9.9 copy-start.9
  1063.5 19.9 all-to-all-start.1
  1086.0 13.1 slice-start.13
  1098.8 91.3 %copy-start.4 = (f32[1,256,1152]{2,1,0:T(8,128)}, f32[1,256,1152]{2,1,0:T(8,128)S(1)}, u32[]{:S(2)}) copy-start(f32[1,256,1152]{2,1,0:T(8,128)S(1)} %get-tuple-element.37) | copy-start | bytes 3538948
  1098.8 91.3 %copy-start.54 = (f32[256]{0:T(256)}, f32[256]{0:T(256)S(1)}, u32[]{:S(2)}) copy-start(f32[256]{0:T(256)S(1)} %broadcast_multiply_fusion.2) | copy-start | bytes 3076
  1099.1 91.0 %copy-start.61 = (f32[256]{0:T(256)}, f32[256]{0:T(256)S(1)}, u32[]{:S(2)}) copy-start(f32[256]{0:T(256)S(1)} %fusion.120) | copy-start | bytes 3076
  1099.5 17.0 slice-start.18
  1099.5 18.6 slice-start.20
  1106.0 10.5 copy-start.20
  1106.0 10.5 slice-start.19
  1106.0 10.5 copy-start.67
  1106.0 12.1 slice-start.21
  1136.9 10.3 copy-start.38
  1136.9 17.5 slice-start.22
  1154.4 36.3 copy-start.13
  1173.1 8.3 copy-start.29
  1181.4 8.8 copy-start.11
  1202.9 714.7 %all-to-all-start.2 = ((bf16[4,2,36864]{2,1,0:T(2,128)(2,1)}), bf16[4,2,36864]{2,1,0:T(2,128)(2,1)S(1)}, u32[]{:S(2)}, u32[]{:S(2)}) async-start(bf16[4,2,36864]{2,1,0:T(2,128)(2,1)} %reshape.1042), calls=%async_computation.2 | async-start | bytes 1179648 | tf_op jit(solution)/shard_map/all_to_all | solution.py:368
  1206.8 22.0 slice-start.15
  1213.8 15.1 slice-start.16
  1213.8 15.1 slice-start.17
  1256.7 20.9 copy-start.18
  1287.4 42.3 copy-start.60
  1331.0 142.1 %copy-start.69 = (f32[2048]{0:T(1024)S(1)}, f32[2048]{0:T(1024)}, u32[]{:S(2)}) copy-start(f32[2048]{0:T(1024)} %get-tuple-element.88) | copy-start | bytes 24580
  1474.4 80.6 %copy-start.68 = (f32[2048]{0:T(1024)S(1)}, f32[2048]{0:T(1024)}, u32[]{:S(2)}) copy-start(f32[2048]{0:T(1024)} %get-tuple-element.28) | copy-start | bytes 24580
  1556.3 179.4 %copy-start.53 = (f32[1152]{0:T(1024)S(1)}, f32[1152]{0:T(1024)}, u32[]{:S(2)}) copy-start(f32[1152]{0:T(1024)} %get-tuple-element.26) | copy-start | bytes 13828
  1932.5 12.6 slice-start.1
  1962.8 10.5 copy-start.19
  1981.9 75.1 %all-to-all-start.3 = ((bf16[1,1024,3,288]{3,2,0,1:T(4,128)(2,1)}), bf16[1,1024,3,288]{3,2,0,1:T(4,128)(2,1)}, u32[]{:S(2)}, u32[]{:S(2)}) async-start(bf16[1,1024,3,288]{3,2,0,1:T(4,128)(2,1)} %pad_maximum_fusion), calls=%async_computation.3 | async-start | bytes 6291456 | tf_op jit(solution)/shard_map/all_to_all | solution.py:385
  1990.9 71.8 %copy-start.8 = (bf16[1,256,1152]{2,1,0:T(8,128)(2,1)S(1)}, bf16[1,256,1152]{2,1,0:T(8,128)(2,1)}, u32[]{:S(2)}) copy-start(bf16[1,256,1152]{2,1,0:T(8,128)(2,1)} %param.14) | copy-start | bytes 1769476
  1991.0 71.8 %copy-start.59 = (f32[256]{0:T(256)S(1)}, f32[256]{0:T(256)}, u32[]{:S(2)}) copy-start(f32[256]{0:T(256)} %copy-done.57) | copy-start | bytes 3076
  2069.1 9.0 copy-start.66
  2069.1 9.0 copy-start.64
  2098.4 17.2 copy-start.35
  2098.4 17.2 copy-start.46
  2425.4 43.0 copy-start.31
  2659.3 63.6 %copy-start.42 = (pred[19584]{0:T(1024)(128)(4,1)S(1)}, pred[19584]{0:T(1024)(128)(4,1)}, u32[]{:S(2)}) copy-start(pred[19584]{0:T(1024)(128)(4,1)} %copy-done.41) | copy-start | bytes 58756
  2659.3 63.6 %copy-start.48 = (pred[19584]{0:T(1024)(128)(4,1)S(1)}, pred[19584]{0:T(1024)(128)(4,1)}, u32[]{:S(2)}) copy-start(pred[19584]{0:T(1024)(128)(4,1)} %get-tuple-element.21) | copy-start | bytes 58756
  2785.9 445.4 %slice-start.8 = ((s8[20054016]{0:T(1024)(128)(4,1)}), s8[4194304]{0:T(1024)(128)(4,1)S(1)}, s32[]{:S(2)}) async-start(s8[20054016]{0:T(1024)(128)(4,1)} %bitcast.234), calls=%async_computation.17 | async-start | bytes 8388608
  2785.9 445.4 %slice-start.9 = ((s8[20054016]{0:T(1024)(128)(4,1)}), s8[4194304]{0:T(1024)(128)(4,1)S(1)}, s32[]{:S(2)}) async-start(s8[20054016]{0:T(1024)(128)(4,1)} %bitcast.234), calls=%async_computation.18 | async-start | bytes 8388608
  2785.9 445.4 %slice-start.10 = ((s8[20054016]{0:T(1024)(128)(4,1)}), s8[4194304]{0:T(1024)(128)(4,1)S(1)}, s32[]{:S(2)}) async-start(s8[20054016]{0:T(1024)(128)(4,1)} %bitcast.234), calls=%async_computation.19 | async-start | bytes 8388608
  2785.9 445.4 %slice-start.11 = ((s8[20054016]{0:T(1024)(128)(4,1)}), s8[4194304]{0:T(1024)(128)(4,1)S(1)}, s32[]{:S(2)}) async-start(s8[20054016]{0:T(1024)(128)(4,1)} %bitcast.234), calls=%async_computation.20 | async-start | bytes 8388608
  2786.0 445.4 %slice-start.12 = ((s8[20054016]{0:T(1024)(128)(4,1)}), s8[3276800]{0:T(1024)(128)(4,1)S(1)}, s32[]{:S(2)}) async-start(s8[20054016]{0:T(1024)(128)(4,1)} %bitcast.234), calls=%async_computation.21 | async-start | bytes 6553600
  3231.3 437.0 %slice-start.3 = ((s8[20054016]{0:T(1024)(128)(4,1)}), s8[4194304]{0:T(1024)(128)(4,1)S(1)}, s32[]{:S(2)}) async-start(s8[20054016]{0:T(1024)(128)(4,1)} %bitcast.231), calls=%async_computation.12 | async-start | bytes 8388608
  3231.4 436.9 %slice-start.4 = ((s8[20054016]{0:T(1024)(128)(4,1)}), s8[4194304]{0:T(1024)(128)(4,1)S(1)}, s32[]{:S(2)}) async-start(s8[20054016]{0:T(1024)(128)(4,1)} %bitcast.231), calls=%async_computation.13 | async-start | bytes 8388608
  3231.4 436.9 %slice-start.5 = ((s8[20054016]{0:T(1024)(128)(4,1)}), s8[4194304]{0:T(1024)(128)(4,1)S(1)}, s32[]{:S(2)}) async-start(s8[20054016]{0:T(1024)(128)(4,1)} %bitcast.231), calls=%async_computation.14 | async-start | bytes 8388608
  3231.4 436.9 %slice-start.6 = ((s8[20054016]{0:T(1024)(128)(4,1)}), s8[4194304]{0:T(1024)(128)(4,1)S(1)}, s32[]{:S(2)}) async-start(s8[20054016]{0:T(1024)(128)(4,1)} %bitcast.231), calls=%async_computation.15 | async-start | bytes 8388608
  3231.4 436.9 %slice-start.7 = ((s8[20054016]{0:T(1024)(128)(4,1)}), s8[3276800]{0:T(1024)(128)(4,1)S(1)}, s32[]{:S(2)}) async-start(s8[20054016]{0:T(1024)(128)(4,1)} %bitcast.231), calls=%async_computation.16 | async-start | bytes 6553600
  4104.9 7.9 copy-start.71
  4104.9 440.5 %all-to-all-start.4 = ((bf16[4,4896,512]{2,1,0:T(8,128)(2,1)}), bf16[4,4896,512]{2,1,0:T(8,128)(2,1)}, u32[]{:S(2)}, u32[]{:S(2)}) async-start(bf16[4,4896,512]{2,1,0:T(8,128)(2,1)} %bitcast.230), calls=%async_computation.4 | async-start | bytes 40108032 | tf_op jit(solution)/shard_map/all_to_all | solution.py:435
  4562.7 200.4 %copy-start.36 = (bf16[1,4,6912]{2,1,0:T(4,128)(2,1)S(1)}, bf16[1,4,6912]{2,1,0:T(4,128)(2,1)}, u32[]{:S(2)}) copy-start(bf16[1,4,6912]{2,1,0:T(4,128)(2,1)} %copy-done.35) | copy-start | bytes 165892
  4562.7 200.4 %copy-start.47 = (bf16[1,4,1152]{2,1,0:T(4,128)(2,1)S(1)}, bf16[1,4,1152]{2,1,0:T(4,128)(2,1)}, u32[]{:S(2)}) copy-start(bf16[1,4,1152]{2,1,0:T(4,128)(2,1)} %param.15) | copy-start | bytes 27652
  4758.7 22.9 collective-permute-start.3
  4773.5 10.4 collective-permute-start.2
  4775.5 10.5 collective-permute-start.1
  4779.7 8.4 collective-permute-start
  (42 other events, 163.2 us)
Sparse Core Ops, SparseCore 0:
  11.7 424.0 all-gather.2
where the time goes:
time: 4880 us; the launch traced here: 4810 us
  local copies, waits for them, and re-layouts  1920 us (39%)
  blocking collectives  1530 us (31%)
  waiting for transfers between devices  871 us (18%)
  other arithmetic  251 us (5%)
  matrix products  187 us (4%)
    all_to_all x3, blocking collectives, shards(): lax.all_to_all(terms.astype(jnp.bfloat16), 'seq', split_axis=0, concat_ax...  1320 us
    dynamic_update_slice x16, local copies, waits for them, and re-layouts, place(): lax.dynamic_update_slice_in_dim(buffer, piece.reshape(-1), param_offsets(...  795 us
    all_gather x1, waiting for transfers between devices, shards(): gathered = lax.all_gather(own_low, ('dp', 'seq'), axis=0, tiled=True)  415 us
    all_to_all x1, waiting for transfers between devices, shards(): lax.all_to_all(terms.astype(jnp.bfloat16), 'seq', split_axis=0, concat_ax...  379 us
    gather x4, local copies, waits for them, and re-layouts, shards(): jnp.take(block, slot_tile, axis=0)  254 us
    unnamed x1, blocking collectives  196 us
    gather x1, local copies, waits for them, and re-layouts, shards(): natural = jnp.take(gathered, rows_for, axis=0).reshape(-1)  164 us
    unnamed x213, local copies, waits for them, and re-layouts  131 us
  transfers between devices with their start and end apart: 10, of which 4 were waited for; matrix products, arithmetic and copies ran while one was open for 19% of the time, Pallas kernels for 0%

commit v1 on v0

--- a/solution.py
+++ b/solution.py
@@ -4,6 +4,8 @@
 import jax
 import jax.numpy as jnp
 from jax import lax
+from jax.experimental import pallas as pl
+from jax.experimental.pallas import tpu as pltpu
 from jax.sharding import PartitionSpec as P
 
 HEADS = 16
@@ -26,6 +28,13 @@
 weight_decay = 0.01
 adam_eps = 1e-08
 highest = lax.Precision.HIGHEST
+
+
+LANES = 128
+SUBS = 16
+MOD_ROWS = (D + 1) * 6 * D // LANES
+VMEM_LIMIT = 56 * 1024 * 1024
+MESH = pl.DeviceIdType.MESH
 
 
 def param_shapes():
@@ -50,27 +59,849 @@
     ]
 
 
-def param_offsets():
+def param_rows():
     starts = []
-    offset = 0
+    row = 0
     for dims in param_shapes():
-        starts.append(offset)
-        offset = offset + math.prod(dims)
+        starts.append(row)
+        row = row + math.prod(dims) // LANES
     return starts
 
 
-def unpack(flat):
-    pieces = []
-    offset = 0
-    for dims in param_shapes():
-        extent = math.prod(dims)
-        pieces.append(flat[offset : offset + extent].reshape(dims))
-        offset = offset + extent
-    return pieces
-
-
-def place(buffer, piece, index):
-    return lax.dynamic_update_slice_in_dim(buffer, piece.reshape(-1), param_offsets()[index], 0)
+CHUNK = {0: 128, 2: 128, 5: 384, 7: 128, 9: 512, 11: 384, 13: 256, 15: 1024}
+EDGE_TILES = [3888, 3889, 3890, 3891, 5835, 5836, 6484, 6485, 9077, 9078, 9079, 11671, 12823, 12824, 14872, 14873, 15641, 15642]
+
+
+def chunk_spans():
+    spans = []
+    base = {}
+    rows = param_rows()
+    for index, chunk in CHUNK.items():
+        depth, width = param_shapes()[index]
+        per_chunk = chunk * width // LANES // SUBS
+        extra = 1 if rows[index] % SUBS else 0
+        base[index] = len(spans)
+        for step in range(depth // chunk):
+            first = rows[index] // SUBS + step * per_chunk
+            spans.append((first, first + per_chunk + extra - 1))
+    return spans, base
+
+
+def unpack_body(base, first_tile, per_chunk, tiles, shift, chunk, col_blocks, slots,
+                first_ref, last_ref, starts_ref, packed, out_ref, landed, wide, sems):
+    step = pl.program_id(0)
+
+    def fetch(which, slot):
+        low_tile = first_tile + which * per_chunk
+
+        def one(owner, carry):
+            begin = jnp.maximum(starts_ref[owner], low_tile)
+            end = jnp.minimum(starts_ref[owner + 1], low_tile + tiles)
+            size = pl.multiple_of((end - begin) * SUBS, SUBS)
+            origin = pl.multiple_of((owner * slots + begin - starts_ref[owner]) * SUBS, SUBS)
+            target = pl.multiple_of((begin - low_tile) * SUBS, SUBS)
+            pltpu.make_async_copy(
+                packed.at[pl.ds(origin, size)], landed.at[slot, pl.ds(target, size)], sems.at[slot]
+            ).start()
+            return carry
+
+        lax.fori_loop(first_ref[base + which], last_ref[base + which] + 1, one, 0)
+
+    @pl.when(step == 0)
+    def _():
+        fetch(0, 0)
+
+    slot = step % 2
+
+    @pl.when(step + 1 < pl.num_programs(0))
+    def _():
+        fetch(step + 1, (step + 1) % 2)
+
+    pltpu.make_async_copy(packed.at[pl.ds(0, tiles * SUBS)], landed.at[slot], sems.at[slot]).wait()
+    wide[...] = landed[slot].astype(jnp.float32)
+    for block in range(col_blocks):
+        out_ref[:, block * LANES : (block + 1) * LANES] = wide[
+            pl.ds(shift + block, chunk, stride=col_blocks), :
+        ].astype(jnp.bfloat16)
+
+
+def unpack_weight(index, packed, slots, firsts, lasts, starts):
+    depth, width = param_shapes()[index]
+    chunk = CHUNK[index]
+    col_blocks = width // LANES
+    row = param_rows()[index]
+    shift = row % SUBS
+    per_chunk = chunk * col_blocks // SUBS
+    tiles = per_chunk + (1 if shift else 0)
+    base = chunk_spans()[1][index]
+    return pl.pallas_call(
+        partial(unpack_body, base, row // SUBS, per_chunk, tiles, shift, chunk, col_blocks, slots),
+        out_shape=jax.ShapeDtypeStruct((depth, width), jnp.bfloat16),
+        grid_spec=pltpu.PrefetchScalarGridSpec(
+            num_scalar_prefetch=3,
+            grid=(depth // chunk,),
+            in_specs=[pl.BlockSpec(memory_space=pl.ANY)],
+            out_specs=pl.BlockSpec((chunk, width), lambda i, *_: (i, 0)),
+            scratch_shapes=[
+                pltpu.VMEM((2, tiles * SUBS, LANES), jnp.bfloat16),
+                pltpu.VMEM((tiles * SUBS, LANES), jnp.float32),
+                pltpu.SemaphoreType.DMA((2,)),
+            ],
+        ),
+        compiler_params=pltpu.CompilerParams(vmem_limit_bytes=VMEM_LIMIT),
+        cost_estimate=pl.CostEstimate(flops=0, bytes_accessed=depth * width * 4, transcendentals=0),
+        name="unpack_%d" % index,
+    )(firsts, lasts, starts, packed)
+
+
+def edge_read_body(table_ref, packed, out_ref, sem):
+    count = out_ref.shape[0] // SUBS
+
+    def one(i, carry):
+        origin = pl.multiple_of(table_ref[i] * SUBS, SUBS)
+        target = pl.multiple_of(i * SUBS, SUBS)
+        pltpu.make_async_copy(packed.at[pl.ds(origin, SUBS)], out_ref.at[pl.ds(target, SUBS)], sem).start()
+        return carry
+
+    lax.fori_loop(0, count, one, 0)
+    pltpu.make_async_copy(packed.at[pl.ds(0, count * SUBS)], out_ref, sem).wait()
+
+
+def edge_read(packed, table):
+    return pl.pallas_call(
+        edge_read_body,
+        out_shape=jax.ShapeDtypeStruct((len(EDGE_TILES) * SUBS, LANES), jnp.bfloat16),
+        grid_spec=pltpu.PrefetchScalarGridSpec(
+            num_scalar_prefetch=1,
+            grid=(1,),
+            in_specs=[pl.BlockSpec(memory_space=pl.ANY)],
+            out_specs=pl.BlockSpec(memory_space=pltpu.VMEM),
+            scratch_shapes=[pltpu.SemaphoreType.DMA],
+        ),
+        name="edge_read",
+    )(table, packed)
+
+
+def edge_write_body(layout, table_ref, *refs):
+    pieces = refs[: len(layout)]
+    out, wide, narrow, sem = refs[len(layout) + 1 :]
+    wide[...] = jnp.zeros_like(wide)
+    at = 0
+    for piece, (skip, low, high) in zip(pieces, layout):
+        at = at + skip
+        wide[at : at + high - low, :] = piece[low:high, :]
+        at = at + high - low
+    narrow[...] = wide[...].astype(jnp.bfloat16)
+    count = narrow.shape[0] // SUBS
+
+    def one(i, carry):
+        origin = pl.multiple_of(i * SUBS, SUBS)
+        target = pl.multiple_of(table_ref[i] * SUBS, SUBS)
+        pltpu.make_async_copy(narrow.at[pl.ds(origin, SUBS)], out.at[pl.ds(target, SUBS)], sem).start()
+        return carry
+
+    lax.fori_loop(0, count, one, 0)
+    pltpu.make_async_copy(narrow, out.at[pl.ds(0, count * SUBS)], sem).wait()
+
+
+def edge_write(pieces, buffer, table):
+    count = table.shape[0]
+    layout = [(skip, low, high) for skip, _, low, high in pieces]
+    arrays = [array for _, array, _, _ in pieces]
+    return pl.pallas_call(
+        partial(edge_write_body, layout),
+        out_shape=jax.ShapeDtypeStruct(buffer.shape, buffer.dtype),
+        grid_spec=pltpu.PrefetchScalarGridSpec(
+            num_scalar_prefetch=1,
+            grid=(1,),
+            in_specs=[pl.BlockSpec(memory_space=pltpu.VMEM)] * len(arrays)
+            + [pl.BlockSpec(memory_space=pl.ANY)],
+            out_specs=pl.BlockSpec(memory_space=pl.ANY),
+            scratch_shapes=[
+                pltpu.VMEM((count * SUBS, LANES), jnp.float32),
+                pltpu.VMEM((count * SUBS, LANES), jnp.bfloat16),
+                pltpu.SemaphoreType.DMA,
+            ],
+        ),
+        input_output_aliases={1 + len(arrays): 0},
+        name="edge_write",
+    )(table, *arrays, buffer)
+
+
+def weight_grad_body(base, first_tile, per_chunk, shift, chunk, col_blocks, slots, piece, chained,
+                     first_ref, last_ref, starts_ref, x_ref, dy_ref, *rest):
+    if chained:
+        rest = rest[1:]
+    out, ends_ref, wide, narrow, sems = rest
+    step = pl.program_id(0)
+    steps = pl.num_programs(0)
+    slot = step % 2
+    rows = chunk * col_blocks
+
+    def drain(which):
+        pltpu.make_async_copy(narrow.at[which], out.at[pl.ds(0, rows)], sems.at[which]).wait()
+
+    @pl.when(step == 0)
+    def _():
+        wide[...] = jnp.zeros_like(wide)
+
+    if shift:
+        @pl.when(step > 0)
+        def _():
+            wide[0:SUBS, :] = wide[rows : rows + SUBS, :]
+
+    left = x_ref[...].T
+    for start in range(0, col_blocks, piece):
+        part = jnp.dot(
+            left, dy_ref[:, start * LANES : (start + piece) * LANES], preferred_element_type=jnp.float32
+        )
+        for block in range(piece):
+            wide[pl.ds(shift + start + block, chunk, stride=col_blocks), :] = part[
+                :, block * LANES : (block + 1) * LANES
+            ]
+
+    @pl.when(step >= 2)
+    def _():
+        drain(slot)
+
+    narrow[slot] = wide[0:rows, :].astype(jnp.bfloat16)
+
+    @pl.when(step == 0)
+    def _():
+        ends_ref[0:SUBS, :] = wide[0:SUBS, :]
+
+    if shift:
+        @pl.when(step == steps - 1)
+        def _():
+            ends_ref[SUBS : 2 * SUBS, :] = wide[rows : rows + SUBS, :]
+    else:
+        ends_ref[SUBS : 2 * SUBS, :] = jnp.zeros((SUBS, LANES), jnp.float32)
+
+    low_tile = first_tile + step * per_chunk
+
+    def one(owner, carry):
+        begin = jnp.maximum(starts_ref[owner], low_tile)
+        end = jnp.minimum(starts_ref[owner + 1], low_tile + per_chunk)
+        size = pl.multiple_of(jnp.maximum(end - begin, 0) * SUBS, SUBS)
+        target = pl.multiple_of((owner * slots + begin - starts_ref[owner]) * SUBS, SUBS)
+        origin = pl.multiple_of((begin - low_tile) * SUBS, SUBS)
+
+        @pl.when(end > begin)
+        def _():
+            pltpu.make_async_copy(
+                narrow.at[slot, pl.ds(origin, size)], out.at[pl.ds(target, size)], sems.at[slot]
+            ).start()
+
+        return carry
+
+    lax.fori_loop(first_ref[base + step], last_ref[base + step] + 1, one, 0)
+
+    @pl.when(step == steps - 1)
+    def _():
+        drain(slot)
+
+        @pl.when(steps > 1)
+        def _():
+            drain(1 - slot)
+
+
+def weight_grad(index, left, right, buffer, owners, slots, firsts, lasts, starts):
+    depth, width = param_shapes()[index]
+    tokens = left.shape[0]
+    chunk = CHUNK[index]
+    col_blocks = width // LANES
+    piece = next(p for p in (9, 8, 6) if col_blocks % p == 0)
+    row = param_rows()[index]
+    shift = row % SUBS
+    per_chunk = chunk * col_blocks // SUBS
+    base = chunk_spans()[1][index]
+    shape = (owners * slots * SUBS, LANES)
+    in_specs = [
+        pl.BlockSpec((tokens, chunk), lambda i, *_: (0, i)),
+        pl.BlockSpec((tokens, width), lambda i, *_: (0, 0)),
+    ]
+    operands = [firsts, lasts, starts, left, right]
+    aliases = {}
+    if buffer is not None:
+        in_specs.append(pl.BlockSpec(memory_space=pl.ANY))
+        operands.append(buffer)
+        aliases = {5: 0}
+    return pl.pallas_call(
+        partial(weight_grad_body, base, row // SUBS, per_chunk, shift, chunk, col_blocks, slots, piece,
+                buffer is not None),
+        out_shape=(
+            jax.ShapeDtypeStruct(shape, jnp.bfloat16),
+            jax.ShapeDtypeStruct((2 * SUBS, LANES), jnp.float32),
+        ),
+        grid_spec=pltpu.PrefetchScalarGridSpec(
+            num_scalar_prefetch=3,
+            grid=(depth // chunk,),
+            in_specs=in_specs,
+            out_specs=(
+                pl.BlockSpec(memory_space=pl.ANY),
+                pl.BlockSpec((2 * SUBS, LANES), lambda i, *_: (0, 0)),
+            ),
+            scratch_shapes=[
+                pltpu.VMEM((chunk * col_blocks + SUBS, LANES), jnp.float32),
+                pltpu.VMEM((2, chunk * col_blocks, LANES), jnp.bfloat16),
+                pltpu.SemaphoreType.DMA((2,)),
+            ],
+        ),
+        input_output_aliases=aliases,
+        compiler_params=pltpu.CompilerParams(vmem_limit_bytes=VMEM_LIMIT),
+        cost_estimate=pl.CostEstimate(
+            flops=2 * tokens * depth * width, bytes_accessed=depth * width * 2, transcendentals=0
+        ),
+        name="weight_grad_%d" % index,
+    )(*operands)
+
+
+class Grid:
+    def __init__(self, side, depth):
+        self.side = side
+        self.sizes = {"u": side, "v": side, "z": depth}
+        self.place = lax.axis_index("dp")
+        self.core = self.place % 2
+        outer = self.place // 2 // side
+        inner = self.place // 2 % side
+        self.mine = {
+            "u": jnp.where(self.core == 0, outer, inner),
+            "v": jnp.where(self.core == 0, inner, outer),
+            "z": lax.axis_index("seq"),
+        }
+        self.sibling = (
+            self.place + 1 - 2 * self.core,
+            self.mine["z"],
+        )
+
+    def dp_of(self, first, second, core):
+        outer = jnp.where(core == 0, first, second)
+        inner = jnp.where(core == 0, second, first)
+        return (outer * self.side + inner) * 2 + core
+
+    def device(self, axis, other):
+        at = dict(self.mine)
+        at[axis] = other
+        return (self.dp_of(at["u"], at["v"], self.core), at["z"])
+
+    def other(self, axis, k):
+        return k + (k >= self.mine[axis]).astype(jnp.int32)
+
+    def seat(self, axis, other):
+        mine = self.mine[axis]
+        return mine - (mine > other).astype(jnp.int32)
+
+    def partners(self):
+        found = [self.sibling]
+        for axis in ("u", "v", "z"):
+            for k in range(self.sizes[axis] - 1):
+                found.append(self.device(axis, self.other(axis, k)))
+        return found
+
+    def greet(self):
+        barrier = pltpu.get_barrier_semaphore()
+        partners = self.partners()
+        for partner in partners:
+            pl.semaphore_signal(barrier, inc=1, device_id=partner, device_id_type=MESH)
+        pl.semaphore_wait(barrier, len(partners))
+
+
+def split_slots(slots, shards):
+    room = 32 * 1024 * 1024 // ((HELD + 2 * SLOTS) * shards * SUBS * LANES * 2)
+    part = max(p for p in range(2, 19) if slots % p == 0 and p <= max(room, 2))
+    late = max(1, round(part * 0.37))
+    return slots // part, (part - late, late)
+
+
+ORDERS = (("u", "v", "z"), ("u", "z", "v"))
+LAG = 2
+SLOTS = 4
+HELD = 4 * LAG + 1
+
+
+def gather_stream(grid, order, first_row, span, steps, own_ref, out_ref, sems):
+    (send_a, recv_a, send_b, recv_b, send_c, recv_c, send_d, recv_d) = sems
+    mine = grid.mine
+    side = grid.side
+    near, mid, far = order[2], order[1], order[0]
+
+    def rows(q):
+        return pl.ds(pl.multiple_of(first_row + q * span, SUBS), span)
+
+    def copy(source, target, send, recv, device):
+        return pltpu.make_async_remote_copy(
+            src_ref=source, dst_ref=target, send_sem=send, recv_sem=recv, device_id=device,
+            device_id_type=MESH,
+        )
+
+    def one_a(q, axis, k):
+        other = grid.other(axis, k)
+        mine_dp = grid.dp_of(mine["u"], mine["v"], grid.core)
+        return copy(
+            own_ref.at[rows(q)], out_ref.at[mine_dp, mine["z"], rows(q)],
+            send_a.at[q % 4, k], recv_a.at[q, grid.seat(axis, other)],
+            grid.device(axis, other),
+        )
+
+    def wait_a(q, axis, k):
+        dp = grid.dp_of(mine["u"], mine["v"], grid.core)
+        copy(
+            own_ref.at[rows(q)], out_ref.at[dp, mine["z"], rows(q)],
+            send_a.at[q % 4, k], recv_a.at[q, k], grid.device(axis, grid.other(axis, k)),
+        ).wait_recv()
+
+    def many_b(q, axis, k):
+        other = grid.other(axis, k)
+        seat = grid.seat(axis, other)
+        if axis == "v":
+            at = out_ref.at[grid.dp_of(mine["u"], mine["v"], grid.core), :, rows(q)]
+            return [copy(at, at, send_b.at[q % 4, k], recv_b.at[q, seat], grid.device(axis, other))]
+        found = []
+        for v in range(side):
+            at = out_ref.at[grid.dp_of(mine["u"], v, grid.core), mine["z"], rows(q)]
+            found.append(copy(at, at, send_b.at[q % 4, k], recv_b.at[q, seat], grid.device(axis, other)))
+        return found
+
+    def many_c(q, k):
+        other = grid.other("u", k)
+        seat = grid.seat("u", other)
+        found = []
+        for v in range(side):
+            at = out_ref.at[grid.dp_of(mine["u"], v, grid.core), :, rows(q)]
+            found.append(copy(at, at, send_c.at[q % 4, k], recv_c.at[q, seat], grid.device("u", other)))
+        return found
+
+    def many_d(q):
+        found = []
+        for u in range(side):
+            for v in range(side):
+                at = out_ref.at[grid.dp_of(u, v, grid.core), :, rows(q)]
+                found.append(copy(at, at, send_d.at[q % 4], recv_d.at[q], grid.sibling))
+        return found
+
+    def bulk(q, count, send, recv, device):
+        at = out_ref.at[pl.ds(0, count), :, rows(q)]
+        return copy(at, at, send, recv, device)
+
+    def bulk_b(q, axis, send, recv):
+        if axis == "v":
+            at = out_ref.at[0, :, rows(q)]
+        else:
+            at = out_ref.at[pl.ds(0, side), 0, rows(q)]
+        return copy(at, at, send, recv, grid.sibling)
+
+    far_count = grid.sizes[near] - 1
+    mid_count = grid.sizes[mid] - 1
+
+    def stage_d(q):
+        bulk(q, side, send_c.at[q % 4, 0], recv_c.at[q, 0], grid.sibling).wait_recv()
+        for k in range(1, side - 1):
+            bulk(q, side, send_c.at[q % 4, k], recv_c.at[q, k], grid.sibling).wait_recv()
+        for k in range(side - 1):
+            bulk(q, side, send_c.at[q % 4, k], recv_c.at[q, k], grid.sibling).wait_send()
+        for one in many_d(q):
+            one.start()
+
+    def stage_c(q):
+        for k in range(mid_count):
+            bulk_b(q, mid, send_b.at[q % 4, k], recv_b.at[q, k]).wait_recv()
+        for k in range(mid_count):
+            bulk_b(q, mid, send_b.at[q % 4, k], recv_b.at[q, k]).wait_send()
+        for k in range(side - 1):
+            for one in many_c(q, k):
+                one.start()
+
+    def stage_b(q):
+        for k in range(far_count):
+            wait_a(q, near, k)
+        for k in range(far_count):
+            one_a(q, near, k).wait_send()
+        for k in range(mid_count):
+            for one in many_b(q, mid, k):
+                one.start()
+
+    def stage_a(q):
+        for k in range(far_count):
+            one_a(q, near, k).start()
+
+    def finish(q):
+        whole = bulk(q, side * side, send_d.at[q % 4], recv_d.at[q], grid.sibling)
+        whole.wait_recv()
+        whole.wait_send()
+
+    return (stage_a, stage_b, stage_c, stage_d, finish)
+
+
+def gather_body(side, depth, steps, parts, own_ref, out_ref, own_sem, *sems):
+    grid = Grid(side, depth)
+    keep = pltpu.make_async_copy(
+        own_ref, out_ref.at[grid.dp_of(grid.mine["u"], grid.mine["v"], grid.core), grid.mine["z"]], own_sem
+    )
+    keep.start()
+    grid.greet()
+    streams = []
+    first = 0
+    for number, (order, part) in enumerate(zip(ORDERS, parts)):
+        span = part * SUBS
+        streams.append(
+            gather_stream(grid, order, first, span, steps, own_ref, out_ref, sems[8 * number : 8 * number + 8])
+        )
+        first = first + steps * span
+    keep.wait()
+
+    def round_trip(s, carry):
+        for late in range(4, -1, -1):
+            q = s - LAG * late
+
+            @pl.when((q >= 0) & (q < steps))
+            def _(late=late, q=q):
+                for stream in streams:
+                    stream[late](q)
+
+        return carry
+
+    lax.fori_loop(0, steps + 4 * LAG, round_trip, 0)
+
+
+def gather_slots(own, slots, data_count, seq_count):
+    side = math.isqrt(data_count // 2)
+    steps, parts = split_slots(slots, side * side * seq_count)
+    dma = pltpu.SemaphoreType.DMA
+    sems = []
+    for order in ORDERS:
+        sizes = {"u": side - 1, "v": side - 1, "z": seq_count - 1}
+        for axis in (order[2], order[1], order[0]):
+            sems.append(dma((4, sizes[axis])))
+            sems.append(dma((steps, sizes[axis])))
+        sems.append(dma((4,)))
+        sems.append(dma((steps,)))
+    return pl.pallas_call(
+        partial(gather_body, side, seq_count, steps, parts),
+        out_shape=jax.ShapeDtypeStruct((data_count, seq_count, slots * SUBS, LANES), jnp.bfloat16),
+        in_specs=[pl.BlockSpec(memory_space=pl.ANY)],
+        out_specs=pl.BlockSpec(memory_space=pl.ANY),
+        scratch_shapes=[dma] + sems,
+        compiler_params=pltpu.CompilerParams(
+            collective_id=2, has_side_effects=True, vmem_limit_bytes=VMEM_LIMIT
+        ),
+        name="gather_slots",
+    )(own).reshape(data_count * seq_count * slots * SUBS, LANES)
+
+
+def reduce_stream(grid, order, first_row, span, steps, parts_ref, out_ref, refs):
+    (own, rc, r1, r2, r3, outs, own_sem, out_sem, c_send, c_recv, s1, v1, s2, v2, s3, v3,
+     c_credit, k1, k2, k3) = refs
+    mine = grid.mine
+    side = grid.side
+    held = own.shape[0]
+    mu, mv, mz = mine["u"], mine["v"], mine["z"]
+
+    def rows(q):
+        return pl.ds(pl.multiple_of(first_row + q * span, SUBS), span)
+
+    def load(q, u, v):
+        return pltpu.make_async_copy(
+            parts_ref.at[grid.dp_of(u, v, grid.core), :, rows(q)], own.at[q % held, u, v], own_sem.at[q % held, u, v]
+        )
+
+    def give(q, u, v):
+        return pltpu.make_async_remote_copy(
+            src_ref=parts_ref.at[grid.dp_of(u, v, 1 - grid.core), :, rows(q)],
+            dst_ref=rc.at[q % SLOTS, u, v],
+            send_sem=c_send.at[q % SLOTS, u, v],
+            recv_sem=c_recv.at[q % SLOTS, u, v],
+            device_id=grid.sibling,
+            device_id_type=MESH,
+        )
+
+    def block(q, stage, other):
+        if stage == 0:
+            return own.at[q % held, other]
+        if order[1] == "v":
+            return own.at[q % held, mu, other] if stage == 1 else own.at[q % held, mu, mv, other]
+        return own.at[q % held, mu, :, other] if stage == 1 else own.at[q % held, mu, other, mz]
+
+    landing = (r1, r2, r3)
+    sends = (s1, s2, s3)
+    arrivals = (v1, v2, v3)
+    credits = (k1, k2, k3)
+
+    def send(q, stage, k):
+        axis = order[stage]
+        other = grid.other(axis, k)
+        seat = grid.seat(axis, other)
+        return pltpu.make_async_remote_copy(
+            src_ref=block(q, stage, other),
+            dst_ref=landing[stage].at[q % SLOTS, seat],
+            send_sem=sends[stage].at[q % SLOTS, k],
+            recv_sem=arrivals[stage].at[q % SLOTS, seat],
+            device_id=grid.device(axis, other),
+            device_id_type=MESH,
+        )
+
+    def receive(q, stage, k):
+        axis = order[stage]
+        return pltpu.make_async_remote_copy(
+            src_ref=block(q, stage, 0),
+            dst_ref=landing[stage].at[q % SLOTS, k],
+            send_sem=sends[stage].at[q % SLOTS, k],
+            recv_sem=arrivals[stage].at[q % SLOTS, k],
+            device_id=grid.device(axis, grid.other(axis, k)),
+            device_id_type=MESH,
+        )
+
+    def write(q):
+        return pltpu.make_async_copy(outs.at[q % 2], out_ref.at[rows(q)], out_sem.at[q % 2])
+
+    def collect(q, stage):
+        axis = order[stage]
+        count = grid.sizes[axis] - 1
+        for k in range(count):
+            receive(q, stage, k).wait_recv()
+        kept = block(q, stage, mine[axis])
+        total = kept[...].astype(jnp.float32)
+        for k in range(count):
+            total = total + landing[stage][q % SLOTS, k].astype(jnp.float32)
+        if stage < 2:
+            kept[...] = total.astype(jnp.bfloat16)
+        else:
+            @pl.when(q >= 2)
+            def _():
+                write(q - 2).wait()
+
+            outs[q % 2] = total.astype(jnp.bfloat16)
+            write(q).start()
+        for k in range(count):
+            send(q, stage, k).wait_send()
+
+        @pl.when(q + SLOTS < steps)
+        def _():
+            for k in range(count):
+                pl.semaphore_signal(
+                    credits[stage].at[mine[axis]], inc=1, device_id=grid.device(axis, grid.other(axis, k)),
+                    device_id_type=MESH,
+                )
+
+    def launch(q, stage):
+        axis = order[stage]
+        count = grid.sizes[axis] - 1
+
+        @pl.when(q >= SLOTS)
+        def _():
+            for k in range(count):
+                pl.semaphore_wait(credits[stage].at[grid.other(axis, k)], 1)
+
+        for k in range(count):
+            send(q, stage, k).start()
+
+    def begin(q):
+        @pl.when(q >= SLOTS)
+        def _():
+            pl.semaphore_wait(c_credit, 1)
+
+        for u in range(side):
+            for v in range(side):
+                give(q, u, v).start()
+                load(q, u, v).start()
+
+    def stage_c(q):
+        for u in range(side):
+            for v in range(side):
+                load(q, u, v).wait()
+                give(q, u, v).wait_recv()
+                own[q % held, u, v] = (
+                    own[q % held, u, v].astype(jnp.float32) + rc[q % SLOTS, u, v].astype(jnp.float32)
+                ).astype(jnp.bfloat16)
+        for u in range(side):
+            for v in range(side):
+                give(q, u, v).wait_send()
+
+        @pl.when(q + SLOTS < steps)
+        def _():
+            pl.semaphore_signal(c_credit, inc=1, device_id=grid.sibling, device_id_type=MESH)
+
+        launch(q, 0)
+
+    def stage_one(q):
+        collect(q, 0)
+        launch(q, 1)
+
+    def stage_two(q):
+        collect(q, 1)
+        launch(q, 2)
+
+    def stage_three(q):
+        collect(q, 2)
+
+    return (begin, stage_c, stage_one, stage_two, stage_three), write
+
+
+REDUCE_REFS = 20
+
+
+def reduce_body(side, depth, steps, parts, parts_ref, out_ref, *refs):
+    grid = Grid(side, depth)
+    grid.greet()
+    streams = []
+    writes = []
+    first = 0
+    for number, (order, part) in enumerate(zip(ORDERS, parts)):
+        span = part * SUBS
+        stages, write = reduce_stream(
+            grid, order, first, span, steps, parts_ref, out_ref,
+            refs[REDUCE_REFS * number : REDUCE_REFS * (number + 1)],
+        )
+        streams.append(stages)
+        writes.append(write)
+        first = first + steps * span
+
+    def round_trip(s, carry):
+        for late in range(4, -1, -1):
+            q = s - LAG * late
+
+            @pl.when((q >= 0) & (q < steps))
+            def _(late=late, q=q):
+                for stream in streams:
+                    stream[late](q)
+
+        return carry
+
+    lax.fori_loop(0, steps + 4 * LAG, round_trip, 0)
+    for write in writes:
+        for q in range(max(steps - 2, 0), steps):
+            write(q).wait()
+
+
+def reduce_slots(grads, slots, data_count, seq_count):
+    side = math.isqrt(data_count // 2)
+    steps, parts = split_slots(slots, side * side * seq_count)
+    held = HELD
+    dma = pltpu.SemaphoreType.DMA
+    regular = pltpu.SemaphoreType.REGULAR
+    bf16 = jnp.bfloat16
+    scratch = []
+    for order, part in zip(ORDERS, parts):
+        span = part * SUBS
+        sizes = {"u": side, "v": side, "z": seq_count}
+        left = dict(sizes)
+        scratch.append(pltpu.VMEM((held, side, side, seq_count, span, LANES), bf16))
+        scratch.append(pltpu.VMEM((SLOTS, side, side, seq_count, span, LANES), bf16))
+        for axis in order:
+            del left[axis]
+            rest = tuple(left[name] for name in ("u", "v", "z") if name in left)
+            scratch.append(pltpu.VMEM((SLOTS, sizes[axis] - 1) + rest + (span, LANES), bf16))
+        scratch.append(pltpu.VMEM((2, span, LANES), bf16))
+        scratch.append(dma((held, side, side)))
+        scratch.append(dma((2,)))
+        scratch.append(dma((SLOTS, side, side)))
+        scratch.append(dma((SLOTS, side, side)))
+        for axis in order:
+            scratch.append(dma((SLOTS, sizes[axis] - 1)))
+            scratch.append(dma((SLOTS, sizes[axis] - 1)))
+        scratch.append(regular)
+        for axis in order:
+            scratch.append(regular((sizes[axis],)))
+    return pl.pallas_call(
+        partial(reduce_body, side, seq_count, steps, parts),
+        out_shape=jax.ShapeDtypeStruct((slots * SUBS, LANES), bf16),
+        in_specs=[pl.BlockSpec(memory_space=pl.ANY)],
+        out_specs=pl.BlockSpec(memory_space=pl.ANY),
+        scratch_shapes=scratch,
+        compiler_params=pltpu.CompilerParams(
+            collective_id=1, has_side_effects=True, vmem_limit_bytes=VMEM_LIMIT
+        ),
+        name="reduce_slots",
+    )(grads.reshape(data_count, seq_count, slots * SUBS, LANES))
+
+
+UPDATE_TILES = 72
+
+
+def update_body(mod_depth, own_ref, reduced, cond_ref, mod_ref, master, first, second,
+                new_master, new_first, new_second, mod_rows, wide):
+    step = pl.program_id(0)
+    mod_blocks = 6 * D // LANES
+    start_row = own_ref[0] * SUBS
+    shift = lax.rem(start_row, mod_blocks)
+    tiles = UPDATE_TILES
+    piece = 9
+
+    @pl.when((step == 0) & (start_row < MOD_ROWS))
+    def _():
+        for begin in range(0, mod_blocks, piece):
+            part = jnp.dot(
+                cond_ref[...], mod_ref[:, begin * LANES : (begin + piece) * LANES],
+                preferred_element_type=jnp.float32,
+            )
+            for block in range(piece):
+                mod_rows[pl.ds(begin + block, mod_depth, stride=mod_blocks), :] = part[
+                    :, block * LANES : (block + 1) * LANES
+                ]
+
+    wide[...] = reduced[...].astype(jnp.float32)
+    corr_one = 1.0 - beta_one**STEP
+    corr_two = 1.0 - beta_two**STEP
+    local = step * tiles + lax.broadcasted_iota(jnp.int32, (tiles, LANES), 0)
+    used = local < own_ref[1]
+    for sub in range(SUBS):
+        columns = pl.ds(sub * LANES, LANES)
+        from_mod = mod_rows[pl.ds(shift + step * tiles * SUBS + sub, tiles, stride=SUBS), :]
+        is_mod = start_row + local * SUBS + sub < MOD_ROWS
+        grad = jnp.where(is_mod, from_mod, wide[pl.ds(sub, tiles, stride=SUBS), :])
+        grad = jnp.where(used, grad, 0.0)
+        one = beta_one * first[:, columns] + (1.0 - beta_one) * grad
+        two = beta_two * second[:, columns] + (1.0 - beta_two) * grad * grad
+        held = master[:, columns]
+        new_first[:, columns] = one
+        new_second[:, columns] = two
+        new_master[:, columns] = held - learn_rate * (
+            one / corr_one / (jnp.sqrt(two / corr_two) + adam_eps) + weight_decay * held
+        )
+
+
+def update(reduced, cond_all, mod_all, own_first, master, first, second):
+    slots, tile_len = master.shape
+    images = cond_all.shape[0]
+    tiles = UPDATE_TILES
+    steps = -(-slots // tiles)
+    mod_blocks = 6 * D // LANES
+    mod_depth = -(-(steps * tiles * SUBS + mod_blocks) // mod_blocks)
+    mod_depth = -(-mod_depth // 8) * 8
+    extended = jnp.concatenate(
+        [
+            cond_all.T,
+            jnp.ones((1, images), jnp.bfloat16),
+            jnp.zeros((mod_depth, images), jnp.bfloat16),
+        ],
+        axis=0,
+    )
+    cond_own = lax.dynamic_slice_in_dim(
+        extended, jnp.minimum(own_first[0] * SUBS // mod_blocks, D + 1), mod_depth, 0
+    )
+    wide_block = pl.BlockSpec((tiles, tile_len), lambda i, *_: (i, 0))
+    return pl.pallas_call(
+        partial(update_body, mod_depth),
+        out_shape=(jax.ShapeDtypeStruct(master.shape, jnp.float32),) * 3,
+        grid_spec=pltpu.PrefetchScalarGridSpec(
+            num_scalar_prefetch=1,
+            grid=(steps,),
+            in_specs=[
+                pl.BlockSpec((tiles * SUBS, LANES), lambda i, *_: (i, 0)),
+                pl.BlockSpec((mod_depth, images), lambda i, *_: (0, 0)),
+                pl.BlockSpec((images, 6 * D), lambda i, *_: (0, 0)),
+                wide_block,
+                wide_block,
+                wide_block,
+            ],
+            out_specs=(wide_block,) * 3,
+            scratch_shapes=[
+                pltpu.VMEM((mod_depth * mod_blocks, LANES), jnp.float32),
+                pltpu.VMEM((tiles * SUBS, LANES), jnp.float32),
+            ],
+        ),
+        compiler_params=pltpu.CompilerParams(vmem_limit_bytes=VMEM_LIMIT),
+        name="update",
+    )(own_first, reduced, cond_own, mod_all, master, first, second)
 
 
 def normalize(values):
@@ -182,54 +1013,63 @@
     seq_count = lax.axis_size("seq")
     data_count = lax.axis_size("dp")
     seq_place = lax.axis_index("seq")
+    data_place = lax.axis_index("dp")
+    owners = data_count * seq_count
     slot_count, tile_len = master.shape
+    own_rows = slot_count * SUBS
     tile_ends = jnp.cumsum(tile_counts)
-    tile_starts = tile_ends - tile_counts
-    tile_ids = jnp.arange(TILES, dtype=jnp.int32)
-    owner_of = jnp.sum((tile_ids[:, None] >= tile_ends[None, :]).astype(jnp.int32), axis=1)
-    start_of = jnp.max(
-        jnp.where(tile_ids[:, None] >= tile_starts[None, :], tile_starts[None, :], 0), axis=1
-    )
-    own_low = master.astype(jnp.bfloat16)
-    gathered = lax.all_gather(own_low, ("dp", "seq"), axis=0, tiled=True)
-    rows_for = owner_of * slot_count + tile_ids - start_of
-    natural = jnp.take(gathered, rows_for, axis=0).reshape(-1)
-    (
-        mod_weight,
-        mod_bias,
-        attend_weight,
-        query_bias,
-        value_bias,
-        output_weight,
-        output_bias,
-        hidden_weight,
-        hidden_bias,
-        return_weight,
-        return_bias,
-        proj_one,
-        proj_bias_one,
-        proj_two,
-        proj_bias_two,
-        proj_three,
-        proj_bias_three,
-    ) = unpack(natural)
+    starts = jnp.concatenate([jnp.zeros((1,), jnp.int32), tile_ends.astype(jnp.int32)])
+    spans = jnp.asarray(chunk_spans()[0], jnp.int32)
+    firsts = jnp.sum((tile_ends[None, :] <= spans[:, :1]).astype(jnp.int32), axis=1)
+    lasts = jnp.sum((tile_ends[None, :] <= spans[:, 1:]).astype(jnp.int32), axis=1)
+    edge_ids = jnp.asarray(EDGE_TILES, jnp.int32)
+    edge_owner = jnp.sum((tile_ends[None, :] <= edge_ids[:, None]).astype(jnp.int32), axis=1)
+    edge_slots = edge_owner * slot_count + edge_ids - jnp.take(starts, edge_owner)
+    own_place = data_place * seq_count + seq_place
+    own_start = lax.dynamic_index_in_dim(starts, own_place, 0, False)
+    own_count = lax.dynamic_index_in_dim(tile_counts, own_place, 0, False)
+    own_low = master.astype(jnp.bfloat16).reshape(own_rows, LANES)
+    packed = gather_slots(own_low, slot_count, data_count, seq_count)
+
+    mod_blocks = 6 * D // LANES
+    own_first = jnp.stack([own_start, own_count])
+    cond_f = conditions.astype(jnp.float32)
+    cond_act, silu_cond_back = jax.vjp(jax.nn.silu, cond_f)
+    cond_low = cond_act.astype(jnp.bfloat16)
+    cond_all = lax.all_gather(cond_low, "dp", axis=0, tiled=True)
+    image_rows = cond_all.shape[0]
+    cond_all = cond_all.reshape(image_rows * SEGS, D)
+
+    weights = {
+        index: unpack_weight(index, packed, slot_count, firsts, lasts, starts) for index in CHUNK
+    }
+    mod_weight, attend_weight, output_weight, hidden_weight, return_weight, proj_one, proj_two, proj_three = (
+        weights[index] for index in (0, 2, 5, 7, 9, 11, 13, 15)
+    )
+    edges = edge_read(packed, edge_slots)
+    edge_flat = edges.reshape(-1)
+
+    def bias(index):
+        row = param_rows()[index]
+        at = EDGE_TILES.index(row // SUBS) * SUBS + row % SUBS
+        return edge_flat[at * LANES : at * LANES + param_shapes()[index][0]]
+
+    mod_bias = bias(1)
+    modulation = (
+        jnp.einsum("rsd,dc->rsc", cond_low, mod_weight, preferred_element_type=jnp.float32) + mod_bias
+    )
+    query_bias, value_bias, output_bias, hidden_bias, return_bias = (bias(i) for i in (3, 4, 6, 8, 10))
+    proj_bias_one, proj_bias_two, proj_bias_three = (bias(i) for i in (12, 14, 16))
     rows_dev, local_len, model_width = tokens.shape
     full_len = segment_ids.shape[1]
     heads_local = HEADS // seq_count
     group_width = model_width // seq_count
     scaling = HEAD_DIM ** (-0.5)
     block_len = min(512, full_len)
-    own_start = seq_place * local_len
-    local_seg = lax.dynamic_slice_in_dim(segment_ids, own_start, local_len, 1)
-    local_pad = lax.dynamic_slice_in_dim(padding, own_start, local_len, 1).astype(jnp.float32)
+    token_start = seq_place * local_len
+    local_seg = lax.dynamic_slice_in_dim(segment_ids, token_start, local_len, 1)
+    local_pad = lax.dynamic_slice_in_dim(padding, token_start, local_len, 1).astype(jnp.float32)
     onehot = (local_seg[:, :, None] == jnp.arange(SEGS, dtype=jnp.int32)).astype(jnp.float32)
-    cond_f = conditions.astype(jnp.float32)
-    cond_act, silu_cond_back = jax.vjp(jax.nn.silu, cond_f)
-    cond_low = cond_act.astype(jnp.bfloat16)
-    modulation = (
-        jnp.einsum("rsd,dc->rsc", cond_low, mod_weight, preferred_element_type=jnp.float32)
-        + mod_bias
-    )
     per_token = jnp.einsum("rts,rsc->rtc", onehot, modulation, precision=highest)
     shift_one, scale_one, gate_one, shift_two, scale_two, gate_two = jnp.split(
         per_token, 6, axis=-1
@@ -244,6 +1084,11 @@
     )
     triple_low = triple.astype(jnp.bfloat16).reshape(rows_dev, local_len, 3, model_width)
     head_rows = lax.all_to_all(triple_low, "seq", split_axis=3, concat_axis=1, tiled=True)
+    (head_rows, output_weight, hidden_weight, return_weight, proj_one, proj_two, proj_three) = (
+        lax.optimization_barrier(
+            (head_rows, output_weight, hidden_weight, return_weight, proj_one, proj_two, proj_three)
+        )
+    )
     head_view = head_rows.reshape(rows_dev, full_len, 3, heads_local, HEAD_DIM)
     row_index = 0
     head_out, head_lse = attend_forward(
@@ -296,58 +1141,56 @@
     )
     target_f = targets.astype(jnp.float32)
     cosine, cosine_back = jax.vjp(partial(cosine_of, target_f), projected)
-    grad_buffer = jnp.zeros((TILES * tile_len,), jnp.float32)
+    ends = {}
+
+    def put(buffer, index, left, right):
+        buffer, ends[index] = weight_grad(
+            index,
+            left.reshape(-1, left.shape[-1]),
+            right.reshape(-1, right.shape[-1]),
+            buffer,
+            owners,
+            slot_count,
+            firsts,
+            lasts,
+            starts,
+        )
+        return buffer
+
+    def summed(grad):
+        return jnp.sum(grad.astype(jnp.float32), axis=(0, 1))
+
     (grad_projected,) = cosine_back(local_pad * -repa_weight)
     grad_projected = grad_projected.astype(jnp.bfloat16)
-    grad_buffer = place(
-        grad_buffer,
-        jnp.einsum("rtc,rto->co", second_low, grad_projected, preferred_element_type=jnp.float32),
-        15,
-    )
-    grad_buffer = place(grad_buffer, jnp.sum(grad_projected.astype(jnp.float32), axis=(0, 1)), 16)
+    grad_buffer = put(None, 15, second_low, grad_projected)
+    sum_sixteen = summed(grad_projected)
     (grad_second,) = second_back(
         jnp.einsum("rto,co->rtc", grad_projected, proj_three, preferred_element_type=jnp.float32)
     )
     grad_second = grad_second.astype(jnp.bfloat16)
-    grad_buffer = place(
-        grad_buffer,
-        jnp.einsum("rtp,rtc->pc", first_low, grad_second, preferred_element_type=jnp.float32),
-        13,
-    )
-    grad_buffer = place(grad_buffer, jnp.sum(grad_second.astype(jnp.float32), axis=(0, 1)), 14)
+    grad_buffer = put(grad_buffer, 13, first_low, grad_second)
+    sum_fourteen = summed(grad_second)
     (grad_first,) = first_back(
         jnp.einsum("rtc,pc->rtp", grad_second, proj_two, preferred_element_type=jnp.float32)
     )
     grad_first = grad_first.astype(jnp.bfloat16)
-    grad_buffer = place(
-        grad_buffer,
-        jnp.einsum("rtd,rtp->dp", feature, grad_first, preferred_element_type=jnp.float32),
-        11,
-    )
-    grad_buffer = place(grad_buffer, jnp.sum(grad_first.astype(jnp.float32), axis=(0, 1)), 12)
+    grad_buffer = put(grad_buffer, 11, feature, grad_first)
+    sum_twelve = summed(grad_first)
     grad_result = cotangent + jnp.einsum(
         "rtp,dp->rtd", grad_first, proj_one, preferred_element_type=jnp.float32
     )
     grad_gate_two = grad_result * branch_two
     grad_branch_two = (grad_result * gate_two).astype(jnp.bfloat16)
-    grad_buffer = place(
-        grad_buffer,
-        jnp.einsum("rtf,rtd->fd", activated, grad_branch_two, preferred_element_type=jnp.float32),
-        9,
-    )
-    grad_buffer = place(grad_buffer, jnp.sum(grad_branch_two.astype(jnp.float32), axis=(0, 1)), 10)
+    grad_buffer = put(grad_buffer, 9, activated, grad_branch_two)
+    sum_ten = summed(grad_branch_two)
     (grad_hidden,) = gelu_back(
         jnp.einsum(
             "rtd,fd->rtf", grad_branch_two, return_weight, preferred_element_type=jnp.float32
         )
     )
     grad_hidden = grad_hidden.astype(jnp.bfloat16)
-    grad_buffer = place(
-        grad_buffer,
-        jnp.einsum("rtd,rtf->df", mlp_in, grad_hidden, preferred_element_type=jnp.float32),
-        7,
-    )
-    grad_buffer = place(grad_buffer, jnp.sum(grad_hidden.astype(jnp.float32), axis=(0, 1)), 8)
+    grad_buffer = put(grad_buffer, 7, mlp_in, grad_hidden)
+    sum_eight = summed(grad_hidden)
     grad_mlp_in = jnp.einsum(
         "rtf,df->rtd", grad_hidden, hidden_weight, preferred_element_type=jnp.float32
     )
@@ -356,12 +1199,8 @@
     grad_middle = grad_result + grad_through_two
     grad_gate_one = grad_middle * branch_one
     grad_branch_one = (grad_middle * gate_one).astype(jnp.bfloat16)
-    grad_buffer = place(
-        grad_buffer,
-        jnp.einsum("rtd,rtc->dc", attended, grad_branch_one, preferred_element_type=jnp.float32),
-        5,
-    )
-    grad_buffer = place(grad_buffer, jnp.sum(grad_branch_one.astype(jnp.float32), axis=(0, 1)), 6)
+    grad_buffer = put(grad_buffer, 5, attended, grad_branch_one)
+    sum_six = summed(grad_branch_one)
     grad_attended = jnp.einsum(
         "rtc,dc->rtd", grad_branch_one, output_weight, preferred_element_type=jnp.float32
     ).astype(jnp.bfloat16)
@@ -385,14 +1224,8 @@
     grad_triple = lax.all_to_all(
         grad_triple_heads, "seq", split_axis=1, concat_axis=3, tiled=True
     ).reshape(rows_dev, local_len, 3 * model_width)
-    grad_buffer = place(
-        grad_buffer,
-        jnp.einsum("rtd,rtc->dc", attend_in, grad_triple, preferred_element_type=jnp.float32),
-        2,
-    )
-    triple_sums = jnp.sum(grad_triple.astype(jnp.float32), axis=(0, 1))
-    grad_buffer = place(grad_buffer, triple_sums[:model_width], 3)
-    grad_buffer = place(grad_buffer, triple_sums[2 * model_width :], 4)
+    grad_buffer = put(grad_buffer, 2, attend_in, grad_triple)
+    triple_sums = summed(grad_triple)
     grad_attend_in = jnp.einsum(
         "rtc,dc->rtd", grad_triple, attend_weight, preferred_element_type=jnp.float32
     )
@@ -405,49 +1238,53 @@
     )
     mod_part = jnp.einsum("rts,rtc->rsc", onehot, token_mod_grad, precision=highest)
     mod_grad = lax.psum(mod_part.astype(jnp.bfloat16), "seq")
-    first_share = (seq_place == 0).astype(jnp.float32)
-    grad_buffer = place(
-        grad_buffer,
-        jnp.einsum("rsd,rsc->dc", cond_low, mod_grad, preferred_element_type=jnp.float32)
-        * first_share,
-        0,
-    )
-    grad_buffer = place(
-        grad_buffer, jnp.sum(mod_grad.astype(jnp.float32), axis=(0, 1)) * first_share, 1
-    )
+    mod_all = lax.all_gather(mod_grad, "dp", axis=0, tiled=True).reshape(image_rows * SEGS, 6 * D)
     (grad_conditions,) = silu_cond_back(
         jnp.einsum("rsc,dc->rsd", mod_grad, mod_weight, preferred_element_type=jnp.float32)
     )
-    grad_tiles = grad_buffer.reshape(TILES, tile_len)
-    seq_ids = jnp.arange(seq_count, dtype=jnp.int32)[:, None, None]
-    data_ids = jnp.arange(data_count, dtype=jnp.int32)[None, :, None]
-    within_ids = jnp.arange(slot_count, dtype=jnp.int32)[None, None, :]
-    device_ids = data_ids * seq_count + seq_ids
-    slot_valid = within_ids < jnp.take(tile_counts, device_ids)
-    slot_tile = jnp.where(slot_valid, jnp.take(tile_starts, device_ids) + within_ids, 0).reshape(-1)
-    slot_valid = slot_valid.reshape(-1)
-    width_part = tile_len // 4
-    columns = []
-    for piece_index in range(4):
-        block = grad_tiles[:, piece_index * width_part : (piece_index + 1) * width_part]
-        terms = jnp.where(slot_valid[:, None], jnp.take(block, slot_tile, axis=0), 0.0)
-        terms = terms.reshape(seq_count, data_count * slot_count, width_part)
-        arrived = lax.all_to_all(
-            terms.astype(jnp.bfloat16), "seq", split_axis=0, concat_axis=0, tiled=True
-        ).astype(terms.dtype)
-        seq_summed = jnp.sum(arrived, axis=0)
-        columns.append(
-            lax.psum_scatter(
-                seq_summed.astype(jnp.bfloat16), "dp", scatter_dimension=0, tiled=True
-            ).astype(jnp.float32)
-        )
-    reduced = jnp.concatenate(columns, 1)
-    new_first = beta_one * first_moment + (1.0 - beta_one) * reduced
-    new_second = beta_two * second_moment + (1.0 - beta_two) * reduced * reduced
-    corr_one = 1.0 - beta_one**STEP
-    corr_two = 1.0 - beta_two**STEP
-    new_master = master - learn_rate * (
-        new_first / corr_one / (jnp.sqrt(new_second / corr_two) + adam_eps) + weight_decay * master
+
+    def rows(vector):
+        return vector.reshape(-1, LANES)
+
+    rows_at = param_rows()
+
+    def head(index):
+        return (0, ends[index], rows_at[index] % SUBS, SUBS)
+
+    def tail(index):
+        return (0, ends[index], SUBS, SUBS + rows_at[index] % SUBS)
+
+    def whole(vector):
+        return (0, rows(vector), 0, vector.shape[0] // LANES)
+
+    pieces = [
+        (6,) + head(2)[1:],
+        tail(2),
+        whole(triple_sums[:model_width]),
+        whole(triple_sums[2 * model_width :]),
+        head(5),
+        tail(5),
+        whole(sum_six),
+        head(7),
+        tail(7),
+        whole(sum_eight),
+        head(9),
+        tail(9),
+        whole(sum_ten),
+        head(11),
+        tail(11),
+        whole(sum_twelve),
+        head(13),
+        tail(13),
+        whole(sum_fourteen),
+        head(15),
+        tail(15),
+        whole(sum_sixteen),
+    ]
+    grad_buffer = edge_write(pieces, grad_buffer, edge_slots[EDGE_TILES.index(3891) :])
+    reduced = reduce_slots(grad_buffer, slot_count, data_count, seq_count)
+    new_master, new_first, new_second = update(
+        reduced, cond_all, mod_all, own_first, master, first_moment, second_moment
     )
     return (
         result.astype(jnp.bfloat16),

time: 4880 us -> 1280 us (0.26); the launches traced: 4810 us -> 1270 us
  local copies, waits for them, and re-layouts: 1920 us -> 82.3 us
  blocking collectives: 1530 us -> 39.3 us
  Pallas kernels: 0 us -> 891 us
  waiting for transfers between devices: 871 us -> 28 us
  other arithmetic: 251 us -> 74 us
  matrix products: 187 us -> 131 us
    all_to_all x3 -> x0, blocking collectives: 1320 us -> none  [shards(): lax.all_to_all(terms.astype(jnp.bfloat16), 'seq', split_axis=0, concat_ax...]
    pallas_call x0 -> x20, Pallas kernels: none -> 891 us  [the longest x1 397 us: gather_slots(): pl.pallas_call(partial(gather_body, side, seq_count, steps, parts), out_s...]
    dynamic_update_slice x16 -> x0, local copies, waits for them, and re-layouts: 795 us -> none  [place(): lax.dynamic_update_slice_in_dim(buffer, piece.reshape(-1), param_offsets(...]
    gather x9 -> x1, local copies, waits for them, and re-layouts: 420 us -> 0.7 us  [shards(): jnp.take(starts, edge_owner)]
    all_gather x1 -> x0, waiting for transfers between devices: 415 us -> none  [shards(): gathered = lax.all_gather(own_low, ('dp', 'seq'), axis=0, tiled=True)]
    all_to_all x1 -> x0, waiting for transfers between devices: 379 us -> none  [shards(): lax.all_to_all(terms.astype(jnp.bfloat16), 'seq', split_axis=0, concat_ax...]
    reshape x16 -> x3, local copies, waits for them, and re-layouts: 326 us -> 3.49 us  [the longest x1 2.61 us: shards(): own_low = master.astype(jnp.bfloat16).reshape(own_rows, LANES)]
    unnamed x1 -> x0, blocking collectives: 196 us -> none
  transfers between devices with their start and end apart: 10 -> 4, of which waited for: 4 -> 2; matrix products, arithmetic and copies ran while one was open for 19% -> 1% of each run, Pallas kernels for 0% -> 9%
where the time goes in v1:
time: 1280 us; the launch traced here: 1270 us
  Pallas kernels  891 us (70%)
  matrix products  131 us (10%)
  local copies, waits for them, and re-layouts  82.3 us (6%)
  other arithmetic  74 us (6%)
  blocking collectives  39.3 us (3%)
  waiting for transfers between devices  28 us (2%)
  starting transfers between devices  18.8 us (1%)
    pallas_call x1, Pallas kernels, gather_slots(): pl.pallas_call(partial(gather_body, side, seq_count, steps, parts), out_s...  397 us
    pallas_call x1, Pallas kernels, reduce_slots(): pl.pallas_call(partial(reduce_body, side, seq_count, steps, parts), out_s...  319 us
    pallas_call x8, Pallas kernels, unpack_weight(): pl.pallas_call(partial(unpack_body, base, row // SUBS, per_chunk, tiles,...  86.6 us
    pallas_call x7, Pallas kernels, weight_grad(): pl.pallas_call(partial(weight_grad_body, base, row // SUBS, per_chunk, sh...  65.8 us
  transfers between devices with their start and end apart: 4, of which 2 were waited for; matrix products, arithmetic and copies ran while one was open for 1% of the time, Pallas kernels for 9%

profile of v1, /device:TPU:1, one launch (start us, length us, event | category | flops | bytes accessed | tf_op | source)
XLA Modules:
  0.0 1267.8 jit_solution(8352360058566082585)
XLA Ops:
  4.3 2.8 convert_element_type.231
  7.2 2.6 reshape.858.own_ref
  9.8 396.8 %gather_slots.1 = bf16[8,4,9792,128]{3,2,1,0:T(8,128)(2,1)} custom-call(bf16[9792,128]{1,0:T(8,128)(2,1)} %reshape.858.own_ref), custom_call_target="tpu_custom_call" | custom-call | tf_op jit(solution)/shard_map/gather_slots/pallas_call | solution.py:578
  411.6 11.4 unpack_2.1
  423.0 17.3 %unpack_0.1 = bf16[1152,6912]{1,0:T(8,128)(2,1)} custom-call(s32[52]{0:T(128)} %get-tuple-element.57.first_ref, s32[52]{0:T(128)} %get-tuple-element.56.last_ref, s32[33]{0:T(128)} %copy-done, bf16[313344,128]{1,0:T(8,128)(2,1)} %bitcast.3.packed), custom_call_target="tpu_custom_call" | custom-call | bytes 31850496 | tf_op jit(solution)/shard_map/unpack_0/pallas_call | solution.py:137
  442.1 7.7 convolution_add_fusion
  449.8 3.0 convolution_bitcast_fusion
  452.8 2.9 copy-done.4
  456.9 2.5 fusion.6
  460.4 10.4 copy.96
  470.7 6.8 all-to-all-start
  477.5 5.2 unpack_5.1
  482.7 4.2 unpack_15.1
  487.0 8.5 unpack_11.1
  495.5 13.3 %unpack_13.1 = bf16[2048,2048]{1,0:T(8,128)(2,1)} custom-call(s32[52]{0:T(128)} %get-tuple-element.57.first_ref, s32[52]{0:T(128)} %get-tuple-element.56.last_ref, s32[33]{0:T(128)} %copy-done, bf16[313344,128]{1,0:T(8,128)(2,1)} %bitcast.3.packed), custom_call_target="tpu_custom_call" | custom-call | bytes 16777216 | tf_op jit(solution)/shard_map/unpack_13/pallas_call | solution.py:137
  508.8 13.3 %unpack_9.1 = bf16[4608,1152]{1,0:T(8,128)(2,1)} custom-call(s32[52]{0:T(128)} %get-tuple-element.57.first_ref, s32[52]{0:T(128)} %get-tuple-element.56.last_ref, s32[33]{0:T(128)} %copy-done, bf16[313344,128]{1,0:T(8,128)(2,1)} %bitcast.3.packed), custom_call_target="tpu_custom_call" | custom-call | bytes 21233664 | tf_op jit(solution)/shard_map/unpack_9/pallas_call | solution.py:137
  522.1 13.4 %unpack_7.1 = bf16[1152,4608]{1,0:T(8,128)(2,1)} custom-call(s32[52]{0:T(128)} %get-tuple-element.57.first_ref, s32[52]{0:T(128)} %get-tuple-element.56.last_ref, s32[33]{0:T(128)} %copy-done, bf16[313344,128]{1,0:T(8,128)(2,1)} %bitcast.3.packed), custom_call_target="tpu_custom_call" | custom-call | bytes 21233664 | tf_op jit(solution)/shard_map/unpack_7/pallas_call | solution.py:137
  546.7 11.4 fusion.1
  563.3 5.7 reduce.22
  570.9 4.5 all-to-all-start.1
  578.2 12.7 %all-to-all-done.1 = bf16[4,2,36864]{2,1,0:T(2,128)(2,1)S(1)} async-done(((bf16[4,2,36864]{2,1,0:T(2,128)(2,1)}), bf16[4,2,36864]{2,1,0:T(2,128)(2,1)S(1)}, u32[]{:S(2)}, u32[]{:S(2)}) %all-to-all-start.1) | async-done | bytes 589856 | tf_op jit(solution)/shard_map/all_to_all | solution.py:1106
  590.9 2.6 reshape.899
  593.4 4.7 copy.100
  601.7 4.4 fusion.117
  606.9 11.4 multiply_convert_fusion.2
  618.4 6.3 add_convert_fusion
  624.7 3.1 multiply_convert_fusion.4
  627.8 2.6 multiply_convert_fusion.3
  632.9 3.0 convert_reduce_fusion.2
  635.8 5.5 convert_reduce_fusion.3
  641.4 4.3 convert_reduce_fusion.5
  645.7 9.7 convert_reduce_fusion
  655.4 8.3 multiply_reduce_fusion.2
  670.7 6.2 reduce.23
  677.9 3.7 all-to-all-start.2
  681.6 15.3 %all-to-all-done.2 = bf16[4,2,36864]{2,1,0:T(2,128)(2,1)S(1)} async-done(((bf16[4,2,36864]{2,1,0:T(2,128)(2,1)}), bf16[4,2,36864]{2,1,0:T(2,128)(2,1)S(1)}, u32[]{:S(2)}, u32[]{:S(2)}) %all-to-all-start.2) | async-done | bytes 589856 | tf_op jit(solution)/shard_map/all_to_all | solution.py:1207
  699.0 4.7 multiply_reduce_fusion.1
  703.6 4.4 multiply_convert_fusion.1
  713.3 5.0 fusion.14
  718.3 7.2 multiply_reduce_fusion
  727.9 4.5 copy.107
  732.5 6.7 multiply_convert_fusion
  743.1 4.1 copy.106
  749.1 4.5 copy.105
  753.6 8.9 pad_maximum_fusion
  762.5 3.8 all-to-all-start.3
  768.9 11.0 all_gather.6
  784.8 5.6 weight_grad_15.1
  790.5 12.2 weight_grad_13.1
  802.7 8.3 weight_grad_11.1
  811.1 11.8 weight_grad_9.1
  822.9 11.4 weight_grad_7.1
  834.2 5.9 weight_grad_5.1
  841.9 5.5 copy.115
  849.9 7.3 constant_dynamic-update-slice_fusion.1
  857.2 4.0 copy.111.dy_ref
  861.2 3.0 fusion.115
  870.8 5.3 fusion
  876.1 16.3 %psum.7 = bf16[1,4,6912]{2,1,0:T(4,128)(2,1)S(1)} all-reduce(bf16[1,4,6912]{2,1,0:T(4,128)(2,1)S(1)} %fusion), channel_id=1, replica_groups=mesh['dp'=8,'seq'=4] {'seq'}, use_global_device_ids=true, to_apply=%region_21.22 | all-reduce | flops 27648 | bytes 110592 | tf_op jit(solution)/shard_map/psum | solution.py:1240
  892.5 10.4 fusion.80
  902.8 12.1 all_gather.7
  917.4 10.5 weight_grad_2.1
  930.2 318.5 %reduce_slots.1.reduced = bf16[9792,128]{1,0:T(8,128)(2,1)} custom-call(bf16[8,4,9792,128]{3,2,1,0:T(8,128)(2,1)} %bitcast.74.parts_ref), custom_call_target="tpu_custom_call" | custom-call | tf_op jit(solution)/shard_map/reduce_slots/pallas_call | solution.py:804
  1248.7 18.9 %update.1 = (f32[612,2048]{1,0:T(8,128)}, f32[612,2048]{1,0:T(8,128)}, f32[612,2048]{1,0:T(8,128)}) custom-call(s32[2]{0:T(128)} %pad_add_fusion.1.own_ref, bf16[9792,128]{1,0:T(8,128)(2,1)} %reduce_slots.1.reduced, bf16[200,32]{1,0:T(8,128)(2,1)} %copy.117.cond_ref, bf16[32,6912]{1,0:T(8,128)(2,1)} %reshape.880.mod_ref, f32[612,2048]{1,0:T(8,128)} %master.1, ...), custom_call_target="tpu_custom_call" | custom-call | tf_op jit(solution)/shard_map/update/pallas_call | solution.py:882
  (253 shorter events, 85.6 us)
Async XLA Ops:
  1.6 5.5 copy-start
  406.6 4.4 copy-start.59
  406.6 4.4 copy-start.60
  423.0 17.3 %copy-start.7 = (bf16[1,256,1152]{2,1,0:T(8,128)(2,1)S(1)}, bf16[1,256,1152]{2,1,0:T(8,128)(2,1)}, u32[]{:S(2)}) copy-start(bf16[1,256,1152]{2,1,0:T(8,128)(2,1)} %param.12) | copy-start | bytes 1769476
  423.0 19.1 %copy-start.37 = (bf16[1,4,1152]{2,1,0:T(4,128)(2,1)S(1)}, bf16[1,4,1152]{2,1,0:T(4,128)(2,1)}, u32[]{:S(2)}) copy-start(bf16[1,4,1152]{2,1,0:T(4,128)(2,1)} %param.13) | copy-start | bytes 27652
  440.5 12.3 copy-start.46
  441.4 11.4 copy-start.50
  442.1 7.7 copy-start.40
  449.8 7.1 copy-start.18
  452.8 2.9 copy-start.4
  470.7 66.3 %all-to-all-start = ((bf16[1,256,3,1152]{1,2,0,3:T(4,128)(2,1)}), bf16[1,256,3,1152]{1,2,0,3:T(4,128)(2,1)S(1)}, u32[]{:S(2)}, u32[]{:S(2)}) async-start(bf16[1,256,3,1152]{1,2,0,3:T(4,128)(2,1)} %copy.96), calls=%async_computation | async-start | bytes 4718592 | tf_op jit(solution)/shard_map/all_to_all | solution.py:1086
  522.1 13.4 %copy-start.55 = (s32[1,1024]{1,0:T(1,128)S(1)}, s32[1,1024]{1,0:T(1,128)}, u32[]{:S(2)}) copy-start(s32[1,1024]{1,0:T(1,128)} %param.15) | copy-start | bytes 12292
  522.1 13.5 %copy-start.45 = (s32[1,1024]{1,0:T(1,128)S(1)}, s32[1,1024]{1,0:T(1,128)}, u32[]{:S(2)}) copy-start(s32[1,1024]{1,0:T(1,128)} %param.14) | copy-start | bytes 12292
  537.5 20.7 %copy-start.10 = (bf16[1,3,4,36,8,256]{5,4,2,3,1,0:T(8,128)(2,1)}, bf16[1,3,4,36,8,256]{5,4,2,3,1,0:T(8,128)(2,1)S(1)}, u32[]{:S(2)}) copy-start(bf16[1,3,4,36,8,256]{5,4,2,3,1,0:T(8,128)(2,1)S(1)} %copy.118) | copy-start | bytes 5308420
  539.4 3.3 copy-start.2
  546.7 11.5 copy-start.3
  570.9 19.9 %all-to-all-start.1 = ((bf16[4,2,36864]{2,1,0:T(2,128)(2,1)}), bf16[4,2,36864]{2,1,0:T(2,128)(2,1)S(1)}, u32[]{:S(2)}, u32[]{:S(2)}) async-start(bf16[4,2,36864]{2,1,0:T(2,128)(2,1)} %reshape.898), calls=%async_computation.1 | async-start | bytes 1179648 | tf_op jit(solution)/shard_map/all_to_all | solution.py:1106
  590.9 15.6 %slice-start.2 = ((s8[7077888]{0:T(1024)(128)(4,1)}), s8[2883584]{0:T(1024)(128)(4,1)S(1)}, s32[]{:S(2)}) async-start(s8[7077888]{0:T(1024)(128)(4,1)} %bitcast.243), calls=%async_computation.6 | async-start | bytes 5767168
  593.4 8.3 copy-start.8
  593.4 8.3 copy-start.39
  601.7 4.5 copy-start.21
  601.7 4.8 slice-start.3
  606.1 57.6 %copy-start.5 = (f32[1,256,1152]{2,1,0:T(8,128)}, f32[1,256,1152]{2,1,0:T(8,128)S(1)}, u32[]{:S(2)}) copy-start(f32[1,256,1152]{2,1,0:T(8,128)S(1)} %get-tuple-element.72) | copy-start | bytes 3538948
  606.1 57.6 %copy-start.43 = (f32[256]{0:T(256)}, f32[256]{0:T(256)S(1)}, u32[]{:S(2)}) copy-start(f32[256]{0:T(256)S(1)} %broadcast_multiply_fusion.1) | copy-start | bytes 3076
  606.2 18.5 %slice-start.4 = ((s8[4718592]{0:T(1024)(128)(4,1)}), s8[4194304]{0:T(1024)(128)(4,1)S(1)}, s32[]{:S(2)}) async-start(s8[4718592]{0:T(1024)(128)(4,1)} %bitcast.245), calls=%async_computation.8 | async-start | bytes 8388608
  606.5 57.3 %copy-start.48 = (f32[256]{0:T(256)}, f32[256]{0:T(256)S(1)}, u32[]{:S(2)}) copy-start(f32[256]{0:T(256)S(1)} %fusion.99) | copy-start | bytes 3076
  606.5 11.8 slice-start.6
  606.8 11.5 copy-start.29
  606.8 11.5 slice-start.7
  606.8 11.5 slice-start.8
  606.9 11.5 copy-start.54
  606.9 17.8 %slice-start.5 = ((s8[4718592]{0:T(1024)(128)(4,1)}), s8[524288]{0:T(1024)(128)(4,1)S(1)}, s32[]{:S(2)}) async-start(s8[4718592]{0:T(1024)(128)(4,1)} %bitcast.245), calls=%async_computation.9 | async-start | bytes 1048576
  606.9 20.9 %slice-start.9 = ((s8[8388608]{0:T(1024)(128)(4,1)}), s8[4194304]{0:T(1024)(128)(4,1)S(1)}, s32[]{:S(2)}) async-start(s8[8388608]{0:T(1024)(128)(4,1)} %bitcast.261), calls=%async_computation.13 | async-start | bytes 8388608
  618.4 9.4 slice-start.10
  624.7 3.1 copy-start.35
  627.8 2.7 copy-start.34
  627.8 2.7 copy-start.25
  627.8 2.7 copy-start.56
  632.9 3.0 copy-start.36
  641.4 4.3 copy-start.24
  645.7 9.7 copy-start.30
  645.7 19.1 %copy-start.16 = (f32[1,256,1152]{2,1,0:T(8,128)}, f32[1,256,1152]{2,1,0:T(8,128)S(1)}, u32[]{:S(2)}) copy-start(f32[1,256,1152]{2,1,0:T(8,128)S(1)} %get-tuple-element.109) | copy-start | bytes 3538948
  655.4 8.3 copy-start.28
  664.8 2.7 copy-start.13
  677.9 19.0 %all-to-all-start.2 = ((bf16[4,2,36864]{2,1,0:T(2,128)(2,1)}), bf16[4,2,36864]{2,1,0:T(2,128)(2,1)S(1)}, u32[]{:S(2)}, u32[]{:S(2)}) async-start(bf16[4,2,36864]{2,1,0:T(2,128)(2,1)} %reshape.900), calls=%async_computation.2 | async-start | bytes 1179648 | tf_op jit(solution)/shard_map/all_to_all | solution.py:1207
  713.3 12.2 slice-start
  718.3 7.2 slice-start.1
  725.5 7.0 copy-start.42
  743.1 4.1 copy-start.33
  743.1 10.5 copy-start.20
  762.5 3.9 copy-start.1
  762.5 5.1 copy-start.57
  762.5 5.8 copy-start.58
  762.5 6.4 copy-start.38
  762.5 77.6 %all-to-all-start.3 = ((bf16[1,1024,3,288]{3,2,0,1:T(4,128)(2,1)}), bf16[1,1024,3,288]{3,2,0,1:T(4,128)(2,1)S(1)}, u32[]{:S(2)}, u32[]{:S(2)}) async-start(bf16[1,1024,3,288]{3,2,0,1:T(4,128)(2,1)} %pad_maximum_fusion), calls=%async_computation.3 | async-start | bytes 6291456 | tf_op jit(solution)/shard_map/all_to_all | solution.py:1224
  847.4 2.5 copy-start.9
  847.4 2.5 copy-start.47
  857.2 4.0 copy-start.53
  857.2 4.0 copy-start.51
  861.2 3.0 copy-start.22
  861.2 3.0 copy-start.23
  865.9 1.7 copy-start.49
  867.6 2.1 copy-start.32
  868.9 1.9 copy-start.41
  (13 other events, 16.5 us)

commit v2 on v1

--- a/solution.py
+++ b/solution.py
@@ -408,8 +408,8 @@
 
 def split_slots(slots, shards):
     room = 32 * 1024 * 1024 // ((HELD + 2 * SLOTS) * shards * SUBS * LANES * 2)
-    part = max(p for p in range(2, 19) if slots % p == 0 and p <= max(room, 2))
-    late = max(1, round(part * 0.37))
+    part = max(p for p in range(2, 13) if slots % p == 0 and p <= max(room, 2))
+    late = max(1, round(part * 0.34))
     return slots // part, (part - late, late)
 
 
@@ -578,7 +578,7 @@
     return pl.pallas_call(
         partial(gather_body, side, seq_count, steps, parts),
         out_shape=jax.ShapeDtypeStruct((data_count, seq_count, slots * SUBS, LANES), jnp.bfloat16),
-        in_specs=[pl.BlockSpec(memory_space=pl.ANY)],
+        in_specs=[pl.BlockSpec(memory_space=pltpu.VMEM)],
         out_specs=pl.BlockSpec(memory_space=pl.ANY),
         scratch_shapes=[dma] + sems,
         compiler_params=pltpu.CompilerParams(
@@ -739,9 +739,145 @@
 REDUCE_REFS = 20
 
 
-def reduce_body(side, depth, steps, parts, parts_ref, out_ref, *refs):
+MOD_BLOCKS = 6 * D // LANES
+IMAGE_ROWS = SEGS * MOD_BLOCKS
+SENT_ROWS = -(-IMAGE_ROWS // SUBS) * SUBS
+COND_CHUNK = 128
+MOD_REFS = 14
+MOD_STEPS = 11 + D // COND_CHUNK
+
+
+def modulation_stages(grid, part_ref, weight_ref, all_ref, cond_ref, refs):
+    (arrived, dense, held, send_z, recv_z, send_v, recv_v, send_u, recv_u, send_c, recv_c, loads,
+     done_sem, summed) = refs
+    mine = grid.mine
+    side = grid.side
+    depth = grid.sizes["z"]
+    here = grid.dp_of(mine["u"], mine["v"], grid.core)
+    chunks = D // COND_CHUNK
+
+    def to_z(k, seat):
+        return pltpu.make_async_remote_copy(
+            src_ref=part_ref, dst_ref=arrived.at[seat], send_sem=send_z.at[k], recv_sem=recv_z.at[seat],
+            device_id=grid.device("z", grid.other("z", k)), device_id_type=MESH,
+        )
+
+    def rows_of(dp):
+        return summed.at[dp]
+
+    def one(dp, send, recv, device):
+        return pltpu.make_async_remote_copy(
+            src_ref=rows_of(dp), dst_ref=rows_of(dp), send_sem=send, recv_sem=recv, device_id=device,
+            device_id_type=MESH,
+        )
+
+    def load(i):
+        return pltpu.make_async_copy(
+            weight_ref.at[pl.ds(pl.multiple_of(i * COND_CHUNK, COND_CHUNK), COND_CHUNK)],
+            held.at[i % 2], loads.at[i % 2],
+        )
+
+    def v_copies():
+        return [
+            one(here, send_v.at[k], recv_v.at[grid.seat("v", grid.other("v", k))], grid.device("v", grid.other("v", k)))
+            for k in range(side - 1)
+        ]
+
+    def u_copies():
+        return [
+            one(grid.dp_of(mine["u"], v, grid.core), send_u.at[k, v],
+                recv_u.at[grid.seat("u", grid.other("u", k)), v], grid.device("u", grid.other("u", k)))
+            for k in range(side - 1)
+            for v in range(side)
+        ]
+
+    def c_copies():
+        return [
+            one(grid.dp_of(u, v, grid.core), send_c.at[u, v], recv_c.at[u, v], grid.sibling)
+            for u in range(side)
+            for v in range(side)
+        ]
+
+    def run(s):
+        @pl.when(s == 0)
+        def _():
+            for k in range(depth - 1):
+                to_z(k, grid.seat("z", grid.other("z", k))).start()
+
+        @pl.when(s == 2)
+        def _():
+            for k in range(depth - 1):
+                to_z(k, k).wait_recv()
+            total = part_ref[...].astype(jnp.float32)
+            for k in range(depth - 1):
+                total = total + arrived[k].astype(jnp.float32)
+            total = total.astype(jnp.bfloat16).astype(jnp.float32)
+            summed[here] = total[:IMAGE_ROWS]
+            for k in range(depth - 1):
+                to_z(k, 0).wait_send()
+            for copy in v_copies():
+                copy.start()
+            load(0).start()
+            load(1).start()
+            dense[...] = jnp.zeros_like(dense)
+            for block in range(MOD_BLOCKS):
+                dense[0:SEGS, block * LANES : (block + 1) * LANES] = summed[
+                    here, pl.ds(block, SEGS, stride=MOD_BLOCKS), :
+                ]
+
+        @pl.when(s == 4)
+        def _():
+            for k in range(side - 1):
+                one(here, send_v.at[k], recv_v.at[k], grid.sibling).wait_recv()
+            for copy in v_copies():
+                copy.wait_send()
+            for copy in u_copies():
+                copy.start()
+
+        @pl.when(s == 6)
+        def _():
+            for k in range(side - 1):
+                for v in range(side):
+                    one(here, send_u.at[k, v], recv_u.at[k, v], grid.sibling).wait_recv()
+            for copy in u_copies():
+                copy.wait_send()
+            for copy in c_copies():
+                copy.start()
+
+        @pl.when(s == 9)
+        def _():
+            for copy in c_copies():
+                copy.wait_recv()
+            for copy in c_copies():
+                copy.wait_send()
+            pltpu.make_async_copy(summed, all_ref, done_sem).start()
+
+        i = s - 10
+
+        @pl.when((i >= 0) & (i < chunks))
+        def _():
+            load(i).wait()
+            cond_ref[:, pl.ds(pl.multiple_of(i * COND_CHUNK, COND_CHUNK), COND_CHUNK)] = lax.dot_general(
+                dense[...].astype(jnp.bfloat16), held[i % 2], (((1,), (1,)), ((), ())),
+                preferred_element_type=jnp.float32,
+            )
+
+            @pl.when(i + 2 < chunks)
+            def _():
+                load(i + 2).start()
+
+        @pl.when(s == 10 + chunks)
+        def _():
+            pltpu.make_async_copy(summed, all_ref, done_sem).wait()
+
+    return run
+
+
+def reduce_body(side, depth, steps, parts, parts_ref, part_ref, weight_ref, out_ref, all_ref, cond_ref, *refs):
     grid = Grid(side, depth)
     grid.greet()
+    modulation_step = modulation_stages(grid, part_ref, weight_ref, all_ref, cond_ref, refs[:MOD_REFS])
+    refs = refs[MOD_REFS:]
     streams = []
     writes = []
     first = 0
@@ -764,22 +900,39 @@
                 for stream in streams:
                     stream[late](q)
 
+        modulation_step(s)
         return carry
 
-    lax.fori_loop(0, steps + 4 * LAG, round_trip, 0)
+    lax.fori_loop(0, max(steps + 4 * LAG, MOD_STEPS), round_trip, 0)
     for write in writes:
         for q in range(max(steps - 2, 0), steps):
             write(q).wait()
 
 
-def reduce_slots(grads, slots, data_count, seq_count):
+def reduce_slots(grads, mod_part, mod_weight, slots, data_count, seq_count):
     side = math.isqrt(data_count // 2)
     steps, parts = split_slots(slots, side * side * seq_count)
     held = HELD
     dma = pltpu.SemaphoreType.DMA
     regular = pltpu.SemaphoreType.REGULAR
     bf16 = jnp.bfloat16
-    scratch = []
+    f32 = jnp.float32
+    scratch = [
+        pltpu.VMEM((seq_count - 1, SENT_ROWS, LANES), bf16),
+        pltpu.VMEM((8, 6 * D), f32),
+        pltpu.VMEM((2, COND_CHUNK, 6 * D), bf16),
+        dma((seq_count - 1,)),
+        dma((seq_count - 1,)),
+        dma((side - 1,)),
+        dma((side - 1,)),
+        dma((side - 1, side)),
+        dma((side - 1, side)),
+        dma((side, side)),
+        dma((side, side)),
+        dma((2,)),
+        dma,
+        pltpu.VMEM((data_count, IMAGE_ROWS, LANES), f32),
+    ]
     for order, part in zip(ORDERS, parts):
         span = part * SUBS
         sizes = {"u": side, "v": side, "z": seq_count}
@@ -803,15 +956,27 @@
             scratch.append(regular((sizes[axis],)))
     return pl.pallas_call(
         partial(reduce_body, side, seq_count, steps, parts),
-        out_shape=jax.ShapeDtypeStruct((slots * SUBS, LANES), bf16),
-        in_specs=[pl.BlockSpec(memory_space=pl.ANY)],
-        out_specs=pl.BlockSpec(memory_space=pl.ANY),
+        out_shape=(
+            jax.ShapeDtypeStruct((slots * SUBS, LANES), bf16),
+            jax.ShapeDtypeStruct((data_count, IMAGE_ROWS, LANES), f32),
+            jax.ShapeDtypeStruct((8, D), f32),
+        ),
+        in_specs=[
+            pl.BlockSpec(memory_space=pl.ANY),
+            pl.BlockSpec(memory_space=pltpu.VMEM),
+            pl.BlockSpec(memory_space=pl.ANY),
+        ],
+        out_specs=(
+            pl.BlockSpec(memory_space=pl.ANY),
+            pl.BlockSpec(memory_space=pl.ANY),
+            pl.BlockSpec(memory_space=pltpu.VMEM),
+        ),
         scratch_shapes=scratch,
         compiler_params=pltpu.CompilerParams(
             collective_id=1, has_side_effects=True, vmem_limit_bytes=VMEM_LIMIT
         ),
         name="reduce_slots",
-    )(grads.reshape(data_count, seq_count, slots * SUBS, LANES))
+    )(grads.reshape(data_count, seq_count, slots * SUBS, LANES), mod_part, mod_weight)
 
 
 UPDATE_TILES = 72
@@ -828,10 +993,14 @@
 
     @pl.when((step == 0) & (start_row < MOD_ROWS))
     def _():
+        images = cond_ref.shape[1]
         for begin in range(0, mod_blocks, piece):
+            grads = [
+                mod_ref[pl.ds(begin + block, images, stride=mod_blocks), :].astype(jnp.bfloat16)
+                for block in range(piece)
+            ]
             part = jnp.dot(
-                cond_ref[...], mod_ref[:, begin * LANES : (begin + piece) * LANES],
-                preferred_element_type=jnp.float32,
+                cond_ref[...], jnp.concatenate(grads, axis=1), preferred_element_type=jnp.float32
             )
             for block in range(piece):
                 mod_rows[pl.ds(begin + block, mod_depth, stride=mod_blocks), :] = part[
@@ -859,25 +1028,25 @@
         )
 
 
-def update(reduced, cond_all, mod_all, own_first, master, first, second):
+def own_conditions(cond_all, own_first, slots):
+    images = cond_all.shape[0]
+    steps = -(-slots // UPDATE_TILES)
+    depth = -(-(steps * UPDATE_TILES * SUBS + MOD_BLOCKS) // MOD_BLOCKS)
+    depth = -(-depth // 8) * 8
+    extended = jnp.concatenate(
+        [cond_all.T, jnp.ones((1, images), jnp.bfloat16), jnp.zeros((depth, images), jnp.bfloat16)],
+        axis=0,
+    )
+    return lax.dynamic_slice_in_dim(
+        extended, jnp.minimum(own_first[0] * SUBS // MOD_BLOCKS, D + 1), depth, 0
+    )
+
+
+def update(reduced, cond_own, mod_all, own_first, master, first, second):
     slots, tile_len = master.shape
-    images = cond_all.shape[0]
+    mod_depth, images = cond_own.shape
     tiles = UPDATE_TILES
     steps = -(-slots // tiles)
-    mod_blocks = 6 * D // LANES
-    mod_depth = -(-(steps * tiles * SUBS + mod_blocks) // mod_blocks)
-    mod_depth = -(-mod_depth // 8) * 8
-    extended = jnp.concatenate(
-        [
-            cond_all.T,
-            jnp.ones((1, images), jnp.bfloat16),
-            jnp.zeros((mod_depth, images), jnp.bfloat16),
-        ],
-        axis=0,
-    )
-    cond_own = lax.dynamic_slice_in_dim(
-        extended, jnp.minimum(own_first[0] * SUBS // mod_blocks, D + 1), mod_depth, 0
-    )
     wide_block = pl.BlockSpec((tiles, tile_len), lambda i, *_: (i, 0))
     return pl.pallas_call(
         partial(update_body, mod_depth),
@@ -888,14 +1057,14 @@
             in_specs=[
                 pl.BlockSpec((tiles * SUBS, LANES), lambda i, *_: (i, 0)),
                 pl.BlockSpec((mod_depth, images), lambda i, *_: (0, 0)),
-                pl.BlockSpec((images, 6 * D), lambda i, *_: (0, 0)),
+                pl.BlockSpec(mod_all.shape, lambda i, *_: (0, 0)),
                 wide_block,
                 wide_block,
                 wide_block,
             ],
             out_specs=(wide_block,) * 3,
             scratch_shapes=[
-                pltpu.VMEM((mod_depth * mod_blocks, LANES), jnp.float32),
+                pltpu.VMEM((mod_depth * MOD_BLOCKS, LANES), jnp.float32),
                 pltpu.VMEM((tiles * SUBS, LANES), jnp.float32),
             ],
         ),
@@ -1031,20 +1200,16 @@
     own_low = master.astype(jnp.bfloat16).reshape(own_rows, LANES)
     packed = gather_slots(own_low, slot_count, data_count, seq_count)
 
-    mod_blocks = 6 * D // LANES
     own_first = jnp.stack([own_start, own_count])
     cond_f = conditions.astype(jnp.float32)
     cond_act, silu_cond_back = jax.vjp(jax.nn.silu, cond_f)
     cond_low = cond_act.astype(jnp.bfloat16)
-    cond_all = lax.all_gather(cond_low, "dp", axis=0, tiled=True)
-    image_rows = cond_all.shape[0]
-    cond_all = cond_all.reshape(image_rows * SEGS, D)
-
     weights = {
-        index: unpack_weight(index, packed, slot_count, firsts, lasts, starts) for index in CHUNK
+        index: unpack_weight(index, packed, slot_count, firsts, lasts, starts)
+        for index in (0, 2, 5, 7, 9, 15)
     }
-    mod_weight, attend_weight, output_weight, hidden_weight, return_weight, proj_one, proj_two, proj_three = (
-        weights[index] for index in (0, 2, 5, 7, 9, 11, 13, 15)
+    mod_weight, attend_weight, output_weight, hidden_weight, return_weight, proj_three = (
+        weights[index] for index in (0, 2, 5, 7, 9, 15)
     )
     edges = edge_read(packed, edge_slots)
     edge_flat = edges.reshape(-1)
@@ -1084,10 +1249,8 @@
     )
     triple_low = triple.astype(jnp.bfloat16).reshape(rows_dev, local_len, 3, model_width)
     head_rows = lax.all_to_all(triple_low, "seq", split_axis=3, concat_axis=1, tiled=True)
-    (head_rows, output_weight, hidden_weight, return_weight, proj_one, proj_two, proj_three) = (
-        lax.optimization_barrier(
-            (head_rows, output_weight, hidden_weight, return_weight, proj_one, proj_two, proj_three)
-        )
+    (head_rows, output_weight, hidden_weight, return_weight, proj_three) = lax.optimization_barrier(
+        (head_rows, output_weight, hidden_weight, return_weight, proj_three)
     )
     head_view = head_rows.reshape(rows_dev, full_len, 3, heads_local, HEAD_DIM)
     row_index = 0
@@ -1103,7 +1266,10 @@
     attended_parts = [head_out.astype(jnp.bfloat16).reshape(full_len, group_width)]
     lse_rows = [head_lse]
     head_attended = jnp.stack(attended_parts)
+    head_attended, packed = lax.optimization_barrier((head_attended, packed))
+    proj_one, proj_two = (unpack_weight(index, packed, slot_count, firsts, lasts, starts) for index in (11, 13))
     attended = lax.all_to_all(head_attended, "seq", split_axis=1, concat_axis=2, tiled=True)
+    attended, proj_one, proj_two = lax.optimization_barrier((attended, proj_one, proj_two))
     branch_one = (
         jnp.einsum("rtd,dc->rtc", attended, output_weight, preferred_element_type=jnp.float32)
         + output_bias
@@ -1162,26 +1328,22 @@
 
     (grad_projected,) = cosine_back(local_pad * -repa_weight)
     grad_projected = grad_projected.astype(jnp.bfloat16)
-    grad_buffer = put(None, 15, second_low, grad_projected)
     sum_sixteen = summed(grad_projected)
     (grad_second,) = second_back(
         jnp.einsum("rto,co->rtc", grad_projected, proj_three, preferred_element_type=jnp.float32)
     )
     grad_second = grad_second.astype(jnp.bfloat16)
-    grad_buffer = put(grad_buffer, 13, first_low, grad_second)
     sum_fourteen = summed(grad_second)
     (grad_first,) = first_back(
         jnp.einsum("rtc,pc->rtp", grad_second, proj_two, preferred_element_type=jnp.float32)
     )
     grad_first = grad_first.astype(jnp.bfloat16)
-    grad_buffer = put(grad_buffer, 11, feature, grad_first)
     sum_twelve = summed(grad_first)
     grad_result = cotangent + jnp.einsum(
         "rtp,dp->rtd", grad_first, proj_one, preferred_element_type=jnp.float32
     )
     grad_gate_two = grad_result * branch_two
     grad_branch_two = (grad_result * gate_two).astype(jnp.bfloat16)
-    grad_buffer = put(grad_buffer, 9, activated, grad_branch_two)
     sum_ten = summed(grad_branch_two)
     (grad_hidden,) = gelu_back(
         jnp.einsum(
@@ -1189,7 +1351,6 @@
         )
     )
     grad_hidden = grad_hidden.astype(jnp.bfloat16)
-    grad_buffer = put(grad_buffer, 7, mlp_in, grad_hidden)
     sum_eight = summed(grad_hidden)
     grad_mlp_in = jnp.einsum(
         "rtf,df->rtd", grad_hidden, hidden_weight, preferred_element_type=jnp.float32
@@ -1199,12 +1360,15 @@
     grad_middle = grad_result + grad_through_two
     grad_gate_one = grad_middle * branch_one
     grad_branch_one = (grad_middle * gate_one).astype(jnp.bfloat16)
-    grad_buffer = put(grad_buffer, 5, attended, grad_branch_one)
     sum_six = summed(grad_branch_one)
     grad_attended = jnp.einsum(
         "rtc,dc->rtd", grad_branch_one, output_weight, preferred_element_type=jnp.float32
     ).astype(jnp.bfloat16)
+    grad_attended, second_low = lax.optimization_barrier((grad_attended, second_low))
     head_grad = lax.all_to_all(grad_attended, "seq", split_axis=2, concat_axis=1, tiled=True)
+    grad_buffer = put(None, 15, second_low, grad_projected)
+    grad_buffer = put(grad_buffer, 11, feature, grad_first)
+    head_grad, grad_buffer = lax.optimization_barrier((head_grad, grad_buffer))
     row_index = 0
     grad_query, grad_key, grad_value = attend_backward(
         head_view[row_index, :, 0],
@@ -1221,9 +1385,20 @@
         jnp.stack([grad_query, grad_key, grad_value], 1).reshape(full_len, 3, group_width)
     ]
     grad_triple_heads = jnp.stack(triple_parts).astype(jnp.bfloat16)
+    grad_triple_heads, grad_buffer, cond_low = lax.optimization_barrier(
+        (grad_triple_heads, grad_buffer, cond_low)
+    )
     grad_triple = lax.all_to_all(
         grad_triple_heads, "seq", split_axis=1, concat_axis=3, tiled=True
     ).reshape(rows_dev, local_len, 3 * model_width)
+    grad_buffer = put(grad_buffer, 13, first_low, grad_second)
+    grad_buffer = put(grad_buffer, 9, activated, grad_branch_two)
+    grad_buffer = put(grad_buffer, 7, mlp_in, grad_hidden)
+    grad_buffer = put(grad_buffer, 5, attended, grad_branch_one)
+    cond_all = lax.all_gather(cond_low, "dp", axis=0, tiled=True)
+    image_rows = cond_all.shape[0]
+    cond_own = own_conditions(cond_all.reshape(image_rows * SEGS, D), own_first, slot_count)
+    grad_triple, grad_buffer, cond_own = lax.optimization_barrier((grad_triple, grad_buffer, cond_own))
     grad_buffer = put(grad_buffer, 2, attend_in, grad_triple)
     triple_sums = summed(grad_triple)
     grad_attend_in = jnp.einsum(
@@ -1237,16 +1412,14 @@
         axis=-1,
     )
     mod_part = jnp.einsum("rts,rtc->rsc", onehot, token_mod_grad, precision=highest)
-    mod_grad = lax.psum(mod_part.astype(jnp.bfloat16), "seq")
-    mod_all = lax.all_gather(mod_grad, "dp", axis=0, tiled=True).reshape(image_rows * SEGS, 6 * D)
-    (grad_conditions,) = silu_cond_back(
-        jnp.einsum("rsc,dc->rsd", mod_grad, mod_weight, preferred_element_type=jnp.float32)
-    )
+    mod_sent = jnp.pad(
+        mod_part.astype(jnp.bfloat16).reshape(IMAGE_ROWS, LANES), ((0, SENT_ROWS - IMAGE_ROWS), (0, 0))
+    )
+    rows_at = param_rows()
 
     def rows(vector):
         return vector.reshape(-1, LANES)
 
-    rows_at = param_rows()
 
     def head(index):
         return (0, ends[index], rows_at[index] % SUBS, SUBS)
@@ -1282,9 +1455,13 @@
         whole(sum_sixteen),
     ]
     grad_buffer = edge_write(pieces, grad_buffer, edge_slots[EDGE_TILES.index(3891) :])
-    reduced = reduce_slots(grad_buffer, slot_count, data_count, seq_count)
+    reduced, mod_all, cond_grad = reduce_slots(
+        grad_buffer, mod_sent, mod_weight, slot_count, data_count, seq_count
+    )
+    (grad_conditions,) = silu_cond_back(cond_grad[None, :SEGS])
+    mod_all = mod_all.reshape(image_rows * IMAGE_ROWS, LANES)
     new_master, new_first, new_second = update(
-        reduced, cond_all, mod_all, own_first, master, first_moment, second_moment
+        reduced, cond_own, mod_all, own_first, master, first_moment, second_moment
     )
     return (
         result.astype(jnp.bfloat16),

time: 1280 us -> 1150 us (0.90)
  Pallas kernels: 891 us -> 814 us
  blocking collectives: 39.3 us -> 11.3 us
    pallas_call x1, Pallas kernels: 397 us -> 320 us  [gather_slots(): pl.pallas_call(partial(gather_body, side, seq_count, steps, parts), out_s...]
    optimization_barrier x0 -> x5, local copies, waits for them, and re-layouts: none -> 19.6 us  [the longest x1 12.5 us: shards(): head_attended, packed = lax.optimization_barrier((head_attended, packed))]
    psum x1 -> x0, blocking collectives: 16.3 us -> none  [shards(): mod_grad = lax.psum(mod_part.astype(jnp.bfloat16), 'seq')]
    all_to_all x1, waiting for transfers between devices: 0.01 us -> 15.8 us  [shards(): lax.all_to_all(triple_low, 'seq', split_axis=3, concat_axis=1, tiled=True)]
    all_to_all x1, waiting for transfers between devices: 15.3 us -> 0.78 us  [shards(): lax.all_to_all(grad_attended, 'seq', split_axis=2, concat_axis=1, tiled=T...]
  transfers between devices with their start and end apart: 4 -> 4, of which waited for: 2 -> 3; matrix products, arithmetic and copies ran while one was open for 1% -> 1% of each run, Pallas kernels for 9% -> 10%
where the time goes in v2:
time: 1150 us; the launch traced here: 1140 us
  Pallas kernels  814 us (71%)
  matrix products  121 us (11%)
  local copies, waits for them, and re-layouts  82.3 us (7%)
  other arithmetic  63.4 us (6%)
  waiting for transfers between devices  26.7 us (2%)
  starting transfers between devices  19 us (2%)
    pallas_call x1, Pallas kernels, gather_slots(): pl.pallas_call(partial(gather_body, side, seq_count, steps, parts), out_s...  320 us
    pallas_call x1, Pallas kernels, reduce_slots(): pl.pallas_call(partial(reduce_body, side, seq_count, steps, parts), out_s...  318 us
    pallas_call x8, Pallas kernels, unpack_weight(): pl.pallas_call(partial(unpack_body, base, row // SUBS, per_chunk, tiles,...  86.5 us
    pallas_call x7, Pallas kernels, weight_grad(): pl.pallas_call(partial(weight_grad_body, base, row // SUBS, per_chunk, sh...  65.8 us
  transfers between devices with their start and end apart: 4, of which 3 were waited for; matrix products, arithmetic and copies ran while one was open for 1% of the time, Pallas kernels for 10%

profile of v2, /device:TPU:1, one launch (start us, length us, event | category | flops | bytes accessed | tf_op | source)
XLA Modules:
  0.0 1140.5 jit_solution(6647300524370740282)
XLA Ops:
  1.5 2.8 convert_element_type.230
  4.4 2.6 reshape.863.own_ref
  7.0 320.0 %gather_slots.1 = bf16[8,4,9792,128]{3,2,1,0:T(8,128)(2,1)} custom-call(bf16[9792,128]{1,0:T(8,128)(2,1)} %reshape.863.own_ref), custom_call_target="tpu_custom_call" | custom-call | tf_op jit(solution)/shard_map/gather_slots/pallas_call | solution.py:578
  328.6 2.2 edge_read.1
  333.6 17.1 %unpack_0.1.weight_ref = bf16[1152,6912]{1,0:T(8,128)(2,1)} custom-call(s32[52]{0:T(128)} %get-tuple-element.89.first_ref, s32[52]{0:T(128)} %get-tuple-element.88.last_ref, s32[33]{0:T(128)} %copy-done, bf16[313344,128]{1,0:T(8,128)(2,1)} %bitcast.3.packed), custom_call_target="tpu_custom_call" | custom-call | bytes 31850496 | tf_op jit(solution)/shard_map/unpack_0/pallas_call | solution.py:137
  350.7 11.5 %unpack_2.1 = bf16[1152,3456]{1,0:T(8,128)(2,1)} custom-call(s32[52]{0:T(128)} %get-tuple-element.89.first_ref, s32[52]{0:T(128)} %get-tuple-element.88.last_ref, s32[33]{0:T(128)} %copy-done, bf16[313344,128]{1,0:T(8,128)(2,1)} %bitcast.3.packed), custom_call_target="tpu_custom_call" | custom-call | bytes 15925248 | tf_op jit(solution)/shard_map/unpack_2/pallas_call | solution.py:137
  362.8 7.7 convolution_add_fusion
  370.5 3.0 convolution_bitcast_fusion
  373.5 2.9 copy-done.4
  377.6 5.8 fusion.5
  384.3 10.4 copy.86
  394.7 6.7 all-to-all-start
  401.4 5.2 unpack_5.1
  406.6 13.3 %unpack_7.1 = bf16[1152,4608]{1,0:T(8,128)(2,1)} custom-call(s32[52]{0:T(128)} %get-tuple-element.89.first_ref, s32[52]{0:T(128)} %get-tuple-element.88.last_ref, s32[33]{0:T(128)} %copy-done, bf16[313344,128]{1,0:T(8,128)(2,1)} %bitcast.3.packed), custom_call_target="tpu_custom_call" | custom-call | bytes 21233664 | tf_op jit(solution)/shard_map/unpack_7/pallas_call | solution.py:137
  419.9 13.3 %unpack_9.1 = bf16[4608,1152]{1,0:T(8,128)(2,1)} custom-call(s32[52]{0:T(128)} %get-tuple-element.89.first_ref, s32[52]{0:T(128)} %get-tuple-element.88.last_ref, s32[33]{0:T(128)} %copy-done, bf16[313344,128]{1,0:T(8,128)(2,1)} %bitcast.3.packed), custom_call_target="tpu_custom_call" | custom-call | bytes 21233664 | tf_op jit(solution)/shard_map/unpack_9/pallas_call | solution.py:137
  433.3 4.4 unpack_15.1
  439.1 15.8 %all-to-all-done = bf16[1,256,3,1152]{1,2,0,3:T(4,128)(2,1)S(1)} async-done(((bf16[1,256,3,1152]{1,2,0,3:T(4,128)(2,1)}), bf16[1,256,3,1152]{1,2,0,3:T(4,128)(2,1)S(1)}, u32[]{:S(2)}, u32[]{:S(2)}) %all-to-all-start) | async-done | bytes 1769504 | tf_op jit(solution)/shard_map/all_to_all | solution.py:1251
  460.6 2.1 fusion.52
  470.1 12.5 %copy.89 = bf16[1,1024,288]{2,0,1:T(2,128)(2,1)S(1)} copy(bf16[1,1024,288]{1,2,0:T(8,128)(2,1)S(1)} %pad_maximum_fusion.1) | data formatting | bytes 1179648 | tf_op jit(solution)/shard_map/optimization_barrier | solution.py:1269
  483.2 5.7 reduce.21
  490.8 3.5 all-to-all-start.1
  497.0 8.5 unpack_11.1
  505.5 13.3 %unpack_13.1 = bf16[2048,2048]{1,0:T(8,128)(2,1)} custom-call(s32[52]{0:T(128)} %get-tuple-element.89.first_ref, s32[52]{0:T(128)} %get-tuple-element.88.last_ref, s32[33]{0:T(128)} %copy-done, bf16[313344,128]{1,0:T(8,128)(2,1)} %bitcast.3.packed), custom_call_target="tpu_custom_call" | custom-call | bytes 16777216 | tf_op jit(solution)/shard_map/unpack_13/pallas_call | solution.py:137
  518.8 2.6 reshape.906
  521.4 4.7 copy.90
  526.1 2.4 all_to_all.55
  529.7 4.4 fusion.116
  534.9 11.6 %multiply_convert_fusion.2 = (bf16[256,4608]{1,0:T(8,128)(2,1)}, f32[256,4608]{1,0:T(8,128)}) fusion(f32[4608]{0:T(1024)S(1)} %fusion.82, bf16[256,1152]{1,0:T(8,128)(2,1)S(1)} %fusion.68.x_ref, bf16[1152,4608]{1,0:T(8,128)(2,1)} %unpack_7.1), kind=kOutput, calls=%fused_computation.34 | convolution fusion | flops 2729705472 | bytes 18302976 | tf_op jit(solution)/shard_map/rtd,df->rtf/dot_general | solution.py:1281
  546.6 6.2 add_convert_fusion
  552.8 3.1 multiply_convert_fusion.4
  556.0 2.4 convolution_add_fusion.5
  563.1 3.0 convert_reduce_fusion.2
  566.1 5.5 convert_reduce_fusion.3
  571.6 4.1 convert_reduce_fusion.5
  575.7 9.7 convert_reduce_fusion
  585.4 8.3 multiply_reduce_fusion.2
  600.7 6.2 reduce.22
  607.9 4.9 all-to-all-start.2
  613.5 5.6 weight_grad_15.1
  619.1 8.3 weight_grad_11.1
  629.0 5.0 fusion.13
  634.1 7.2 multiply_reduce_fusion
  641.2 2.6 multiply_reduce_fusion.1
  650.3 2.9 copy.97
  653.2 6.7 multiply_convert_fusion
  663.9 4.1 copy.96
  669.9 4.5 copy.95
  674.4 8.5 pad_maximum_fusion
  682.9 3.9 all-to-all-start.3
  693.2 11.3 all_gather.3
  705.4 12.3 %weight_grad_13.1 = (bf16[313344,128]{1,0:T(8,128)(2,1)}, f32[32,128]{1,0:T(8,128)}) custom-call(s32[52]{0:T(128)} %get-tuple-element.89.first_ref, s32[52]{0:T(128)} %get-tuple-element.88.last_ref, s32[33]{0:T(128)} %copy-done, bf16[256,2048]{1,0:T(8,128)(2,1)} %copy-done.31, ...), custom_call_target="tpu_custom_call", output_to_operand_aliasing={{0}: (5, {})} | custom-call | flops 2147483648 | bytes 8388608 | tf_op jit(solution)/shard_map/weight_grad_13/pallas_call | solution.py:329
  717.8 11.8 %weight_grad_9.1 = (bf16[313344,128]{1,0:T(8,128)(2,1)}, f32[32,128]{1,0:T(8,128)}) custom-call(s32[52]{0:T(128)} %get-tuple-element.89.first_ref, s32[52]{0:T(128)} %get-tuple-element.88.last_ref, s32[33]{0:T(128)} %copy-done, bf16[256,4608]{1,0:T(8,128)(2,1)} %get-tuple-element.131.x_ref, ...), custom_call_target="tpu_custom_call", output_to_operand_aliasing={{0}: (5, {})} | custom-call | flops 2717908992 | bytes 10616832 | tf_op jit(solution)/shard_map/weight_grad_9/pallas_call | solution.py:329
  729.6 11.4 weight_grad_7.1
  741.0 5.9 weight_grad_5.1
  746.9 10.1 all-to-all-done.3
  757.0 4.0 copy.102
  762.9 7.2 constant_dynamic-update-slice_fusion.1
  770.1 2.2 copy.101
  772.9 3.0 fusion.114
  783.1 5.3 convolution_convert_fusion
  789.1 10.5 weight_grad_2.1
  799.6 2.3 edge_write.1
  801.9 318.0 %reduce_slots.1 = (bf16[9792,128]{1,0:T(8,128)(2,1)}, f32[8,216,128]{2,1,0:T(8,128)}, f32[8,1152]{1,0:T(8,128)}) custom-call(bf16[8,4,9792,128]{3,2,1,0:T(8,128)(2,1)} %bitcast.80.parts_ref, bf16[224,128]{1,0:T(8,128)(2,1)} %pad.4.part_ref, bf16[1152,6912]{1,0:T(8,128)(2,1)} %unpack_0.1.weight_ref), custom_call_target="tpu_custom_call" | custom-call | tf_op jit(solution)/shard_map/reduce_slots/pallas_call | solution.py:957
  1121.3 19.0 %update.1 = (f32[612,2048]{1,0:T(8,128)}, f32[612,2048]{1,0:T(8,128)}, f32[612,2048]{1,0:T(8,128)}) custom-call(s32[2]{0:T(128)} %pad_add_fusion.1.own_ref, bf16[9792,128]{1,0:T(8,128)(2,1)} %get-tuple-element.80.reduced, bf16[200,32]{1,0:T(8,128)(2,1)} %copy.104.cond_ref, f32[1728,128]{1,0:T(8,128)} %bitcast.298, f32[612,2048]{1,0:T(8,128)} %master.1, ...), custom_call_target="tpu_custom_call" | custom-call | tf_op jit(solution)/shard_map/update/pallas_call | solution.py:1051
  (242 shorter events, 74.5 us)
Async XLA Ops:
  7.0 320.1 %copy-start.59 = (s32[18]{0:T(128)S(1)}, s32[18]{0:T(128)}, u32[]{:S(2)}) copy-start(s32[18]{0:T(128)} %constant.134.clone) | copy-start | bytes 220
  327.1 3.7 copy-start
  328.6 4.3 copy-start.57
  328.6 4.3 copy-start.58
  350.7 11.6 %copy-start.7 = (bf16[1,256,1152]{2,1,0:T(8,128)(2,1)S(1)}, bf16[1,256,1152]{2,1,0:T(8,128)(2,1)}, u32[]{:S(2)}) copy-start(bf16[1,256,1152]{2,1,0:T(8,128)(2,1)} %param.12) | copy-start | bytes 1769476
  350.7 12.1 %copy-start.43 = (s32[1,1024]{1,0:T(1,128)S(1)}, s32[1,1024]{1,0:T(1,128)}, u32[]{:S(2)}) copy-start(s32[1,1024]{1,0:T(1,128)} %param.14) | copy-start | bytes 12292
  350.7 12.1 %copy-start.34 = (bf16[1,4,1152]{2,1,0:T(4,128)(2,1)S(1)}, bf16[1,4,1152]{2,1,0:T(4,128)(2,1)}, u32[]{:S(2)}) copy-start(bf16[1,4,1152]{2,1,0:T(4,128)(2,1)} %param.13) | copy-start | bytes 27652
  362.4 11.1 copy-start.44
  362.7 7.8 copy-start.50
  362.7 10.7 copy-start.48
  362.8 7.7 copy-start.38
  373.5 2.9 copy-start.4
  394.7 60.2 %all-to-all-start = ((bf16[1,256,3,1152]{1,2,0,3:T(4,128)(2,1)}), bf16[1,256,3,1152]{1,2,0,3:T(4,128)(2,1)S(1)}, u32[]{:S(2)}, u32[]{:S(2)}) async-start(bf16[1,256,3,1152]{1,2,0,3:T(4,128)(2,1)} %copy.86), calls=%async_computation | async-start | bytes 4718592 | tf_op jit(solution)/shard_map/all_to_all | solution.py:1251
  433.3 4.4 copy-start.53
  455.4 11.1 copy-start.10
  457.3 3.3 copy-start.2
  464.7 3.2 copy-start.3
  490.8 28.0 %all-to-all-start.1 = ((bf16[4,2,36864]{2,1,0:T(2,128)(2,1)}), bf16[4,2,36864]{2,1,0:T(2,128)(2,1)S(1)}, u32[]{:S(2)}, u32[]{:S(2)}) async-start(bf16[4,2,36864]{2,1,0:T(2,128)(2,1)} %reshape.905), calls=%async_computation.1 | async-start | bytes 1179648 | tf_op jit(solution)/shard_map/all_to_all | solution.py:1271
  518.8 15.6 %slice-start.2 = ((s8[7077888]{0:T(1024)(128)(4,1)}), s8[2883584]{0:T(1024)(128)(4,1)S(1)}, s32[]{:S(2)}) async-start(s8[7077888]{0:T(1024)(128)(4,1)} %bitcast.252), calls=%async_computation.6 | async-start | bytes 5767168
  521.4 8.3 copy-start.8
  521.4 8.3 copy-start.37
  529.7 4.5 copy-start.18
  529.7 4.8 slice-start.3
  534.1 59.6 %copy-start.5 = (f32[1,256,1152]{2,1,0:T(8,128)}, f32[1,256,1152]{2,1,0:T(8,128)S(1)}, u32[]{:S(2)}) copy-start(f32[1,256,1152]{2,1,0:T(8,128)S(1)} %get-tuple-element.104) | copy-start | bytes 3538948
  534.2 59.6 %copy-start.41 = (f32[256]{0:T(256)}, f32[256]{0:T(256)S(1)}, u32[]{:S(2)}) copy-start(f32[256]{0:T(256)S(1)} %broadcast_multiply_fusion.1) | copy-start | bytes 3076
  534.2 12.4 %slice-start.6 = ((s8[10616832]{0:T(1024)(128)(4,1)}), s8[4194304]{0:T(1024)(128)(4,1)S(1)}, s32[]{:S(2)}) async-start(s8[10616832]{0:T(1024)(128)(4,1)} %bitcast.270), calls=%async_computation.10 | async-start | bytes 8388608
  534.5 59.3 %copy-start.46 = (f32[256]{0:T(256)}, f32[256]{0:T(256)S(1)}, u32[]{:S(2)}) copy-start(f32[256]{0:T(256)S(1)} %fusion.97) | copy-start | bytes 3076
  534.5 18.3 %slice-start.4 = ((s8[4718592]{0:T(1024)(128)(4,1)}), s8[4194304]{0:T(1024)(128)(4,1)S(1)}, s32[]{:S(2)}) async-start(s8[4718592]{0:T(1024)(128)(4,1)} %bitcast.254), calls=%async_computation.8 | async-start | bytes 8388608
  534.8 11.7 %copy-start.26 = (bf16[256,1152]{1,0:T(8,128)(2,1)}, bf16[256,1152]{1,0:T(8,128)(2,1)S(1)}, u32[]{:S(2)}) copy-start(bf16[256,1152]{1,0:T(8,128)(2,1)S(1)} %fusion.68.x_ref) | copy-start | bytes 1769476
  534.8 11.7 %slice-start.7 = ((s8[10616832]{0:T(1024)(128)(4,1)}), s8[4194304]{0:T(1024)(128)(4,1)S(1)}, s32[]{:S(2)}) async-start(s8[10616832]{0:T(1024)(128)(4,1)} %bitcast.270), calls=%async_computation.11 | async-start | bytes 8388608
  534.8 11.7 %slice-start.8 = ((s8[10616832]{0:T(1024)(128)(4,1)}), s8[2228224]{0:T(1024)(128)(4,1)S(1)}, s32[]{:S(2)}) async-start(s8[10616832]{0:T(1024)(128)(4,1)} %bitcast.270), calls=%async_computation.12 | async-start | bytes 4456448
  534.9 11.7 %copy-start.52 = (f32[1152]{0:T(1024)S(1)}, f32[1152]{0:T(1024)}, u32[]{:S(2)}) copy-start(f32[1152]{0:T(1024)} %get-tuple-element.114) | copy-start | bytes 13828
  534.9 18.0 %slice-start.5 = ((s8[4718592]{0:T(1024)(128)(4,1)}), s8[524288]{0:T(1024)(128)(4,1)S(1)}, s32[]{:S(2)}) async-start(s8[4718592]{0:T(1024)(128)(4,1)} %bitcast.254), calls=%async_computation.9 | async-start | bytes 1048576
  534.9 21.1 %slice-start.9 = ((s8[8388608]{0:T(1024)(128)(4,1)}), s8[4194304]{0:T(1024)(128)(4,1)S(1)}, s32[]{:S(2)}) async-start(s8[8388608]{0:T(1024)(128)(4,1)} %bitcast.272), calls=%async_computation.13 | async-start | bytes 8388608
  546.6 9.4 slice-start.10
  552.8 3.1 copy-start.32
  555.9 2.4 copy-start.31
  556.0 4.0 copy-start.54
  558.4 2.3 copy-start.22
  563.1 3.0 copy-start.33
  571.6 4.1 copy-start.21
  575.7 9.7 copy-start.27
  575.7 19.1 %copy-start.15 = (f32[1,256,1152]{2,1,0:T(8,128)}, f32[1,256,1152]{2,1,0:T(8,128)S(1)}, u32[]{:S(2)}) copy-start(f32[1,256,1152]{2,1,0:T(8,128)S(1)} %get-tuple-element.139) | copy-start | bytes 3538948
  585.4 8.3 copy-start.25
  594.8 2.7 copy-start.12
  600.7 12.1 %copy-start.35 = (bf16[1,4,1152]{2,1,0:T(4,128)(2,1)S(1)}, bf16[1,4,1152]{2,1,0:T(4,128)(2,1)}, u32[]{:S(2)}) copy-start(bf16[1,4,1152]{2,1,0:T(4,128)(2,1)} %param.13) | copy-start | bytes 27652
  607.9 20.3 %all-to-all-start.2 = ((bf16[4,2,36864]{2,1,0:T(2,128)(2,1)}), bf16[4,2,36864]{2,1,0:T(2,128)(2,1)S(1)}, u32[]{:S(2)}, u32[]{:S(2)}) async-start(bf16[4,2,36864]{2,1,0:T(2,128)(2,1)} %reshape.907), calls=%async_computation.2 | async-start | bytes 1179648 | tf_op jit(solution)/shard_map/all_to_all | solution.py:1368
  629.0 5.0 copy-start.11
  629.0 12.2 %slice-start = ((s8[8388608]{0:T(1024)(128)(4,1)}), s8[4194304]{0:T(1024)(128)(4,1)S(1)}, s32[]{:S(2)}) async-start(s8[8388608]{0:T(1024)(128)(4,1)} %bitcast.250), calls=%async_computation.4 | async-start | bytes 8388608
  634.0 7.2 slice-start.1
  663.9 4.1 copy-start.30
  663.9 10.5 copy-start.17
  682.9 3.9 copy-start.1
  682.9 5.1 copy-start.55
  682.9 5.7 copy-start.56
  682.9 10.3 copy-start.40
  682.9 74.1 %all-to-all-start.3 = ((bf16[1,1024,3,288]{3,2,0,1:T(4,128)(2,1)}), bf16[1,1024,3,288]{3,2,0,1:T(4,128)(2,1)S(1)}, u32[]{:S(2)}, u32[]{:S(2)}) async-start(bf16[1,1024,3,288]{3,2,0,1:T(4,128)(2,1)} %pad_maximum_fusion), calls=%async_computation.3 | async-start | bytes 6291456 | tf_op jit(solution)/shard_map/all_to_all | solution.py:1391
  761.1 1.8 copy-start.45
  770.1 2.8 copy-start.51
  770.1 2.8 copy-start.49
  772.9 3.6 copy-start.19
  772.9 3.6 copy-start.20
  779.9 2.1 copy-start.29
  801.9 318.0 %copy-start.36 = (bf16[1,4,1152]{2,1,0:T(4,128)(2,1)S(1)}, bf16[1,4,1152]{2,1,0:T(4,128)(2,1)}, u32[]{:S(2)}) copy-start(bf16[1,4,1152]{2,1,0:T(4,128)(2,1)} %param.13) | copy-start | bytes 27652
  (11 other events, 15.8 us)

commit v3 on v2

--- a/solution.py
+++ b/solution.py
@@ -1092,79 +1092,192 @@
     return jax.nn.gelu(values, approximate=True)
 
 
-def block_mask(seg_row, pad_row, start_row, block_len):
-    full_len = seg_row.shape[0]
-    query_seg = seg_row[start_row : start_row + block_len]
-    query_pos = start_row + jnp.arange(block_len, dtype=jnp.int32)
-    key_pos = jnp.arange(full_len, dtype=jnp.int32)
-    same_image = query_seg[:, None] == seg_row[None, :]
-    usable = (pad_row[None, :] == 1) | (query_pos[:, None] == key_pos[None, :])
-    return same_image & usable
-
-
-def attend_forward(queries, key_rows, values, seg_row, pad_row, block_len, scaling):
-    out_parts = []
-    lse_parts = []
-    for start_row in range(0, queries.shape[0], block_len):
-        allowed = block_mask(seg_row, pad_row, start_row, block_len)
-        scores = (
-            jnp.einsum(
-                "qhe,khe->hqk",
-                queries[start_row : start_row + block_len],
-                key_rows,
-                preferred_element_type=jnp.float32,
-            )
-            * scaling
-        )
-        scores = jnp.where(allowed[None], scores, -1e30)
-        row_max = jnp.max(scores, axis=-1, keepdims=True)
-        shifted = jnp.exp(scores - row_max)
-        row_sum = jnp.sum(shifted, axis=-1, keepdims=True)
-        probs_low = (shifted / row_sum).astype(jnp.bfloat16)
-        out_parts.append(
-            jnp.einsum("hqk,khe->qhe", probs_low, values, preferred_element_type=jnp.float32)
-        )
-        lse_parts.append(row_max[..., 0] + jnp.log(row_sum[..., 0]))
-    return (jnp.concatenate(out_parts, 0), jnp.concatenate(lse_parts, 1))
-
-
-def attend_backward(
-    queries, key_rows, values, grad_out, row_lse, seg_row, pad_row, block_len, scaling
-):
-    grad_keys = jnp.zeros(key_rows.shape, jnp.float32)
-    grad_values = jnp.zeros(values.shape, jnp.float32)
-    query_parts = []
-    for start_row in range(0, queries.shape[0], block_len):
-        allowed = block_mask(seg_row, pad_row, start_row, block_len)
-        query_block = queries[start_row : start_row + block_len]
-        grad_block = grad_out[start_row : start_row + block_len]
-        scores = (
-            jnp.einsum("qhe,khe->hqk", query_block, key_rows, preferred_element_type=jnp.float32)
-            * scaling
-        )
-        scores = jnp.where(allowed[None], scores, -1e30)
-        probs = jnp.exp(scores - row_lse[:, start_row : start_row + block_len, None])
-        probs_low = probs.astype(jnp.bfloat16)
-        grad_probs = jnp.einsum(
-            "qhe,khe->hqk", grad_block, values, preferred_element_type=jnp.float32
-        )
-        inner_sum = jnp.sum(probs * grad_probs, axis=-1, keepdims=True)
-        grad_scores = (probs * (grad_probs - inner_sum)).astype(jnp.bfloat16)
-        query_parts.append(
-            jnp.einsum("hqk,khe->qhe", grad_scores, key_rows, preferred_element_type=jnp.float32)
-            * scaling
-        )
-        grad_keys = (
-            grad_keys
-            + jnp.einsum(
-                "hqk,qhe->khe", grad_scores, query_block, preferred_element_type=jnp.float32
-            )
-            * scaling
-        )
-        grad_values = grad_values + jnp.einsum(
-            "hqk,qhe->khe", probs_low, grad_block, preferred_element_type=jnp.float32
-        )
-    return (jnp.concatenate(query_parts, 0), grad_keys, grad_values)
+def lane_pad(width):
+    return -(-width // LANES) * LANES
+
+
+def regroup_body(moves, fill, x_ref, out_ref):
+    if fill is not None:
+        start, width = fill
+        for group in range(out_ref.shape[0]):
+            out_ref[group, :, start : start + width] = jnp.zeros((out_ref.shape[1], width), out_ref.dtype)
+    for from_group, start, to_group, target, width in moves:
+        if from_group is None:
+            values = x_ref[:, start : start + width]
+        else:
+            values = x_ref[from_group, :, start : start + width]
+        if to_group is None:
+            out_ref[:, target : target + width] = values
+        else:
+            out_ref[to_group, :, target : target + width] = values
+
+
+def split_groups(x, parts, groups):
+    tokens, total = x.shape
+    width = total // parts // groups
+    padded = lane_pad(parts * width) if parts > 1 else width
+    moves = [
+        (None, (part * groups + group) * width, group, part * width, width)
+        for group in range(groups)
+        for part in range(parts)
+    ]
+    fill = (parts * width, padded - parts * width) if padded > parts * width and parts > 1 else None
+    return pl.pallas_call(
+        partial(regroup_body, moves, fill),
+        out_shape=jax.ShapeDtypeStruct((groups, tokens, padded), x.dtype),
+        compiler_params=pltpu.CompilerParams(vmem_limit_bytes=VMEM_LIMIT),
+        name="split_groups_%d" % parts,
+    )(x)
+
+
+def join_groups(x, parts, width):
+    groups, tokens, _ = x.shape
+    moves = [
+        (group, part * width, None, (part * groups + group) * width, width)
+        for group in range(groups)
+        for part in range(parts)
+    ]
+    return pl.pallas_call(
+        partial(regroup_body, moves, None),
+        out_shape=jax.ShapeDtypeStruct((tokens, parts * groups * width), x.dtype),
+        compiler_params=pltpu.CompilerParams(vmem_limit_bytes=VMEM_LIMIT),
+        name="join_groups_%d" % parts,
+    )(x)
+
+
+QUERY_BLOCK = 256
+
+
+def key_bias(seg_col, pad_col, seg_row, first):
+    keys = seg_col.shape[0]
+    queries = seg_row.shape[1]
+    key_at = lax.broadcasted_iota(jnp.int32, (keys, queries), 0)
+    query_at = first + lax.broadcasted_iota(jnp.int32, (keys, queries), 1)
+    allowed = (seg_col == seg_row) & ((pad_col == 1) | (key_at == query_at))
+    return jnp.where(allowed, 0.0, -1e30)
+
+
+def spread_heads(rows_ref, held, heads):
+    held[...] = jnp.zeros_like(held)
+    for part in range(held.shape[0]):
+        for head in range(heads):
+            start = (part * heads + head) * HEAD_DIM
+            held[part, head, :, 0:HEAD_DIM] = rows_ref[:, start : start + HEAD_DIM]
+
+
+def probabilities(held, head, block, bias):
+    scores = lax.dot_general(
+        held[1, head], held[0, head, block, :], (((1,), (1,)), ((), ())), preferred_element_type=jnp.float32
+    )
+    scores = scores * (HEAD_DIM ** (-0.5)) + bias
+    shifted = jnp.exp(scores - jnp.max(scores, axis=0, keepdims=True))
+    return shifted * (1.0 / jnp.sum(shifted, axis=0, keepdims=True))
+
+
+def attention_body(heads, rows_ref, seg_col, pad_col, seg_row, out_ref, held):
+    step = pl.program_id(0)
+
+    @pl.when(step == 0)
+    def _():
+        spread_heads(rows_ref, held, heads)
+
+    first = pl.multiple_of(step * QUERY_BLOCK, QUERY_BLOCK)
+    block = pl.ds(first, QUERY_BLOCK)
+    bias = key_bias(seg_col[...], pad_col[...], seg_row[...], first)
+    for head in range(heads):
+        probs = probabilities(held, head, block, bias).astype(jnp.bfloat16)
+        result = lax.dot_general(
+            held[2, head], probs, (((0,), (0,)), ((), ())), preferred_element_type=jnp.float32
+        )
+        out_ref[:, head * HEAD_DIM : (head + 1) * HEAD_DIM] = result.T[:, :HEAD_DIM].astype(jnp.bfloat16)
+
+
+def attention(rows, segments, padding, heads):
+    length = rows.shape[0]
+    whole = pl.BlockSpec((length, 1), lambda i: (0, 0))
+    return pl.pallas_call(
+        partial(attention_body, heads),
+        out_shape=jax.ShapeDtypeStruct((length, heads * HEAD_DIM), jnp.bfloat16),
+        grid=(length // QUERY_BLOCK,),
+        in_specs=[
+            pl.BlockSpec(rows.shape, lambda i: (0, 0)),
+            whole,
+            whole,
+            pl.BlockSpec((1, QUERY_BLOCK), lambda i: (0, i)),
+        ],
+        out_specs=pl.BlockSpec((QUERY_BLOCK, heads * HEAD_DIM), lambda i: (i, 0)),
+        scratch_shapes=[pltpu.VMEM((3, heads, length, LANES), jnp.bfloat16)],
+        compiler_params=pltpu.CompilerParams(vmem_limit_bytes=VMEM_LIMIT),
+        name="attention",
+    )(rows, segments.reshape(length, 1), padding.reshape(length, 1), segments.reshape(1, length))
+
+
+def attention_grad_body(heads, rows_ref, grad_ref, seg_col, pad_col, seg_row, out_ref, held, given, grad_k, grad_v):
+    step = pl.program_id(0)
+    scaling = HEAD_DIM ** (-0.5)
+
+    @pl.when(step == 0)
+    def _():
+        spread_heads(rows_ref, held, heads)
+        given[...] = jnp.zeros_like(given)
+        grad_k[...] = jnp.zeros_like(grad_k)
+        grad_v[...] = jnp.zeros_like(grad_v)
+        out_ref[...] = jnp.zeros_like(out_ref)
+
+    first = pl.multiple_of(step * QUERY_BLOCK, QUERY_BLOCK)
+    block = pl.ds(first, QUERY_BLOCK)
+    bias = key_bias(seg_col[...], pad_col[...], seg_row[...], first)
+    for head in range(heads):
+        given[:, 0:HEAD_DIM] = grad_ref[:, head * HEAD_DIM : (head + 1) * HEAD_DIM]
+        upstream = given[...]
+        probs = probabilities(held, head, block, bias)
+        grad_v[head] += jnp.dot(probs.astype(jnp.bfloat16), upstream, preferred_element_type=jnp.float32)
+        grad_probs = lax.dot_general(
+            held[2, head], upstream, (((1,), (1,)), ((), ())), preferred_element_type=jnp.float32
+        )
+        inner = jnp.sum(probs * grad_probs, axis=0, keepdims=True)
+        grad_scores = (probs * (grad_probs - inner)).astype(jnp.bfloat16)
+        grad_k[head] += jnp.dot(grad_scores, held[0, head, block, :], preferred_element_type=jnp.float32)
+        grad_q = lax.dot_general(
+            held[1, head], grad_scores, (((0,), (0,)), ((), ())), preferred_element_type=jnp.float32
+        )
+        out_ref[block, head * HEAD_DIM : (head + 1) * HEAD_DIM] = (
+            grad_q.T[:, :HEAD_DIM] * scaling
+        ).astype(jnp.bfloat16)
+
+    @pl.when(step == pl.num_programs(0) - 1)
+    def _():
+        for head in range(heads):
+            start = (heads + head) * HEAD_DIM
+            out_ref[:, start : start + HEAD_DIM] = (grad_k[head][:, :HEAD_DIM] * scaling).astype(jnp.bfloat16)
+            start = (2 * heads + head) * HEAD_DIM
+            out_ref[:, start : start + HEAD_DIM] = grad_v[head][:, :HEAD_DIM].astype(jnp.bfloat16)
+
+
+def attention_grad(rows, grad, segments, padding, heads):
+    length = rows.shape[0]
+    whole = pl.BlockSpec((length, 1), lambda i: (0, 0))
+    return pl.pallas_call(
+        partial(attention_grad_body, heads),
+        out_shape=jax.ShapeDtypeStruct(rows.shape, jnp.bfloat16),
+        grid=(length // QUERY_BLOCK,),
+        in_specs=[
+            pl.BlockSpec(rows.shape, lambda i: (0, 0)),
+            pl.BlockSpec((QUERY_BLOCK, grad.shape[1]), lambda i: (i, 0)),
+            whole,
+            whole,
+            pl.BlockSpec((1, QUERY_BLOCK), lambda i: (0, i)),
+        ],
+        out_specs=pl.BlockSpec(rows.shape, lambda i: (0, 0)),
+        scratch_shapes=[
+            pltpu.VMEM((3, heads, length, LANES), jnp.bfloat16),
+            pltpu.VMEM((QUERY_BLOCK, LANES), jnp.bfloat16),
+            pltpu.VMEM((heads, length, LANES), jnp.float32),
+            pltpu.VMEM((heads, length, LANES), jnp.float32),
+        ],
+        compiler_params=pltpu.CompilerParams(vmem_limit_bytes=VMEM_LIMIT),
+        name="attention_grad",
+    )(rows, grad, segments.reshape(length, 1), padding.reshape(length, 1), segments.reshape(1, length))
 
 
 def shards(
@@ -1229,8 +1342,6 @@
     full_len = segment_ids.shape[1]
     heads_local = HEADS // seq_count
     group_width = model_width // seq_count
-    scaling = HEAD_DIM ** (-0.5)
-    block_len = min(512, full_len)
     token_start = seq_place * local_len
     local_seg = lax.dynamic_slice_in_dim(segment_ids, token_start, local_len, 1)
     local_pad = lax.dynamic_slice_in_dim(padding, token_start, local_len, 1).astype(jnp.float32)
@@ -1247,29 +1358,19 @@
         jnp.einsum("rtd,dc->rtc", attend_in, attend_weight, preferred_element_type=jnp.float32)
         + triple_bias
     )
-    triple_low = triple.astype(jnp.bfloat16).reshape(rows_dev, local_len, 3, model_width)
-    head_rows = lax.all_to_all(triple_low, "seq", split_axis=3, concat_axis=1, tiled=True)
+    triple_low = split_groups(triple[0].astype(jnp.bfloat16), 3, seq_count)
+    head_rows = lax.all_to_all(triple_low, "seq", split_axis=0, concat_axis=0, tiled=True)
     (head_rows, output_weight, hidden_weight, return_weight, proj_three) = lax.optimization_barrier(
         (head_rows, output_weight, hidden_weight, return_weight, proj_three)
     )
-    head_view = head_rows.reshape(rows_dev, full_len, 3, heads_local, HEAD_DIM)
-    row_index = 0
-    head_out, head_lse = attend_forward(
-        head_view[row_index, :, 0],
-        head_view[row_index, :, 1],
-        head_view[row_index, :, 2],
-        segment_ids[row_index],
-        padding[row_index],
-        block_len,
-        scaling,
-    )
-    attended_parts = [head_out.astype(jnp.bfloat16).reshape(full_len, group_width)]
-    lse_rows = [head_lse]
-    head_attended = jnp.stack(attended_parts)
+    head_rows = head_rows.reshape(full_len, head_rows.shape[-1])
+    head_attended = attention(head_rows, segment_ids[0], padding[0], heads_local)
+    head_attended = head_attended.reshape(seq_count, local_len, group_width)
     head_attended, packed = lax.optimization_barrier((head_attended, packed))
     proj_one, proj_two = (unpack_weight(index, packed, slot_count, firsts, lasts, starts) for index in (11, 13))
-    attended = lax.all_to_all(head_attended, "seq", split_axis=1, concat_axis=2, tiled=True)
+    attended = lax.all_to_all(head_attended, "seq", split_axis=0, concat_axis=0, tiled=True)
     attended, proj_one, proj_two = lax.optimization_barrier((attended, proj_one, proj_two))
+    attended = join_groups(attended, 1, group_width)[None]
     branch_one = (
         jnp.einsum("rtd,dc->rtc", attended, output_weight, preferred_element_type=jnp.float32)
         + output_bias
@@ -1364,33 +1465,19 @@
     grad_attended = jnp.einsum(
         "rtc,dc->rtd", grad_branch_one, output_weight, preferred_element_type=jnp.float32
     ).astype(jnp.bfloat16)
+    grad_attended = split_groups(grad_attended[0], 1, seq_count)
     grad_attended, second_low = lax.optimization_barrier((grad_attended, second_low))
-    head_grad = lax.all_to_all(grad_attended, "seq", split_axis=2, concat_axis=1, tiled=True)
+    head_grad = lax.all_to_all(grad_attended, "seq", split_axis=0, concat_axis=0, tiled=True)
     grad_buffer = put(None, 15, second_low, grad_projected)
     grad_buffer = put(grad_buffer, 11, feature, grad_first)
     head_grad, grad_buffer = lax.optimization_barrier((head_grad, grad_buffer))
-    row_index = 0
-    grad_query, grad_key, grad_value = attend_backward(
-        head_view[row_index, :, 0],
-        head_view[row_index, :, 1],
-        head_view[row_index, :, 2],
-        head_grad[row_index].reshape(full_len, heads_local, HEAD_DIM),
-        lse_rows[row_index],
-        segment_ids[row_index],
-        padding[row_index],
-        block_len,
-        scaling,
-    )
-    triple_parts = [
-        jnp.stack([grad_query, grad_key, grad_value], 1).reshape(full_len, 3, group_width)
-    ]
-    grad_triple_heads = jnp.stack(triple_parts).astype(jnp.bfloat16)
+    grad_triple_heads = attention_grad(
+        head_rows, head_grad.reshape(full_len, group_width), segment_ids[0], padding[0], heads_local
+    ).reshape(seq_count, local_len, head_rows.shape[-1])
     grad_triple_heads, grad_buffer, cond_low = lax.optimization_barrier(
         (grad_triple_heads, grad_buffer, cond_low)
     )
-    grad_triple = lax.all_to_all(
-        grad_triple_heads, "seq", split_axis=1, concat_axis=3, tiled=True
-    ).reshape(rows_dev, local_len, 3 * model_width)
+    grad_triple = lax.all_to_all(grad_triple_heads, "seq", split_axis=0, concat_axis=0, tiled=True)
     grad_buffer = put(grad_buffer, 13, first_low, grad_second)
     grad_buffer = put(grad_buffer, 9, activated, grad_branch_two)
     grad_buffer = put(grad_buffer, 7, mlp_in, grad_hidden)
@@ -1399,6 +1486,7 @@
     image_rows = cond_all.shape[0]
     cond_own = own_conditions(cond_all.reshape(image_rows * SEGS, D), own_first, slot_count)
     grad_triple, grad_buffer, cond_own = lax.optimization_barrier((grad_triple, grad_buffer, cond_own))
+    grad_triple = join_groups(grad_triple, 3, group_width)[None]
     grad_buffer = put(grad_buffer, 2, attend_in, grad_triple)
     triple_sums = summed(grad_triple)
     grad_attend_in = jnp.einsum(

time: 1150 us -> 1070 us (0.930)
  Pallas kernels: 814 us -> 872 us
  local copies, waits for them, and re-layouts: 82.3 us -> 32.6 us
  other arithmetic: 63.4 us -> 26.8 us
  matrix products: 121 us -> 88.5 us
  waiting for transfers between devices: 26.7 us -> 5.47 us
    pallas_call x0 -> x6, Pallas kernels: none -> 58.7 us  [the longest x1 28.7 us: attention_grad(): pl.pallas_call(partial(attention_grad_body, heads), out_shape=jax.ShapeDt...]
    dot_general x12 -> x0, matrix products: 31.5 us -> none  [the longest x2 9.74 us: attend_backward(): jnp.einsum('qhe,khe->hqk', grad_block, values, preferred_element_type=jnp...]
    all_to_all x4, waiting for transfers between devices: 26.7 us -> 5.47 us  [the longest x1 4.12 us: shards(): lax.all_to_all(triple_low, 'seq', split_axis=0, concat_axis=0, tiled=True)]
    all_to_all x8 -> x0, local copies, waits for them, and re-layouts: 14.6 us -> none  [the longest x3 8.24 us: shards(): lax.all_to_all(head_attended, 'seq', split_axis=1, concat_axis=2, tiled=T...]
    unnamed x9 -> x5, other arithmetic: 14.9 us -> 3.22 us
  transfers between devices with their start and end apart: 4 -> 4, of which waited for: 3 -> 2; matrix products, arithmetic and copies ran while one was open for 1% -> 1% of each run, Pallas kernels for 10% -> 11%
where the time goes in v3:
time: 1070 us; the launch traced here: 1060 us
  Pallas kernels  872 us (81%)
  matrix products  88.5 us (8%)
  local copies, waits for them, and re-layouts  32.6 us (3%)
  other arithmetic  26.8 us (3%)
  starting transfers between devices  19.7 us (2%)
  blocking collectives  10.9 us (1%)
    pallas_call x1, Pallas kernels, gather_slots(): pl.pallas_call(partial(gather_body, side, seq_count, steps, parts), out_s...  320 us
    pallas_call x1, Pallas kernels, reduce_slots(): pl.pallas_call(partial(reduce_body, side, seq_count, steps, parts), out_s...  317 us
    pallas_call x8, Pallas kernels, unpack_weight(): pl.pallas_call(partial(unpack_body, base, row // SUBS, per_chunk, tiles,...  87 us
    pallas_call x7, Pallas kernels, weight_grad(): pl.pallas_call(partial(weight_grad_body, base, row // SUBS, per_chunk, sh...  66.4 us
    pallas_call x1, Pallas kernels, attention_grad(): pl.pallas_call(partial(attention_grad_body, heads), out_shape=jax.ShapeDt...  28.7 us
  transfers between devices with their start and end apart: 4, of which 2 were waited for; matrix products, arithmetic and copies ran while one was open for 1% of the time, Pallas kernels for 11%

profile of v3, /device:TPU:1, one launch (start us, length us, event | category | flops | bytes accessed | tf_op | source)
XLA Modules:
  0.0 1058.5 jit_solution(17509377011808910711)
XLA Ops:
  1.5 2.8 convert_element_type.193
  4.4 2.6 reshape.619.own_ref
  7.0 320.0 %gather_slots.1 = bf16[8,4,9792,128]{3,2,1,0:T(8,128)(2,1)} custom-call(bf16[9792,128]{1,0:T(8,128)(2,1)} %reshape.619.own_ref), custom_call_target="tpu_custom_call" | custom-call | tf_op jit(solution)/shard_map/gather_slots/pallas_call | solution.py:578
  328.4 2.2 edge_read.1
  331.4 1.4 fusion.50
  333.4 17.0 %unpack_0.1.weight_ref = bf16[1152,6912]{1,0:T(8,128)(2,1)} custom-call(s32[52]{0:T(128)} %get-tuple-element.89.first_ref, s32[52]{0:T(128)} %get-tuple-element.88.last_ref, s32[33]{0:T(128)} %copy-done, bf16[313344,128]{1,0:T(8,128)(2,1)} %bitcast.3.packed), custom_call_target="tpu_custom_call" | custom-call | bytes 31850496 | tf_op jit(solution)/shard_map/unpack_0/pallas_call | solution.py:137
  350.5 11.5 %unpack_2.1 = bf16[1152,3456]{1,0:T(8,128)(2,1)} custom-call(s32[52]{0:T(128)} %get-tuple-element.89.first_ref, s32[52]{0:T(128)} %get-tuple-element.88.last_ref, s32[33]{0:T(128)} %copy-done, bf16[313344,128]{1,0:T(8,128)(2,1)} %bitcast.3.packed), custom_call_target="tpu_custom_call" | custom-call | bytes 15925248 | tf_op jit(solution)/shard_map/unpack_2/pallas_call | solution.py:137
  363.1 7.7 convolution_add_fusion
  370.8 3.0 convolution_bitcast_fusion
  373.8 2.9 copy-done.2
  377.9 7.0 fusion.1.x_ref
  384.9 3.4 split_groups_3.1
  388.3 7.0 all-to-all-start
  395.3 5.1 unpack_5.1
  400.4 13.3 %unpack_7.1 = bf16[1152,4608]{1,0:T(8,128)(2,1)} custom-call(s32[52]{0:T(128)} %get-tuple-element.89.first_ref, s32[52]{0:T(128)} %get-tuple-element.88.last_ref, s32[33]{0:T(128)} %copy-done, bf16[313344,128]{1,0:T(8,128)(2,1)} %bitcast.3.packed), custom_call_target="tpu_custom_call" | custom-call | bytes 21233664 | tf_op jit(solution)/shard_map/unpack_7/pallas_call | solution.py:137
  413.7 13.3 %unpack_9.1 = bf16[4608,1152]{1,0:T(8,128)(2,1)} custom-call(s32[52]{0:T(128)} %get-tuple-element.89.first_ref, s32[52]{0:T(128)} %get-tuple-element.88.last_ref, s32[33]{0:T(128)} %copy-done, bf16[313344,128]{1,0:T(8,128)(2,1)} %bitcast.3.packed), custom_call_target="tpu_custom_call" | custom-call | bytes 21233664 | tf_op jit(solution)/shard_map/unpack_9/pallas_call | solution.py:137
  427.0 4.4 unpack_15.1
  433.4 4.1 all-to-all-done
  438.8 18.8 %attention.1 = bf16[1024,288]{1,0:T(8,128)(2,1)} custom-call(bf16[1024,896]{1,0:T(8,128)(2,1)} %bitcast.163, s32[1024,1]{1,0:T(8,128)} %copy.44.seg_col, s32[1024,1]{1,0:T(8,128)} %copy.45.pad_col, s32[1,1024]{1,0:T(1,128)} %seg_row.3), custom_call_target="tpu_custom_call" | custom-call | tf_op jit(solution)/shard_map/attention/pallas_call | solution.py:1198
  457.6 2.2 copy.46
  459.8 4.2 all-to-all-start.1
  466.1 8.6 unpack_11.1
  474.7 13.8 %unpack_13.1 = bf16[2048,2048]{1,0:T(8,128)(2,1)} custom-call(s32[52]{0:T(128)} %get-tuple-element.89.first_ref, s32[52]{0:T(128)} %get-tuple-element.88.last_ref, s32[33]{0:T(128)} %copy-done, bf16[313344,128]{1,0:T(8,128)(2,1)} %bitcast.3.packed), custom_call_target="tpu_custom_call" | custom-call | bytes 16777216 | tf_op jit(solution)/shard_map/unpack_13/pallas_call | solution.py:137
  488.5 2.3 copy.47.x_ref
  490.8 2.2 join_groups_1.1.x_ref
  493.0 3.5 fusion.80
  496.8 2.5 fusion.36.x_ref
  499.4 11.2 %multiply_convert_fusion = (bf16[256,4608]{1,0:T(8,128)(2,1)S(1)}, f32[256,4608]{1,0:T(8,128)}) fusion(f32[4608]{0:T(1024)S(1)} %fusion.46, bf16[256,1152]{1,0:T(8,128)(2,1)S(1)} %fusion.36.x_ref, bf16[1152,4608]{1,0:T(8,128)(2,1)} %unpack_7.1), kind=kOutput, calls=%fused_computation.18 | convolution fusion | flops 2729705472 | bytes 18302976 | tf_op jit(solution)/shard_map/rtd,df->rtf/dot_general | solution.py:1382
  510.7 4.4 add_convert_fusion
  515.1 3.1 multiply_convert_fusion.2
  518.2 6.1 convolution_add_fusion.5
  524.4 1.5 fusion.75
  526.6 1.5 multiply_reduce_fusion.2
  529.2 2.0 convert_reduce_fusion.2
  531.2 7.9 convert_reduce_fusion.3
  539.1 2.3 convert_reduce_fusion.5
  541.4 9.6 convert_reduce_fusion
  550.9 8.3 multiply_reduce_fusion
  560.3 1.9 convert_reduce_fusion.6
  563.0 1.9 convolution_convert_fusion.1.x_ref
  564.9 2.2 split_groups_1.1
  567.1 2.2 copy.48
  569.3 4.9 all-to-all-start.2
  574.3 5.6 weight_grad_15.1
  579.9 8.4 weight_grad_11.1
  590.8 28.7 %attention_grad.1 = bf16[1024,896]{1,0:T(8,128)(2,1)} custom-call(bf16[1024,896]{1,0:T(8,128)(2,1)} %bitcast.164, bf16[1024,288]{1,0:T(8,128)(2,1)} %bitcast.168, s32[1024,1]{1,0:T(8,128)} %copy.44.seg_col, s32[1024,1]{1,0:T(8,128)} %copy.45.pad_col, s32[1,1024]{1,0:T(1,128)} %seg_row.3), custom_call_target="tpu_custom_call" | custom-call | tf_op jit(solution)/shard_map/attention_grad/pallas_call | solution.py:1260
  619.5 3.6 all-to-all-start.3
  625.7 1.9 pad_add_fusion.1.own_ref
  627.5 10.9 %all_gather.3 = bf16[8,4,1152]{2,1,0:T(4,128)(2,1)S(1)} all-gather(bf16[1,4,1152]{2,1,0:T(4,128)(2,1)S(1)} %fusion.42), channel_id=1, replica_groups=mesh['dp'=8,'seq'=4] {'dp'}, dimensions={0}, use_global_device_ids=true | all-gather | bytes 82944 | tf_op jit(solution)/shard_map/all_gather | solution.py:1485
  639.4 12.3 %weight_grad_13.1 = (bf16[313344,128]{1,0:T(8,128)(2,1)}, f32[32,128]{1,0:T(8,128)}) custom-call(s32[52]{0:T(128)} %get-tuple-element.89.first_ref, s32[52]{0:T(128)} %get-tuple-element.88.last_ref, s32[33]{0:T(128)} %copy-done, bf16[256,2048]{1,0:T(8,128)(2,1)} %copy-done.30, bf16[256,2048]{1,0:T(8,128)(2,1)} %copy-done.31, ...), custom_call_target="tpu_custom_call", output_to_operand_aliasing={{0}: (5, {})} | custom-call | flops 2147483648 | bytes 8388608 | tf_op jit(solution)/shard_map/weight_grad_13/pallas_call | solution.py:329
  651.7 11.8 %weight_grad_9.1 = (bf16[313344,128]{1,0:T(8,128)(2,1)}, f32[32,128]{1,0:T(8,128)}) custom-call(s32[52]{0:T(128)} %get-tuple-element.89.first_ref, s32[52]{0:T(128)} %get-tuple-element.88.last_ref, s32[33]{0:T(128)} %copy-done, bf16[256,4608]{1,0:T(8,128)(2,1)} %copy-done.23, bf16[256,1152]{1,0:T(8,128)(2,1)} %bitcast.171, ...), custom_call_target="tpu_custom_call", output_to_operand_aliasing={{0}: (5, {})} | custom-call | flops 2717908992 | bytes 10616832 | tf_op jit(solution)/shard_map/weight_grad_9/pallas_call | solution.py:329
  663.5 11.4 %weight_grad_7.1 = (bf16[313344,128]{1,0:T(8,128)(2,1)}, f32[32,128]{1,0:T(8,128)}) custom-call(s32[52]{0:T(128)} %get-tuple-element.89.first_ref, s32[52]{0:T(128)} %get-tuple-element.88.last_ref, s32[33]{0:T(128)} %copy-done, bf16[256,1152]{1,0:T(8,128)(2,1)} %copy-done.25, bf16[256,4608]{1,0:T(8,128)(2,1)} %copy-done.24, ...), custom_call_target="tpu_custom_call", output_to_operand_aliasing={{0}: (5, {})} | custom-call | flops 2717908992 | bytes 10616832 | tf_op jit(solution)/shard_map/weight_grad_7/pallas_call | solution.py:329
  674.9 5.9 weight_grad_5.1
  682.1 3.4 join_groups_3.1.dy_ref
  685.5 6.8 constant_dynamic-update-slice_fusion.1
  692.6 2.8 fusion.78
  695.4 2.9 copy-done.16
  698.3 11.0 %weight_grad_2.1 = (bf16[313344,128]{1,0:T(8,128)(2,1)}, f32[32,128]{1,0:T(8,128)}) custom-call(s32[52]{0:T(128)} %get-tuple-element.89.first_ref, s32[52]{0:T(128)} %get-tuple-element.88.last_ref, s32[33]{0:T(128)} %copy-done, bf16[256,1152]{1,0:T(8,128)(2,1)} %copy-done.22, ...), custom_call_target="tpu_custom_call", output_to_operand_aliasing={{0}: (5, {})} | custom-call | flops 2038431744 | bytes 7962624 | tf_op jit(solution)/shard_map/weight_grad_2/pallas_call | solution.py:329
  709.9 3.0 multiply_dynamic-update-slice_fusion.2
  715.9 2.4 convolution_convert_fusion
  718.9 2.3 edge_write.1
  721.3 316.5 %reduce_slots.1 = (bf16[9792,128]{1,0:T(8,128)(2,1)}, f32[8,216,128]{2,1,0:T(8,128)}, f32[8,1152]{1,0:T(8,128)}) custom-call(bf16[8,4,9792,128]{3,2,1,0:T(8,128)(2,1)} %bitcast.53.parts_ref, bf16[224,128]{1,0:T(8,128)(2,1)} %pad.4.part_ref, bf16[1152,6912]{1,0:T(8,128)(2,1)} %unpack_0.1.weight_ref), custom_call_target="tpu_custom_call" | custom-call | tf_op jit(solution)/shard_map/reduce_slots/pallas_call | solution.py:957
  1037.8 1.4 fusion.44
  1039.2 19.0 %update.1 = (f32[612,2048]{1,0:T(8,128)}, f32[612,2048]{1,0:T(8,128)}, f32[612,2048]{1,0:T(8,128)}) custom-call(s32[2]{0:T(128)} %pad_add_fusion.1.own_ref, bf16[9792,128]{1,0:T(8,128)(2,1)} %get-tuple-element.80.reduced, bf16[200,32]{1,0:T(8,128)(2,1)} %copy.53.cond_ref, f32[1728,128]{1,0:T(8,128)} %bitcast.173, f32[612,2048]{1,0:T(8,128)} %master.1, ...), custom_call_target="tpu_custom_call" | custom-call | tf_op jit(solution)/shard_map/update/pallas_call | solution.py:1051
  (189 shorter events, 26.6 us)
Async XLA Ops:
  7.0 320.1 %copy-start.57 = (s32[18]{0:T(128)S(1)}, s32[18]{0:T(128)}, u32[]{:S(2)}) copy-start(s32[18]{0:T(128)} %constant.122.clone) | copy-start | bytes 220
  327.0 3.6 copy-start
  328.4 4.3 copy-start.55
  328.4 4.3 copy-start.56
  350.5 11.6 %copy-start.7 = (bf16[1,256,1152]{2,1,0:T(8,128)(2,1)S(1)}, bf16[1,256,1152]{2,1,0:T(8,128)(2,1)}, u32[]{:S(2)}) copy-start(bf16[1,256,1152]{2,1,0:T(8,128)(2,1)} %param.12) | copy-start | bytes 1769476
  350.5 12.6 %copy-start.38 = (s32[1,1024]{1,0:T(1,128)S(1)}, s32[1,1024]{1,0:T(1,128)}, u32[]{:S(2)}) copy-start(s32[1,1024]{1,0:T(1,128)} %seg_row.3) | copy-start | bytes 12292
  350.5 12.6 %copy-start.34 = (bf16[1,4,1152]{2,1,0:T(4,128)(2,1)S(1)}, bf16[1,4,1152]{2,1,0:T(4,128)(2,1)}, u32[]{:S(2)}) copy-start(bf16[1,4,1152]{2,1,0:T(4,128)(2,1)} %param.13) | copy-start | bytes 27652
  362.2 11.6 %copy-start.43 = (f32[256]{0:T(256)}, f32[256]{0:T(256)S(1)}, u32[]{:S(2)}) copy-start(f32[256]{0:T(256)S(1)} %broadcast_multiply_fusion.2) | copy-start | bytes 3076
  363.1 10.7 %copy-start.47 = (f32[256]{0:T(256)}, f32[256]{0:T(256)S(1)}, u32[]{:S(2)}) copy-start(f32[256]{0:T(256)S(1)} %fusion.60) | copy-start | bytes 3076
  363.1 7.7 copy-start.39
  373.8 2.9 copy-start.2
  388.3 49.3 %all-to-all-start = ((bf16[4,256,896]{2,1,0:T(8,128)(2,1)}), bf16[4,256,896]{2,1,0:T(8,128)(2,1)S(1)}, u32[]{:S(2)}, u32[]{:S(2)}) async-start(bf16[4,256,896]{2,1,0:T(8,128)(2,1)} %split_groups_3.1), calls=%async_computation | async-start | bytes 3670016 | tf_op jit(solution)/shard_map/all_to_all | solution.py:1362
  427.0 5.4 copy-start.52
  459.8 28.7 %all-to-all-start.1 = ((bf16[4,256,288]{1,2,0:T(8,128)(2,1)}), bf16[4,256,288]{1,2,0:T(8,128)(2,1)}, u32[]{:S(2)}, u32[]{:S(2)}) async-start(bf16[4,256,288]{1,2,0:T(8,128)(2,1)} %copy.46), calls=%async_computation.1 | async-start | bytes 1179648 | tf_op jit(solution)/shard_map/all_to_all | solution.py:1371
  474.7 18.3 %copy-start.10 = (bf16[1152,1152]{1,0:T(8,128)(2,1)S(1)}, bf16[1152,1152]{1,0:T(8,128)(2,1)}, u32[]{:S(2)}) copy-start(bf16[1152,1152]{1,0:T(8,128)(2,1)} %unpack_5.1) | copy-start | bytes 7962628
  488.5 4.5 copy-start.8
  488.5 4.5 copy-start.37
  496.5 62.7 %copy-start.3 = (f32[1,256,1152]{2,1,0:T(8,128)}, f32[1,256,1152]{2,1,0:T(8,128)S(1)}, u32[]{:S(2)}) copy-start(f32[1,256,1152]{2,1,0:T(8,128)S(1)} %get-tuple-element.104) | copy-start | bytes 3538948
  496.5 62.7 %copy-start.41 = (f32[256]{0:T(256)}, f32[256]{0:T(256)S(1)}, u32[]{:S(2)}) copy-start(f32[256]{0:T(256)S(1)} %broadcast_multiply_fusion.1) | copy-start | bytes 3076
  496.5 14.1 %slice-start = ((s8[7077888]{0:T(1024)(128)(4,1)}), s8[4194304]{0:T(1024)(128)(4,1)S(1)}, s32[]{:S(2)}) async-start(s8[7077888]{0:T(1024)(128)(4,1)} %bitcast.159), calls=%async_computation.4 | async-start | bytes 8388608
  496.8 62.5 %copy-start.45 = (f32[256]{0:T(256)}, f32[256]{0:T(256)S(1)}, u32[]{:S(2)}) copy-start(f32[256]{0:T(256)S(1)} %fusion.61) | copy-start | bytes 3076
  496.8 13.8 %slice-start.4 = ((s8[10616832]{0:T(1024)(128)(4,1)}), s8[4194304]{0:T(1024)(128)(4,1)S(1)}, s32[]{:S(2)}) async-start(s8[10616832]{0:T(1024)(128)(4,1)} %bitcast.165), calls=%async_computation.8 | async-start | bytes 8388608
  496.8 18.3 %slice-start.2 = ((s8[4718592]{0:T(1024)(128)(4,1)}), s8[4194304]{0:T(1024)(128)(4,1)S(1)}, s32[]{:S(2)}) async-start(s8[4718592]{0:T(1024)(128)(4,1)} %bitcast.161), calls=%async_computation.6 | async-start | bytes 8388608
  499.4 11.3 %copy-start.25 = (bf16[256,1152]{1,0:T(8,128)(2,1)}, bf16[256,1152]{1,0:T(8,128)(2,1)S(1)}, u32[]{:S(2)}) copy-start(bf16[256,1152]{1,0:T(8,128)(2,1)S(1)} %fusion.36.x_ref) | copy-start | bytes 1769476
  499.4 11.3 %slice-start.1 = ((s8[7077888]{0:T(1024)(128)(4,1)}), s8[2883584]{0:T(1024)(128)(4,1)S(1)}, s32[]{:S(2)}) async-start(s8[7077888]{0:T(1024)(128)(4,1)} %bitcast.159), calls=%async_computation.5 | async-start | bytes 5767168
  499.4 11.3 %slice-start.5 = ((s8[10616832]{0:T(1024)(128)(4,1)}), s8[4194304]{0:T(1024)(128)(4,1)S(1)}, s32[]{:S(2)}) async-start(s8[10616832]{0:T(1024)(128)(4,1)} %bitcast.165), calls=%async_computation.9 | async-start | bytes 8388608
  499.4 11.3 %slice-start.6 = ((s8[10616832]{0:T(1024)(128)(4,1)}), s8[2228224]{0:T(1024)(128)(4,1)S(1)}, s32[]{:S(2)}) async-start(s8[10616832]{0:T(1024)(128)(4,1)} %bitcast.165), calls=%async_computation.10 | async-start | bytes 4456448
  499.4 11.3 %copy-start.51 = (f32[1152]{0:T(1024)S(1)}, f32[1152]{0:T(1024)}, u32[]{:S(2)}) copy-start(f32[1152]{0:T(1024)} %get-tuple-element.112) | copy-start | bytes 13828
  499.4 15.7 %slice-start.3 = ((s8[4718592]{0:T(1024)(128)(4,1)}), s8[524288]{0:T(1024)(128)(4,1)S(1)}, s32[]{:S(2)}) async-start(s8[4718592]{0:T(1024)(128)(4,1)} %bitcast.161), calls=%async_computation.7 | async-start | bytes 1048576
  510.6 4.5 copy-start.23
  515.1 3.1 copy-start.32
  518.2 6.1 copy-start.30
  524.3 2.3 copy-start.20
  526.6 1.5 copy-start.27
  529.2 2.0 copy-start.33
  531.2 7.9 copy-start.31
  531.2 7.9 copy-start.29
  539.1 2.3 copy-start.19
  541.4 9.6 copy-start.26
  541.4 18.9 %copy-start.13 = (f32[1,256,1152]{2,1,0:T(8,128)}, f32[1,256,1152]{2,1,0:T(8,128)S(1)}, u32[]{:S(2)}) copy-start(f32[1,256,1152]{2,1,0:T(8,128)S(1)} %get-tuple-element.129) | copy-start | bytes 3538948
  550.9 8.3 copy-start.24
  564.9 9.4 copy-start.35
  569.3 20.3 %all-to-all-start.2 = ((bf16[4,256,288]{1,2,0:T(8,128)(2,1)}), bf16[4,256,288]{1,2,0:T(8,128)(2,1)S(1)}, u32[]{:S(2)}, u32[]{:S(2)}) async-start(bf16[4,256,288]{1,2,0:T(8,128)(2,1)} %copy.48), calls=%async_computation.2 | async-start | bytes 1179648 | tf_op jit(solution)/shard_map/all_to_all | solution.py:1470
  619.5 3.6 copy-start.1
  619.5 4.9 copy-start.53
  619.5 5.6 copy-start.54
  619.5 61.3 %all-to-all-start.3 = ((bf16[4,256,896]{2,1,0:T(8,128)(2,1)}), bf16[4,256,896]{2,1,0:T(8,128)(2,1)S(1)}, u32[]{:S(2)}, u32[]{:S(2)}) async-start(bf16[4,256,896]{2,1,0:T(8,128)(2,1)} %bitcast.167), calls=%async_computation.3 | async-start | bytes 3670016 | tf_op jit(solution)/shard_map/all_to_all | solution.py:1480
  680.8 4.6 copy-start.9
  680.8 4.6 copy-start.44
  680.8 1.2 copy-start.15
  685.5 6.8 copy-start.6
  685.5 7.1 copy-start.50
  685.5 7.2 copy-start.48
  695.4 2.9 copy-start.16
  698.3 11.6 %copy-start.17 = (f32[1,256,6912]{2,1,0:T(8,128)S(1)}, f32[1,256,6912]{2,1,0:T(8,128)}, u32[]{:S(2)}) copy-start(f32[1,256,6912]{2,1,0:T(8,128)} %copy-done.16) | copy-start | bytes 21233668
  698.3 11.6 %copy-start.18 = (f32[1,256,1152]{2,1,0:T(8,128)S(1)}, f32[1,256,1152]{2,1,0:T(8,128)}, u32[]{:S(2)}) copy-start(f32[1,256,1152]{2,1,0:T(8,128)} %get-tuple-element.98) | copy-start | bytes 3538948
  709.9 3.0 copy-start.12
  712.9 1.3 copy-start.4
  712.9 1.3 copy-start.42
  712.9 1.3 copy-start.46
  714.1 1.3 copy-start.14
  714.1 1.6 copy-start.28
  714.4 1.5 copy-start.40
  721.2 316.6 %copy-start.36 = (bf16[1,4,1152]{2,1,0:T(4,128)(2,1)S(1)}, bf16[1,4,1152]{2,1,0:T(4,128)(2,1)}, u32[]{:S(2)}) copy-start(bf16[1,4,1152]{2,1,0:T(4,128)(2,1)} %param.13) | copy-start | bytes 27652
  (5 other events, 4.5 us)

commit v4 on v3

--- a/solution.py
+++ b/solution.py
@@ -228,11 +228,12 @@
     )(table, *arrays, buffer)
 
 
-def weight_grad_body(base, first_tile, per_chunk, shift, chunk, col_blocks, slots, piece, chained,
-                     first_ref, last_ref, starts_ref, x_ref, dy_ref, *rest):
+def weight_grad_body(base, first_tile, per_chunk, shift, chunk, col_blocks, slots, plan, piece, chained,
+                     first_ref, last_ref, starts_ref, guests_ref, x_ref, dy_ref, *rest):
     if chained:
         rest = rest[1:]
     out, ends_ref, wide, narrow, sems = rest
+    hosts, kept = plan
     step = pl.program_id(0)
     steps = pl.num_programs(0)
     slot = step % 2
@@ -279,11 +280,9 @@
 
     low_tile = first_tile + step * per_chunk
 
-    def one(owner, carry):
-        begin = jnp.maximum(starts_ref[owner], low_tile)
-        end = jnp.minimum(starts_ref[owner + 1], low_tile + per_chunk)
+    def run(begin, end, place):
         size = pl.multiple_of(jnp.maximum(end - begin, 0) * SUBS, SUBS)
-        target = pl.multiple_of((owner * slots + begin - starts_ref[owner]) * SUBS, SUBS)
+        target = pl.multiple_of(place * SUBS, SUBS)
         origin = pl.multiple_of((begin - low_tile) * SUBS, SUBS)
 
         @pl.when(end > begin)
@@ -292,6 +291,14 @@
                 narrow.at[slot, pl.ds(origin, size)], out.at[pl.ds(target, size)], sems.at[slot]
             ).start()
 
+    def one(owner, carry):
+        begin = jnp.maximum(starts_ref[owner], low_tile)
+        end = jnp.minimum(starts_ref[owner + 1], low_tile + per_chunk)
+        turn = starts_ref[owner] + kept
+        run(begin, jnp.minimum(end, turn), owner * kept + begin - starts_ref[owner])
+        if hosts:
+            begin = jnp.maximum(begin, turn)
+            run(begin, end, guests_ref[owner] + begin - turn)
         return carry
 
     lax.fori_loop(first_ref[base + step], last_ref[base + step] + 1, one, 0)
@@ -305,7 +312,7 @@
             drain(1 - slot)
 
 
-def weight_grad(index, left, right, buffer, owners, slots, firsts, lasts, starts):
+def weight_grad(index, left, right, buffer, owners, slots, firsts, lasts, starts, guests, plan):
     depth, width = param_shapes()[index]
     tokens = left.shape[0]
     chunk = CHUNK[index]
@@ -315,26 +322,26 @@
     shift = row % SUBS
     per_chunk = chunk * col_blocks // SUBS
     base = chunk_spans()[1][index]
-    shape = (owners * slots * SUBS, LANES)
+    shape = (owners * plan[1] * SUBS, LANES)
     in_specs = [
         pl.BlockSpec((tokens, chunk), lambda i, *_: (0, i)),
         pl.BlockSpec((tokens, width), lambda i, *_: (0, 0)),
     ]
-    operands = [firsts, lasts, starts, left, right]
+    operands = [firsts, lasts, starts, guests, left, right]
     aliases = {}
     if buffer is not None:
         in_specs.append(pl.BlockSpec(memory_space=pl.ANY))
         operands.append(buffer)
-        aliases = {5: 0}
+        aliases = {6: 0}
     return pl.pallas_call(
-        partial(weight_grad_body, base, row // SUBS, per_chunk, shift, chunk, col_blocks, slots, piece,
+        partial(weight_grad_body, base, row // SUBS, per_chunk, shift, chunk, col_blocks, slots, plan, piece,
                 buffer is not None),
         out_shape=(
             jax.ShapeDtypeStruct(shape, jnp.bfloat16),
             jax.ShapeDtypeStruct((2 * SUBS, LANES), jnp.float32),
         ),
         grid_spec=pltpu.PrefetchScalarGridSpec(
-            num_scalar_prefetch=3,
+            num_scalar_prefetch=4,
             grid=(depth // chunk,),
             in_specs=in_specs,
             out_specs=(
@@ -398,12 +405,50 @@
                 found.append(self.device(axis, self.other(axis, k)))
         return found
 
-    def greet(self):
+    def greet(self, hosting=None):
         barrier = pltpu.get_barrier_semaphore()
         partners = self.partners()
         for partner in partners:
             pl.semaphore_signal(barrier, inc=1, device_id=partner, device_id_type=MESH)
-        pl.semaphore_wait(barrier, len(partners))
+        expected = len(partners)
+        if hosting is not None:
+            @pl.when(jnp.logical_not(hosting.is_host))
+            def _():
+                pl.semaphore_signal(barrier, inc=1, device_id=hosting.host, device_id_type=MESH)
+
+            expected = expected + hosting.guests
+        pl.semaphore_wait(barrier, expected)
+
+
+class Hosting:
+    def __init__(self, grid, owners, hosts, share, kept, left):
+        depth = grid.sizes["z"]
+        z = grid.mine["z"]
+        self.grid, self.depth, self.hosts, self.share, self.kept, self.left = grid, depth, hosts, share, kept, left
+        self.places = owners // depth
+        self.is_host = grid.place * depth + z < hosts
+        here, _, room = level_counts(hosts, share, self.places, depth, z)
+        index = grid.place - here
+        back_here, _, back_room = level_counts(hosts, share, self.places, depth, z - depth // 2)
+        own = index < room
+        spot = jnp.maximum(jnp.where(own, index, back_room - 1 - (index - room)), 0)
+        self.host = (spot // share, jnp.where(own | self.is_host, z, z - depth // 2))
+        count = jnp.int32(0)
+        for piece in range(share):
+            count = count + self.guest_at(piece)[1].astype(jnp.int32)
+        self.guests = jnp.where(self.is_host, count, 0)
+
+    def guest_at(self, piece):
+        there, near, over = guest_of(
+            self.hosts, self.share, self.places, self.depth, self.grid.place, self.grid.mine["z"], piece
+        )
+        device = (jnp.where(near[0], near[1], over[1]), jnp.where(near[0], near[2], over[2]))
+        return device, there & (piece < self.share)
+
+    def guest(self, tile):
+        piece = tile // self.left
+        device, there = self.guest_at(piece)
+        return device, there, self.kept + tile - piece * self.left
 
 
 def split_slots(slots, shards):
@@ -413,9 +458,66 @@
     return slots // part, (part - late, late)
 
 
+def level_counts(hosts, share, places, depth, z):
+    here = (hosts - z + depth - 1) // depth
+    return here, places - here, share * here
+
+
+def guest_of(hosts, share, places, depth, place, z, piece):
+    here, guests, room = level_counts(hosts, share, places, depth, z)
+    index = place * share + piece
+    far = z + depth // 2
+    far_here, far_guests, far_room = level_counts(hosts, share, places, depth, far)
+    back = room - 1 - index
+    near = index < guests
+    over = (far < depth) & (far_room + back < far_guests)
+    return near | over, (near, here + index, z), (over, far_here + far_room + back, far)
+
+
+def guest_places(plan, owners, depth):
+    hosts, share, kept, left = plan
+    places = [0] * owners
+    for host in range(hosts):
+        for piece in range(share):
+            there, near, over = guest_of(hosts, share, owners // depth, depth, host // depth, host % depth, piece)
+            if there:
+                _, place, z = near if near[0] else over
+                places[place * depth + z] = host * kept + piece * left
+    return places
+
+
+def host_plan(slots, owners, depth):
+    hosts = MOD_ROWS // (slots * SUBS)
+    shards = owners // 2
+    room = 32 * 1024 * 1024 // ((HELD + 2 * SLOTS) * shards * SUBS * LANES * 2)
+    share = -(-(owners - hosts) // hosts) if hosts else 0
+    levels = [level_counts(hosts, share, owners // depth, depth, z) for z in range(depth)]
+    for z, (_, guests, room_here) in enumerate(levels):
+        if guests > room_here and (
+            z < depth // 2
+            or guests - room_here > levels[z - depth // 2][2] - levels[z - depth // 2][1]
+        ):
+            hosts = 0
+    for kept in range(1, slots) if hosts else ():
+        left = slots - kept
+        if share * left > kept:
+            continue
+        for step in range(min(12, max(room, 2)), 5, -1):
+            for late in (round(step * 0.34), step // 3, -(-step // 3)):
+                early = step - late
+                if kept % step or left % early:
+                    continue
+                middle = kept // step * early
+                if all((i * left - middle) % late == 0 for i in range(share + 1) if i * left > middle):
+                    return hosts, share, kept, kept // step, (early, late)
+    steps, parts = split_slots(slots, shards)
+    return 0, 0, slots, steps, parts
+
+
 ORDERS = (("u", "v", "z"), ("u", "z", "v"))
 LAG = 2
 SLOTS = 4
+OUTS = 8
 HELD = 4 * LAG + 1
 
 
@@ -588,8 +690,8 @@
     )(own).reshape(data_count * seq_count * slots * SUBS, LANES)
 
 
-def reduce_stream(grid, order, first_row, span, steps, parts_ref, out_ref, refs):
-    (own, rc, r1, r2, r3, outs, own_sem, out_sem, c_send, c_recv, s1, v1, s2, v2, s3, v3,
+def reduce_stream(grid, order, first_row, span, steps, parts_ref, out_ref, refs, hosting, passed):
+    (own, rc, r1, r2, r3, outs, own_sem, out_sem, hand_sem, c_send, c_recv, s1, v1, s2, v2, s3, v3,
      c_credit, k1, k2, k3) = refs
     mine = grid.mine
     side = grid.side
@@ -650,8 +752,38 @@
             device_id_type=MESH,
         )
 
-    def write(q):
-        return pltpu.make_async_copy(outs.at[q % 2], out_ref.at[rows(q)], out_sem.at[q % 2])
+    def keep(q):
+        return pltpu.make_async_copy(outs.at[q % OUTS], out_ref.at[rows(q)], out_sem.at[q % OUTS])
+
+    def hand_over(q):
+        device, there, slot = hosting.guest((first_row + q * span) // SUBS)
+        copy = pltpu.make_async_remote_copy(
+            src_ref=outs.at[q % OUTS],
+            dst_ref=out_ref.at[pl.ds(pl.multiple_of(slot * SUBS, SUBS), span)],
+            send_sem=hand_sem.at[q % OUTS],
+            recv_sem=passed,
+            device_id=device,
+            device_id_type=MESH,
+        )
+        return copy, there
+
+    def write(q, action):
+        if hosting is None:
+            getattr(keep(q), action)()
+            return
+
+        @pl.when(jnp.logical_not(hosting.is_host))
+        def _():
+            getattr(keep(q), action)()
+
+        copy, there = hand_over(q)
+
+        @pl.when(hosting.is_host & there)
+        def _():
+            if action == "start":
+                copy.start()
+            else:
+                copy.wait_send()
 
     def collect(q, stage):
         axis = order[stage]
@@ -665,12 +797,12 @@
         if stage < 2:
             kept[...] = total.astype(jnp.bfloat16)
         else:
-            @pl.when(q >= 2)
+            @pl.when(q >= OUTS)
             def _():
-                write(q - 2).wait()
-
-            outs[q % 2] = total.astype(jnp.bfloat16)
-            write(q).start()
+                write(q - OUTS, "wait")
+
+            outs[q % OUTS] = total.astype(jnp.bfloat16)
+            write(q, "start")
         for k in range(count):
             send(q, stage, k).wait_send()
 
@@ -736,7 +868,7 @@
     return (begin, stage_c, stage_one, stage_two, stage_three), write
 
 
-REDUCE_REFS = 20
+REDUCE_REFS = 21
 
 
 MOD_BLOCKS = 6 * D // LANES
@@ -873,9 +1005,12 @@
     return run
 
 
-def reduce_body(side, depth, steps, parts, parts_ref, part_ref, weight_ref, out_ref, all_ref, cond_ref, *refs):
+def reduce_body(side, depth, plan, slots, parts_ref, part_ref, weight_ref, out_ref, all_ref, cond_ref, *refs):
+    hosts, share, kept, steps, parts = plan
     grid = Grid(side, depth)
-    grid.greet()
+    hosting = Hosting(grid, 2 * side * side * depth, hosts, share, kept, slots - kept) if hosts else None
+    grid.greet(hosting)
+    passed = refs[-1]
     modulation_step = modulation_stages(grid, part_ref, weight_ref, all_ref, cond_ref, refs[:MOD_REFS])
     refs = refs[MOD_REFS:]
     streams = []
@@ -885,7 +1020,7 @@
         span = part * SUBS
         stages, write = reduce_stream(
             grid, order, first, span, steps, parts_ref, out_ref,
-            refs[REDUCE_REFS * number : REDUCE_REFS * (number + 1)],
+            refs[REDUCE_REFS * number : REDUCE_REFS * (number + 1)], hosting, passed,
         )
         streams.append(stages)
         writes.append(write)
@@ -905,13 +1040,22 @@
 
     lax.fori_loop(0, max(steps + 4 * LAG, MOD_STEPS), round_trip, 0)
     for write in writes:
-        for q in range(max(steps - 2, 0), steps):
-            write(q).wait()
+        for q in range(max(steps - OUTS, 0), steps):
+            write(q, "wait")
+    if hosting is not None:
+        @pl.when(jnp.logical_not(hosting.is_host))
+        def _():
+            at = out_ref.at[pl.ds(kept * SUBS, (slots - kept) * SUBS)]
+            pltpu.make_async_remote_copy(
+                src_ref=at, dst_ref=at, send_sem=passed, recv_sem=passed, device_id=grid.sibling,
+                device_id_type=MESH,
+            ).wait_recv()
 
 
 def reduce_slots(grads, mod_part, mod_weight, slots, data_count, seq_count):
     side = math.isqrt(data_count // 2)
-    steps, parts = split_slots(slots, side * side * seq_count)
+    plan = host_plan(slots, data_count * seq_count, seq_count)
+    kept, parts = plan[2], plan[4]
     held = HELD
     dma = pltpu.SemaphoreType.DMA
     regular = pltpu.SemaphoreType.REGULAR
@@ -943,9 +1087,10 @@
             del left[axis]
             rest = tuple(left[name] for name in ("u", "v", "z") if name in left)
             scratch.append(pltpu.VMEM((SLOTS, sizes[axis] - 1) + rest + (span, LANES), bf16))
-        scratch.append(pltpu.VMEM((2, span, LANES), bf16))
+        scratch.append(pltpu.VMEM((OUTS, span, LANES), bf16))
         scratch.append(dma((held, side, side)))
-        scratch.append(dma((2,)))
+        scratch.append(dma((OUTS,)))
+        scratch.append(dma((OUTS,)))
         scratch.append(dma((SLOTS, side, side)))
         scratch.append(dma((SLOTS, side, side)))
         for axis in order:
@@ -954,8 +1099,9 @@
         scratch.append(regular)
         for axis in order:
             scratch.append(regular((sizes[axis],)))
+    scratch.append(dma)
     return pl.pallas_call(
-        partial(reduce_body, side, seq_count, steps, parts),
+        partial(reduce_body, side, seq_count, plan, slots),
         out_shape=(
             jax.ShapeDtypeStruct((slots * SUBS, LANES), bf16),
             jax.ShapeDtypeStruct((data_count, IMAGE_ROWS, LANES), f32),
@@ -976,7 +1122,7 @@
             collective_id=1, has_side_effects=True, vmem_limit_bytes=VMEM_LIMIT
         ),
         name="reduce_slots",
-    )(grads.reshape(data_count, seq_count, slots * SUBS, LANES), mod_part, mod_weight)
+    )(grads.reshape(data_count, seq_count, kept * SUBS, LANES), mod_part, mod_weight)
 
 
 UPDATE_TILES = 72
@@ -1304,6 +1450,10 @@
     spans = jnp.asarray(chunk_spans()[0], jnp.int32)
     firsts = jnp.sum((tile_ends[None, :] <= spans[:, :1]).astype(jnp.int32), axis=1)
     lasts = jnp.sum((tile_ends[None, :] <= spans[:, 1:]).astype(jnp.int32), axis=1)
+    plan = host_plan(slot_count, owners, seq_count)
+    guests = jnp.asarray(
+        guest_places((*plan[:3], slot_count - plan[2]), owners, seq_count), jnp.int32
+    )
     edge_ids = jnp.asarray(EDGE_TILES, jnp.int32)
     edge_owner = jnp.sum((tile_ends[None, :] <= edge_ids[:, None]).astype(jnp.int32), axis=1)
     edge_slots = edge_owner * slot_count + edge_ids - jnp.take(starts, edge_owner)
@@ -1421,6 +1571,8 @@
             firsts,
             lasts,
             starts,
+            guests,
+            (plan[0], plan[2]),
         )
         return buffer
 
@@ -1542,7 +1694,14 @@
         tail(15),
         whole(sum_sixteen),
     ]
-    grad_buffer = edge_write(pieces, grad_buffer, edge_slots[EDGE_TILES.index(3891) :])
+    hosts, _, kept = plan[:3]
+    edge_within = edge_ids - jnp.take(starts, edge_owner)
+    edge_places = edge_owner * kept + edge_within
+    if hosts:
+        edge_places = jnp.where(
+            edge_within < kept, edge_places, jnp.take(guests, edge_owner) + edge_within - kept
+        )
+    grad_buffer = edge_write(pieces, grad_buffer, edge_places[EDGE_TILES.index(3891) :])
     reduced, mod_all, cond_grad = reduce_slots(
         grad_buffer, mod_sent, mod_weight, slot_count, data_count, seq_count
     )

time: 1070 us -> 1040 us (0.972)
  Pallas kernels: 872 us -> 846 us
    pallas_call x1, Pallas kernels: 317 us -> 291 us  [reduce_slots(): pl.pallas_call(partial(reduce_body, side, seq_count, plan, slots), out_sh...]
where the time goes in v4:
time: 1040 us; the launch traced here: 1030 us
  Pallas kernels  846 us (81%)
  matrix products  89.8 us (9%)
  local copies, waits for them, and re-layouts  30.8 us (3%)
  other arithmetic  28.5 us (3%)
  starting transfers between devices  19.8 us (2%)
  blocking collectives  10.6 us (1%)
    pallas_call x1, Pallas kernels, gather_slots(): pl.pallas_call(partial(gather_body, side, seq_count, steps, parts), out_s...  320 us
    pallas_call x1, Pallas kernels, reduce_slots(): pl.pallas_call(partial(reduce_body, side, seq_count, plan, slots), out_sh...  291 us
    pallas_call x8, Pallas kernels, unpack_weight(): pl.pallas_call(partial(unpack_body, base, row // SUBS, per_chunk, tiles,...  86.6 us
    pallas_call x7, Pallas kernels, weight_grad(): pl.pallas_call(partial(weight_grad_body, base, row // SUBS, per_chunk, sh...  66 us
    pallas_call x1, Pallas kernels, attention_grad(): pl.pallas_call(partial(attention_grad_body, heads), out_shape=jax.ShapeDt...  28.7 us
  transfers between devices with their start and end apart: 4, of which 2 were waited for; matrix products, arithmetic and copies ran while one was open for 1% of the time, Pallas kernels for 11%

profile of v4, /device:TPU:1, one launch (start us, length us, event | category | flops | bytes accessed | tf_op | source)
XLA Modules:
  0.0 1033.8 jit_solution(9430511547000668816)
XLA Ops:
  2.5 4.3 convert_element_type.193
  6.8 5.2 reshape.624.own_ref
  11.9 320.1 %gather_slots.1 = bf16[8,4,9792,128]{3,2,1,0:T(8,128)(2,1)} custom-call(bf16[9792,128]{1,0:T(8,128)(2,1)} %reshape.624.own_ref), custom_call_target="tpu_custom_call" | custom-call | tf_op jit(solution)/shard_map/gather_slots/pallas_call | solution.py:680
  334.1 2.2 edge_read.1
  337.0 1.4 fusion.50
  339.1 17.1 %unpack_0.1.weight_ref = bf16[1152,6912]{1,0:T(8,128)(2,1)} custom-call(s32[52]{0:T(128)} %get-tuple-element.90.first_ref, s32[52]{0:T(128)} %get-tuple-element.89.last_ref, s32[33]{0:T(128)} %copy-done, bf16[313344,128]{1,0:T(8,128)(2,1)} %bitcast.3.packed), custom_call_target="tpu_custom_call" | custom-call | bytes 31850496 | tf_op jit(solution)/shard_map/unpack_0/pallas_call | solution.py:137
  356.2 11.7 %unpack_2.1 = bf16[1152,3456]{1,0:T(8,128)(2,1)} custom-call(s32[52]{0:T(128)} %get-tuple-element.90.first_ref, s32[52]{0:T(128)} %get-tuple-element.89.last_ref, s32[33]{0:T(128)} %copy-done, bf16[313344,128]{1,0:T(8,128)(2,1)} %bitcast.3.packed), custom_call_target="tpu_custom_call" | custom-call | bytes 15925248 | tf_op jit(solution)/shard_map/unpack_2/pallas_call | solution.py:137
  368.9 7.7 convolution_add_fusion
  376.6 3.0 convolution_bitcast_fusion
  379.6 2.9 copy-done.3
  382.9 7.2 fusion.1.x_ref
  390.1 3.4 split_groups_3.1
  393.5 7.0 all-to-all-start
  400.5 5.2 unpack_5.1
  405.7 13.2 %unpack_7.1 = bf16[1152,4608]{1,0:T(8,128)(2,1)} custom-call(s32[52]{0:T(128)} %get-tuple-element.90.first_ref, s32[52]{0:T(128)} %get-tuple-element.89.last_ref, s32[33]{0:T(128)} %copy-done, bf16[313344,128]{1,0:T(8,128)(2,1)} %bitcast.3.packed), custom_call_target="tpu_custom_call" | custom-call | bytes 21233664 | tf_op jit(solution)/shard_map/unpack_7/pallas_call | solution.py:137
  418.9 13.3 %unpack_9.1 = bf16[4608,1152]{1,0:T(8,128)(2,1)} custom-call(s32[52]{0:T(128)} %get-tuple-element.90.first_ref, s32[52]{0:T(128)} %get-tuple-element.89.last_ref, s32[33]{0:T(128)} %copy-done, bf16[313344,128]{1,0:T(8,128)(2,1)} %bitcast.3.packed), custom_call_target="tpu_custom_call" | custom-call | bytes 21233664 | tf_op jit(solution)/shard_map/unpack_9/pallas_call | solution.py:137
  432.3 4.4 unpack_15.1
  438.7 4.0 all-to-all-done
  443.9 18.8 %attention.1 = bf16[1024,288]{1,0:T(8,128)(2,1)} custom-call(bf16[1024,896]{1,0:T(8,128)(2,1)} %bitcast.163, s32[1024,1]{1,0:T(8,128)} %copy.45.seg_col, s32[1024,1]{1,0:T(8,128)} %copy.46.pad_col, s32[1,1024]{1,0:T(1,128)} %seg_row.3), custom_call_target="tpu_custom_call" | custom-call | tf_op jit(solution)/shard_map/attention/pallas_call | solution.py:1344
  462.8 2.2 copy.47
  465.0 3.7 all-to-all-start.1
  470.8 8.5 unpack_11.1
  479.4 13.2 %unpack_13.1 = bf16[2048,2048]{1,0:T(8,128)(2,1)} custom-call(s32[52]{0:T(128)} %get-tuple-element.90.first_ref, s32[52]{0:T(128)} %get-tuple-element.89.last_ref, s32[33]{0:T(128)} %copy-done, bf16[313344,128]{1,0:T(8,128)(2,1)} %bitcast.3.packed), custom_call_target="tpu_custom_call" | custom-call | bytes 16777216 | tf_op jit(solution)/shard_map/unpack_13/pallas_call | solution.py:137
  493.8 2.2 join_groups_1.1.x_ref
  496.0 4.3 fusion.80
  500.6 2.1 fusion.36.x_ref
  502.7 11.7 %multiply_convert_fusion = (bf16[256,4608]{1,0:T(8,128)(2,1)}, f32[256,4608]{1,0:T(8,128)}) fusion(f32[4608]{0:T(1024)S(1)} %fusion.46, bf16[256,1152]{1,0:T(8,128)(2,1)S(1)} %fusion.36.x_ref, bf16[1152,4608]{1,0:T(8,128)(2,1)} %unpack_7.1), kind=kOutput, calls=%fused_computation.19 | convolution fusion | flops 2729705472 | bytes 18302976 | tf_op jit(solution)/shard_map/rtd,df->rtf/dot_general | solution.py:1532
  514.5 6.3 add_convert_fusion
  520.8 3.1 multiply_convert_fusion.2
  523.9 2.4 convolution_add_fusion.5
  526.3 1.5 fusion.75
  528.6 1.3 multiply_reduce_fusion.2
  531.0 3.0 convert_reduce_fusion.2
  534.0 5.6 convert_reduce_fusion.3
  539.6 2.4 convert_reduce_fusion.5
  542.1 9.6 convert_reduce_fusion
  551.7 8.3 multiply_reduce_fusion
  560.5 1.9 convert_reduce_fusion.6
  562.7 1.9 convolution_convert_fusion.1.x_ref
  564.6 2.2 split_groups_1.1
  566.8 2.2 copy.49
  569.0 4.7 all-to-all-start.2
  573.8 5.5 weight_grad_15.1
  579.3 8.4 weight_grad_11.1
  587.8 1.4 all-to-all-done.2
  590.3 28.7 %attention_grad.1 = bf16[1024,896]{1,0:T(8,128)(2,1)} custom-call(bf16[1024,896]{1,0:T(8,128)(2,1)} %bitcast.164, bf16[1024,288]{1,0:T(8,128)(2,1)} %bitcast.170, s32[1024,1]{1,0:T(8,128)} %copy.45.seg_col, s32[1024,1]{1,0:T(8,128)} %copy.46.pad_col, s32[1,1024]{1,0:T(1,128)} %seg_row.3), custom_call_target="tpu_custom_call" | custom-call | tf_op jit(solution)/shard_map/attention_grad/pallas_call | solution.py:1406
  619.0 4.4 all-to-all-start.3
  625.9 1.8 pad_add_fusion.1.own_ref
  627.8 10.6 %all_gather.3 = bf16[8,4,1152]{2,1,0:T(4,128)(2,1)S(1)} all-gather(bf16[1,4,1152]{2,1,0:T(4,128)(2,1)S(1)} %fusion.42), channel_id=1, replica_groups=mesh['dp'=8,'seq'=4] {'dp'}, dimensions={0}, use_global_device_ids=true | all-gather | bytes 82944 | tf_op jit(solution)/shard_map/all_gather | solution.py:1637
  639.4 12.2 %weight_grad_13.1 = (bf16[264192,128]{1,0:T(8,128)(2,1)}, f32[32,128]{1,0:T(8,128)}) custom-call(s32[52]{0:T(128)} %get-tuple-element.90.first_ref, s32[52]{0:T(128)} %get-tuple-element.89.last_ref, s32[33]{0:T(128)} %copy-done, s32[32]{0:T(128)} %constant.139.clone.guests_ref, bf16[256,2048]{1,0:T(8,128)(2,1)} %copy-done.25, ...), custom_call_target="tpu_custom_call", output_to_operand_aliasing={{0}: (6, {})} | custom-call | flops 2147483648 | bytes 8388608 | tf_op jit(solution)/shard_map/weight_grad_13/pallas_call | solution.py:336
  651.6 11.9 %weight_grad_9.1 = (bf16[264192,128]{1,0:T(8,128)(2,1)}, f32[32,128]{1,0:T(8,128)}) custom-call(s32[52]{0:T(128)} %get-tuple-element.90.first_ref, s32[52]{0:T(128)} %get-tuple-element.89.last_ref, s32[33]{0:T(128)} %copy-done, s32[32]{0:T(128)} %constant.139.clone.guests_ref, ...), custom_call_target="tpu_custom_call", output_to_operand_aliasing={{0}: (6, {})} | custom-call | flops 2717908992 | bytes 10616832 | tf_op jit(solution)/shard_map/weight_grad_9/pallas_call | solution.py:336
  663.5 11.4 %weight_grad_7.1 = (bf16[264192,128]{1,0:T(8,128)(2,1)}, f32[32,128]{1,0:T(8,128)}) custom-call(s32[52]{0:T(128)} %get-tuple-element.90.first_ref, s32[52]{0:T(128)} %get-tuple-element.89.last_ref, s32[33]{0:T(128)} %copy-done, s32[32]{0:T(128)} %constant.139.clone.guests_ref, bf16[256,1152]{1,0:T(8,128)(2,1)} %copy-done.20, ...), custom_call_target="tpu_custom_call", output_to_operand_aliasing={{0}: (6, {})} | custom-call | flops 2717908992 | bytes 10616832 | tf_op jit(solution)/shard_map/weight_grad_7/pallas_call | solution.py:336
  674.9 5.9 weight_grad_5.1
  680.8 3.4 join_groups_3.1.dy_ref
  684.3 6.8 constant_dynamic-update-slice_fusion.1
  691.4 1.8 fusion.78
  693.3 2.8 copy-done.12
  696.1 10.7 %weight_grad_2.1 = (bf16[264192,128]{1,0:T(8,128)(2,1)}, f32[32,128]{1,0:T(8,128)}) custom-call(s32[52]{0:T(128)} %get-tuple-element.90.first_ref, s32[52]{0:T(128)} %get-tuple-element.89.last_ref, s32[33]{0:T(128)} %copy-done, s32[32]{0:T(128)} %constant.139.clone.guests_ref, bf16[256,1152]{1,0:T(8,128)(2,1)} %copy-done.18, ...), custom_call_target="tpu_custom_call", output_to_operand_aliasing={{0}: (6, {})} | custom-call | flops 2038431744 | bytes 7962624 | tf_op jit(solution)/shard_map/weight_grad_2/pallas_call | solution.py:336
  707.3 1.6 multiply_dynamic-update-slice_fusion.2
  713.3 5.3 convolution_convert_fusion
  719.3 2.4 edge_write.1
  721.7 291.2 %reduce_slots.1 = (bf16[9792,128]{1,0:T(8,128)(2,1)}, f32[8,216,128]{2,1,0:T(8,128)}, f32[8,1152]{1,0:T(8,128)}) custom-call(bf16[8,4,8256,128]{3,2,1,0:T(8,128)(2,1)} %bitcast.53.parts_ref, bf16[224,128]{1,0:T(8,128)(2,1)} %pad.4.part_ref, bf16[1152,6912]{1,0:T(8,128)(2,1)} %unpack_0.1.weight_ref), custom_call_target="tpu_custom_call" | custom-call | tf_op jit(solution)/shard_map/reduce_slots/pallas_call | solution.py:1103
  1012.9 1.4 fusion.44
  1014.3 19.0 %update.1 = (f32[612,2048]{1,0:T(8,128)}, f32[612,2048]{1,0:T(8,128)}, f32[612,2048]{1,0:T(8,128)}) custom-call(s32[2]{0:T(128)} %pad_add_fusion.1.own_ref, bf16[9792,128]{1,0:T(8,128)(2,1)} %get-tuple-element.81.reduced, bf16[200,32]{1,0:T(8,128)(2,1)} %copy.54.cond_ref, f32[1728,128]{1,0:T(8,128)} %bitcast.175, f32[612,2048]{1,0:T(8,128)} %master.1, ...), custom_call_target="tpu_custom_call" | custom-call | tf_op jit(solution)/shard_map/update/pallas_call | solution.py:1197
  (181 shorter events, 26.1 us)
Async XLA Ops:
  2.5 330.3 %copy-start = (s32[33]{0:T(128)}, s32[33]{0:T(128)S(1)}, u32[]{:S(2)}) copy-start(s32[33]{0:T(128)S(1)} %pad_add_fusion.starts_ref) | copy-start | bytes 400
  11.9 320.1 %copy-start.2 = (s32[32]{0:T(128)S(1)}, s32[32]{0:T(128)}, u32[]{:S(2)}) copy-start(s32[32]{0:T(128)} %constant.139.clone.guests_ref) | copy-start | bytes 388
  11.9 321.5 %copy-start.49 = (s32[18]{0:T(128)S(1)}, s32[18]{0:T(128)}, u32[]{:S(2)}) copy-start(s32[18]{0:T(128)} %constant.140.clone) | copy-start | bytes 220
  334.0 4.3 copy-start.46
  334.0 4.3 copy-start.47
  356.1 11.7 %copy-start.6 = (bf16[1,256,1152]{2,1,0:T(8,128)(2,1)S(1)}, bf16[1,256,1152]{2,1,0:T(8,128)(2,1)}, u32[]{:S(2)}) copy-start(bf16[1,256,1152]{2,1,0:T(8,128)(2,1)} %param.15) | copy-start | bytes 1769476
  356.1 12.8 %copy-start.32 = (s32[1,1024]{1,0:T(1,128)S(1)}, s32[1,1024]{1,0:T(1,128)}, u32[]{:S(2)}) copy-start(s32[1,1024]{1,0:T(1,128)} %seg_row.3) | copy-start | bytes 12292
  356.1 12.8 %copy-start.28 = (bf16[1,4,1152]{2,1,0:T(4,128)(2,1)S(1)}, bf16[1,4,1152]{2,1,0:T(4,128)(2,1)}, u32[]{:S(2)}) copy-start(bf16[1,4,1152]{2,1,0:T(4,128)(2,1)} %param.16) | copy-start | bytes 27652
  368.0 11.6 %copy-start.35 = (f32[256]{0:T(256)}, f32[256]{0:T(256)S(1)}, u32[]{:S(2)}) copy-start(f32[256]{0:T(256)S(1)} %broadcast_multiply_fusion.2) | copy-start | bytes 3076
  368.3 0.6 copy-start.41
  368.3 11.3 %copy-start.39 = (f32[256]{0:T(256)}, f32[256]{0:T(256)S(1)}, u32[]{:S(2)}) copy-start(f32[256]{0:T(256)S(1)} %fusion.60) | copy-start | bytes 3076
  368.9 7.7 copy-start.33
  379.6 2.9 copy-start.3
  382.9 7.2 copy-start.18
  393.5 49.2 %all-to-all-start = ((bf16[4,256,896]{2,1,0:T(8,128)(2,1)}), bf16[4,256,896]{2,1,0:T(8,128)(2,1)S(1)}, u32[]{:S(2)}, u32[]{:S(2)}) async-start(bf16[4,256,896]{2,1,0:T(8,128)(2,1)} %split_groups_3.1), calls=%async_computation | async-start | bytes 3670016 | tf_op jit(solution)/shard_map/all_to_all | solution.py:1512
  432.2 5.4 copy-start.44
  442.7 1.2 copy-start.4
  465.0 27.6 %all-to-all-start.1 = ((bf16[4,256,288]{1,2,0:T(8,128)(2,1)}), bf16[4,256,288]{1,2,0:T(8,128)(2,1)S(1)}, u32[]{:S(2)}, u32[]{:S(2)}) async-start(bf16[4,256,288]{1,2,0:T(8,128)(2,1)} %copy.47), calls=%async_computation.1 | async-start | bytes 1179648 | tf_op jit(solution)/shard_map/all_to_all | solution.py:1521
  492.6 3.4 copy-start.7
  492.6 3.4 copy-start.31
  500.3 14.1 %slice-start = ((s8[7077888]{0:T(1024)(128)(4,1)}), s8[4194304]{0:T(1024)(128)(4,1)S(1)}, s32[]{:S(2)}) async-start(s8[7077888]{0:T(1024)(128)(4,1)} %bitcast.159), calls=%async_computation.4 | async-start | bytes 8388608
  500.5 59.4 %copy-start.37 = (f32[256]{0:T(256)}, f32[256]{0:T(256)S(1)}, u32[]{:S(2)}) copy-start(f32[256]{0:T(256)S(1)} %fusion.61) | copy-start | bytes 3076
  500.5 13.9 %slice-start.4 = ((s8[10616832]{0:T(1024)(128)(4,1)}), s8[4194304]{0:T(1024)(128)(4,1)S(1)}, s32[]{:S(2)}) async-start(s8[10616832]{0:T(1024)(128)(4,1)} %bitcast.165), calls=%async_computation.8 | async-start | bytes 8388608
  500.6 20.2 %slice-start.2 = ((s8[4718592]{0:T(1024)(128)(4,1)}), s8[4194304]{0:T(1024)(128)(4,1)S(1)}, s32[]{:S(2)}) async-start(s8[4718592]{0:T(1024)(128)(4,1)} %bitcast.161), calls=%async_computation.6 | async-start | bytes 8388608
  502.7 11.7 %copy-start.20 = (bf16[256,1152]{1,0:T(8,128)(2,1)}, bf16[256,1152]{1,0:T(8,128)(2,1)S(1)}, u32[]{:S(2)}) copy-start(bf16[256,1152]{1,0:T(8,128)(2,1)S(1)} %fusion.36.x_ref) | copy-start | bytes 1769476
  502.7 11.8 %slice-start.1 = ((s8[7077888]{0:T(1024)(128)(4,1)}), s8[2883584]{0:T(1024)(128)(4,1)S(1)}, s32[]{:S(2)}) async-start(s8[7077888]{0:T(1024)(128)(4,1)} %bitcast.159), calls=%async_computation.5 | async-start | bytes 5767168
  502.7 11.8 %slice-start.5 = ((s8[10616832]{0:T(1024)(128)(4,1)}), s8[4194304]{0:T(1024)(128)(4,1)S(1)}, s32[]{:S(2)}) async-start(s8[10616832]{0:T(1024)(128)(4,1)} %bitcast.165), calls=%async_computation.9 | async-start | bytes 8388608
  502.7 11.8 %slice-start.6 = ((s8[10616832]{0:T(1024)(128)(4,1)}), s8[2228224]{0:T(1024)(128)(4,1)S(1)}, s32[]{:S(2)}) async-start(s8[10616832]{0:T(1024)(128)(4,1)} %bitcast.165), calls=%async_computation.10 | async-start | bytes 4456448
  502.7 11.8 %copy-start.43 = (f32[1152]{0:T(1024)S(1)}, f32[1152]{0:T(1024)}, u32[]{:S(2)}) copy-start(f32[1152]{0:T(1024)} %get-tuple-element.113) | copy-start | bytes 13828
  502.7 18.1 %slice-start.3 = ((s8[4718592]{0:T(1024)(128)(4,1)}), s8[524288]{0:T(1024)(128)(4,1)S(1)}, s32[]{:S(2)}) async-start(s8[4718592]{0:T(1024)(128)(4,1)} %bitcast.161), calls=%async_computation.7 | async-start | bytes 1048576
  502.7 21.2 %slice-start.7 = ((s8[8388608]{0:T(1024)(128)(4,1)}), s8[4194304]{0:T(1024)(128)(4,1)S(1)}, s32[]{:S(2)}) async-start(s8[8388608]{0:T(1024)(128)(4,1)} %bitcast.167), calls=%async_computation.11 | async-start | bytes 8388608
  514.5 9.4 slice-start.8
  520.8 3.1 copy-start.26
  523.9 2.4 copy-start.25
  526.3 2.3 copy-start.16
  528.6 1.3 copy-start.22
  531.0 3.0 copy-start.27
  534.0 5.6 copy-start.24
  539.6 2.5 copy-start.15
  542.1 9.6 copy-start.21
  542.1 18.4 %copy-start.10 = (f32[1,256,1152]{2,1,0:T(8,128)}, f32[1,256,1152]{2,1,0:T(8,128)S(1)}, u32[]{:S(2)}) copy-start(f32[1,256,1152]{2,1,0:T(8,128)S(1)} %get-tuple-element.132) | copy-start | bytes 3538948
  551.6 8.3 copy-start.19
  560.5 2.2 copy-start.9
  562.4 2.2 copy-start.17
  564.6 9.2 copy-start.29
  569.0 20.1 %all-to-all-start.2 = ((bf16[4,256,288]{1,2,0:T(8,128)(2,1)}), bf16[4,256,288]{1,2,0:T(8,128)(2,1)S(1)}, u32[]{:S(2)}, u32[]{:S(2)}) async-start(bf16[4,256,288]{1,2,0:T(8,128)(2,1)} %copy.49), calls=%async_computation.2 | async-start | bytes 1179648 | tf_op jit(solution)/shard_map/all_to_all | solution.py:1622
  619.0 4.4 copy-start.1
  619.0 5.8 copy-start.48
  619.0 6.4 copy-start.45
  619.0 61.8 %all-to-all-start.3 = ((bf16[4,256,896]{2,1,0:T(8,128)(2,1)}), bf16[4,256,896]{2,1,0:T(8,128)(2,1)}, u32[]{:S(2)}, u32[]{:S(2)}) async-start(bf16[4,256,896]{2,1,0:T(8,128)(2,1)} %bitcast.169), calls=%async_computation.3 | async-start | bytes 3670016 | tf_op jit(solution)/shard_map/all_to_all | solution.py:1632
  680.8 3.5 copy-start.8
  680.8 3.5 copy-start.36
  684.3 6.8 copy-start.5
  684.3 7.1 copy-start.42
  684.3 7.2 copy-start.40
  693.2 2.8 copy-start.12
  696.1 11.3 %copy-start.13 = (f32[1,256,1152]{2,1,0:T(8,128)S(1)}, f32[1,256,1152]{2,1,0:T(8,128)}, u32[]{:S(2)}) copy-start(f32[1,256,1152]{2,1,0:T(8,128)} %get-tuple-element.99) | copy-start | bytes 3538948
  696.1 11.3 %copy-start.14 = (f32[1,256,1152]{2,1,0:T(8,128)S(1)}, f32[1,256,1152]{2,1,0:T(8,128)}, u32[]{:S(2)}) copy-start(f32[1,256,1152]{2,1,0:T(8,128)} %get-tuple-element.123) | copy-start | bytes 3538948
  709.0 1.1 copy-start.38
  710.1 1.5 copy-start.11
  710.1 2.0 copy-start.23
  711.4 1.9 copy-start.34
  721.7 291.2 %copy-start.30 = (bf16[1,4,1152]{2,1,0:T(4,128)(2,1)S(1)}, bf16[1,4,1152]{2,1,0:T(4,128)(2,1)}, u32[]{:S(2)}) copy-start(bf16[1,4,1152]{2,1,0:T(4,128)(2,1)} %param.16) | copy-start | bytes 27652

commit v5 on v4

--- a/solution.py
+++ b/solution.py
@@ -68,8 +68,8 @@
     return starts
 
 
-CHUNK = {0: 128, 2: 128, 5: 384, 7: 128, 9: 512, 11: 384, 13: 256, 15: 1024}
-EDGE_TILES = [3888, 3889, 3890, 3891, 5835, 5836, 6484, 6485, 9077, 9078, 9079, 11671, 12823, 12824, 14872, 14873, 15641, 15642]
+CHUNK = {2: 128, 5: 384, 7: 128, 9: 512, 11: 384, 13: 256, 15: 1024}
+EDGE_TILES = [3891, 5835, 5836, 6484, 6485, 9077, 9078, 9079, 11671, 12823, 12824, 14872, 14873, 15641, 15642]
 
 
 def chunk_spans():
@@ -87,22 +87,32 @@
     return spans, base
 
 
-def unpack_body(base, first_tile, per_chunk, tiles, shift, chunk, col_blocks, slots,
-                first_ref, last_ref, starts_ref, packed, out_ref, landed, wide, sems):
+def unpack_body(base, first_tile, per_chunk, tiles, shift, chunk, col_blocks, hosts, kept,
+                first_ref, last_ref, starts_ref, guests_ref, packed, out_ref, landed, wide, sems):
     step = pl.program_id(0)
 
     def fetch(which, slot):
         low_tile = first_tile + which * per_chunk
+
+        def run(begin, end, place):
+            size = pl.multiple_of(jnp.maximum(end - begin, 0) * SUBS, SUBS)
+            origin = pl.multiple_of(place * SUBS, SUBS)
+            target = pl.multiple_of((begin - low_tile) * SUBS, SUBS)
+
+            @pl.when(end > begin)
+            def _():
+                pltpu.make_async_copy(
+                    packed.at[pl.ds(origin, size)], landed.at[slot, pl.ds(target, size)], sems.at[slot]
+                ).start()
 
         def one(owner, carry):
             begin = jnp.maximum(starts_ref[owner], low_tile)
             end = jnp.minimum(starts_ref[owner + 1], low_tile + tiles)
-            size = pl.multiple_of((end - begin) * SUBS, SUBS)
-            origin = pl.multiple_of((owner * slots + begin - starts_ref[owner]) * SUBS, SUBS)
-            target = pl.multiple_of((begin - low_tile) * SUBS, SUBS)
-            pltpu.make_async_copy(
-                packed.at[pl.ds(origin, size)], landed.at[slot, pl.ds(target, size)], sems.at[slot]
-            ).start()
+            turn = starts_ref[owner] + kept
+            run(begin, jnp.minimum(end, turn), owner * kept + begin - starts_ref[owner])
+            if hosts:
+                begin = jnp.maximum(begin, turn)
+                run(begin, end, guests_ref[owner] + begin - turn)
             return carry
 
         lax.fori_loop(first_ref[base + which], last_ref[base + which] + 1, one, 0)
@@ -125,7 +135,7 @@
         ].astype(jnp.bfloat16)
 
 
-def unpack_weight(index, packed, slots, firsts, lasts, starts):
+def unpack_weight(index, packed, plan, firsts, lasts, starts, guests):
     depth, width = param_shapes()[index]
     chunk = CHUNK[index]
     col_blocks = width // LANES
@@ -135,10 +145,10 @@
     tiles = per_chunk + (1 if shift else 0)
     base = chunk_spans()[1][index]
     return pl.pallas_call(
-        partial(unpack_body, base, row // SUBS, per_chunk, tiles, shift, chunk, col_blocks, slots),
+        partial(unpack_body, base, row // SUBS, per_chunk, tiles, shift, chunk, col_blocks, plan[0], plan[2]),
         out_shape=jax.ShapeDtypeStruct((depth, width), jnp.bfloat16),
         grid_spec=pltpu.PrefetchScalarGridSpec(
-            num_scalar_prefetch=3,
+            num_scalar_prefetch=4,
             grid=(depth // chunk,),
             in_specs=[pl.BlockSpec(memory_space=pl.ANY)],
             out_specs=pl.BlockSpec((chunk, width), lambda i, *_: (i, 0)),
@@ -151,7 +161,7 @@
         compiler_params=pltpu.CompilerParams(vmem_limit_bytes=VMEM_LIMIT),
         cost_estimate=pl.CostEstimate(flops=0, bytes_accessed=depth * width * 4, transcendentals=0),
         name="unpack_%d" % index,
-    )(firsts, lasts, starts, packed)
+    )(firsts, lasts, starts, guests, packed)
 
 
 def edge_read_body(table_ref, packed, out_ref, sem):
@@ -405,13 +415,22 @@
                 found.append(self.device(axis, self.other(axis, k)))
         return found
 
-    def greet(self, hosting=None):
+    def greet(self, hosting=None, to_host=False):
         barrier = pltpu.get_barrier_semaphore()
         partners = self.partners()
         for partner in partners:
             pl.semaphore_signal(barrier, inc=1, device_id=partner, device_id_type=MESH)
         expected = len(partners)
-        if hosting is not None:
+        if hosting is not None and to_host:
+            for piece in range(hosting.share):
+                device, there = hosting.guest_at(piece)
+
+                @pl.when(hosting.is_host & there)
+                def _(device=device):
+                    pl.semaphore_signal(barrier, inc=1, device_id=device, device_id_type=MESH)
+
+            expected = expected + 1 - hosting.is_host.astype(jnp.int32)
+        elif hosting is not None:
             @pl.when(jnp.logical_not(hosting.is_host))
             def _():
                 pl.semaphore_signal(barrier, inc=1, device_id=hosting.host, device_id_type=MESH)
@@ -432,6 +451,7 @@
         back_here, _, back_room = level_counts(hosts, share, self.places, depth, z - depth // 2)
         own = index < room
         spot = jnp.maximum(jnp.where(own, index, back_room - 1 - (index - room)), 0)
+        self.piece = lax.rem(spot, share)
         self.host = (spot // share, jnp.where(own | self.is_host, z, z - depth // 2))
         count = jnp.int32(0)
         for piece in range(share):
@@ -518,11 +538,12 @@
 LAG = 2
 SLOTS = 4
 OUTS = 8
+LEAD = 4
 HELD = 4 * LAG + 1
 
 
-def gather_stream(grid, order, first_row, span, steps, own_ref, out_ref, sems):
-    (send_a, recv_a, send_b, recv_b, send_c, recv_c, send_d, recv_d) = sems
+def gather_stream(grid, order, first_row, span, steps, own_ref, out_ref, sems, hosting):
+    (send_a, recv_a, send_b, recv_b, send_c, recv_c, send_d, recv_d, kept_sem, arrive) = sems
     mine = grid.mine
     side = grid.side
     near, mid, far = order[2], order[1], order[0]
@@ -613,7 +634,12 @@
             for one in many_c(q, k):
                 one.start()
 
+    def keep(q):
+        dp = grid.dp_of(mine["u"], mine["v"], grid.core)
+        return pltpu.make_async_copy(own_ref.at[rows(q)], out_ref.at[dp, mine["z"], rows(q)], kept_sem.at[q % 4])
+
     def stage_b(q):
+        keep(q).wait()
         for k in range(far_count):
             wait_a(q, near, k)
         for k in range(far_count):
@@ -623,6 +649,14 @@
                 one.start()
 
     def stage_a(q):
+        if hosting is not None:
+            _, there, _ = hosting.guest((first_row + q * span) // SUBS)
+
+            @pl.when(hosting.is_host & there)
+            def _():
+                copy(own_ref.at[rows(q)], own_ref.at[rows(q)], arrive.at[q], arrive.at[q], grid.sibling).wait_recv()
+
+        keep(q).start()
         for k in range(far_count):
             one_a(q, near, k).start()
 
@@ -634,22 +668,60 @@
     return (stage_a, stage_b, stage_c, stage_d, finish)
 
 
-def gather_body(side, depth, steps, parts, own_ref, out_ref, own_sem, *sems):
+GATHER_REFS = 10
+
+
+def gather_body(side, depth, plan, slots, images, own_ref, cond_ref, info_ref, out_ref, mod_ref, held_ref,
+                mine_ref, own_sem, guest_sem, *refs):
+    hosts, share, kept, steps, parts = plan
     grid = Grid(side, depth)
-    keep = pltpu.make_async_copy(
-        own_ref, out_ref.at[grid.dp_of(grid.mine["u"], grid.mine["v"], grid.core), grid.mine["z"]], own_sem
-    )
-    keep.start()
-    grid.greet()
+    hosting = Hosting(grid, 2 * side * side * depth, hosts, share, kept, slots - kept) if hosts else None
+    fill = pltpu.make_async_copy(own_ref.at[pl.ds(0, kept * SUBS)], mine_ref, own_sem)
+
+    def when_guest(action):
+        if hosting is None:
+            action()
+        else:
+            pl.when(jnp.logical_not(hosting.is_host))(action)
+
+    when_guest(fill.start)
+    grid.greet(hosting, to_host=True)
     streams = []
+    arrivals = []
     first = 0
     for number, (order, part) in enumerate(zip(ORDERS, parts)):
         span = part * SUBS
-        streams.append(
-            gather_stream(grid, order, first, span, steps, own_ref, out_ref, sems[8 * number : 8 * number + 8])
-        )
+        sems = refs[GATHER_REFS * number : GATHER_REFS * (number + 1)]
+        streams.append(gather_stream(grid, order, first, span, steps, mine_ref, out_ref, sems, hosting))
+        arrivals.append((first // SUBS, part, sems[-1]))
         first = first + steps * span
-    keep.wait()
+    if hosting is not None:
+        left = slots - kept
+
+        def send_chunks(q, carry):
+            for low, part, arrive in arrivals:
+                tile = low + q * part
+                within = tile - hosting.piece * left
+
+                @pl.when(jnp.logical_not(hosting.is_host) & (within >= 0) & (within < left))
+                def _(tile=tile, within=within, part=part, arrive=arrive):
+                    slot = jnp.clip(kept + within, kept, slots - part)
+                    pltpu.make_async_remote_copy(
+                        src_ref=own_ref.at[pl.ds(pl.multiple_of(slot * SUBS, SUBS), part * SUBS)],
+                        dst_ref=mine_ref.at[pl.ds(pl.multiple_of(tile * SUBS, SUBS), part * SUBS)],
+                        send_sem=guest_sem,
+                        recv_sem=arrive.at[q],
+                        device_id=hosting.host,
+                        device_id_type=MESH,
+                    ).start()
+
+            return carry
+
+        lax.fori_loop(0, min(LEAD, steps), send_chunks, 0)
+    when_guest(fill.wait)
+    modulation_step = modulation_stages(
+        grid, images, slots, own_ref, info_ref, cond_ref, mod_ref, held_ref, refs[2 * GATHER_REFS :]
+    )
 
     def round_trip(s, carry):
         for late in range(4, -1, -1):
@@ -660,14 +732,30 @@
                 for stream in streams:
                     stream[late](q)
 
+        if hosting is not None:
+            @pl.when(s + LEAD < steps)
+            def _():
+                send_chunks(s + LEAD, 0)
+
+        modulation_step(s)
         return carry
 
-    lax.fori_loop(0, steps + 4 * LAG, round_trip, 0)
-
-
-def gather_slots(own, slots, data_count, seq_count):
+    lax.fori_loop(0, max(steps + 4 * LAG, MOD_STEPS), round_trip, 0)
+    if hosting is not None:
+        @pl.when(jnp.logical_not(hosting.is_host))
+        def _():
+            at = own_ref.at[pl.ds(kept * SUBS, (slots - kept) * SUBS)]
+            pltpu.make_async_remote_copy(
+                src_ref=at, dst_ref=at, send_sem=guest_sem, recv_sem=guest_sem, device_id=grid.sibling,
+                device_id_type=MESH,
+            ).wait_send()
+
+
+def gather_slots(own, cond_rows, info, slots, data_count, seq_count):
     side = math.isqrt(data_count // 2)
-    steps, parts = split_slots(slots, side * side * seq_count)
+    images = data_count * SEGS
+    plan = host_plan(slots, data_count * seq_count, seq_count)
+    kept, steps = plan[2], plan[3]
     dma = pltpu.SemaphoreType.DMA
     sems = []
     for order in ORDERS:
@@ -677,17 +765,27 @@
             sems.append(dma((steps, sizes[axis])))
         sems.append(dma((4,)))
         sems.append(dma((steps,)))
-    return pl.pallas_call(
-        partial(gather_body, side, seq_count, steps, parts),
-        out_shape=jax.ShapeDtypeStruct((data_count, seq_count, slots * SUBS, LANES), jnp.bfloat16),
-        in_specs=[pl.BlockSpec(memory_space=pltpu.VMEM)],
-        out_specs=pl.BlockSpec(memory_space=pl.ANY),
-        scratch_shapes=[dma] + sems,
+        sems.append(dma((4,)))
+        sems.append(dma((steps,)))
+    vmem = pl.BlockSpec(memory_space=pltpu.VMEM)
+    packed, modulation, held = pl.pallas_call(
+        partial(gather_body, side, seq_count, plan, slots, images),
+        out_shape=(
+            jax.ShapeDtypeStruct((data_count, seq_count, kept * SUBS, LANES), jnp.bfloat16),
+            jax.ShapeDtypeStruct((IMAGE_ROWS, LANES), jnp.float32),
+            jax.ShapeDtypeStruct((condition_rows(slots), LANES), jnp.float32),
+        ),
+        in_specs=[vmem, vmem, pl.BlockSpec(memory_space=pltpu.SMEM)],
+        out_specs=(pl.BlockSpec(memory_space=pl.ANY), vmem, vmem),
+        scratch_shapes=[pltpu.VMEM((kept * SUBS, LANES), jnp.bfloat16), dma, dma]
+        + sems
+        + modulation_refs(side, seq_count, images, slots),
         compiler_params=pltpu.CompilerParams(
             collective_id=2, has_side_effects=True, vmem_limit_bytes=VMEM_LIMIT
         ),
         name="gather_slots",
-    )(own).reshape(data_count * seq_count * slots * SUBS, LANES)
+    )(own, cond_rows, info)
+    return packed.reshape(data_count * seq_count * kept * SUBS, LANES), modulation, held
 
 
 def reduce_stream(grid, order, first_row, span, steps, parts_ref, out_ref, refs, hosting, passed):
@@ -874,145 +972,472 @@
 MOD_BLOCKS = 6 * D // LANES
 IMAGE_ROWS = SEGS * MOD_BLOCKS
 SENT_ROWS = -(-IMAGE_ROWS // SUBS) * SUBS
-COND_CHUNK = 128
-MOD_REFS = 14
-MOD_STEPS = 11 + D // COND_CHUNK
-
-
-def modulation_stages(grid, part_ref, weight_ref, all_ref, cond_ref, refs):
-    (arrived, dense, held, send_z, recv_z, send_v, recv_v, send_u, recv_u, send_c, recv_c, loads,
-     done_sem, summed) = refs
+COND_STRIDE = D // LANES + 1
+COND_ROWS = SEGS * COND_STRIDE
+FRONT = 56
+MOD_STEPS = 31
+FILL_STEPS = 8
+PRODUCT_STEPS = 9
+
+
+def held_depth(slots):
+    depth = -(-(slots * SUBS + MOD_BLOCKS - 1) // MOD_BLOCKS)
+    return -(-depth // 8) * 8
+
+
+def condition_rows(slots):
+    return -(-(D + 8 + max(held_depth(slots) + 32, 2 * LANES)) // LANES) * LANES
+
+
+def spread_modulation(s, own_ref, info_ref, wide):
+    rows = own_ref.shape[0]
+    count = -(-rows // FILL_STEPS // SUBS) * SUBS
+
+    @pl.when(s == 0)
+    def _():
+        wide[0:FRONT, :] = jnp.zeros((FRONT, LANES), jnp.float32)
+        rest = wide.shape[0] - FRONT - rows
+        wide[FRONT + rows :, :] = jnp.zeros((rest, LANES), jnp.float32)
+
+    @pl.when(s < FILL_STEPS)
+    def _():
+        first = pl.multiple_of(jnp.minimum(s * count, rows - count), SUBS)
+        at = first + lax.broadcasted_iota(jnp.int32, (count, LANES), 0)
+        values = own_ref[pl.ds(first, count), :].astype(jnp.float32)
+        wide[pl.ds(pl.multiple_of(FRONT + first, 8), count), :] = jnp.where(at < info_ref[2], values, 0.0)
+
+
+def wide_rows(slots):
+    return FRONT + MOD_BLOCKS * (held_depth(slots) + 1) + 8
+
+
+def held_columns(wide, info_ref, depth, block):
+    return wide[pl.ds(FRONT + block - info_ref[1], depth, stride=MOD_BLOCKS), :].astype(jnp.bfloat16)
+
+
+def gather_blocks(grid, buffer, rows, sems):
+    send_v, recv_v, send_u, recv_u, send_c, recv_c = sems
+    mine = grid.mine
+    side = grid.side
+
+    def one(u, v, send, recv, device):
+        at = buffer.at[pl.ds(pl.multiple_of(grid.dp_of(u, v, grid.core) * rows, 8), rows)]
+        return pltpu.make_async_remote_copy(
+            src_ref=at, dst_ref=at, send_sem=send, recv_sem=recv, device_id=device, device_id_type=MESH
+        )
+
+    def along(axis, k):
+        return grid.device(axis, grid.other(axis, k)), grid.seat(axis, grid.other(axis, k))
+
+    def v_copies():
+        found = []
+        for k in range(side - 1):
+            device, seat = along("v", k)
+            found.append(one(mine["u"], mine["v"], send_v.at[k], recv_v.at[seat], device))
+        return found
+
+    def u_copies():
+        found = []
+        for k in range(side - 1):
+            device, seat = along("u", k)
+            for v in range(side):
+                found.append(one(mine["u"], v, send_u.at[k, v], recv_u.at[seat, v], device))
+        return found
+
+    def c_copies():
+        return [
+            one(u, v, send_c.at[u, v], recv_c.at[u, v], grid.sibling) for u in range(side) for v in range(side)
+        ]
+
+    def start():
+        for copy in v_copies():
+            copy.start()
+
+    def second():
+        for k in range(side - 1):
+            one(mine["u"], mine["v"], send_v.at[k], recv_v.at[k], grid.sibling).wait_recv()
+        for copy in v_copies():
+            copy.wait_send()
+        for copy in u_copies():
+            copy.start()
+
+    def third():
+        for k in range(side - 1):
+            for v in range(side):
+                one(mine["u"], v, send_u.at[k, v], recv_u.at[k, v], grid.sibling).wait_recv()
+        for copy in u_copies():
+            copy.wait_send()
+        for copy in c_copies():
+            copy.start()
+
+    def finish():
+        for copy in c_copies():
+            copy.wait_recv()
+        for copy in c_copies():
+            copy.wait_send()
+
+    return start, second, third, finish
+
+
+def gather_sems(side):
+    dma = pltpu.SemaphoreType.DMA
+    return [dma((side - 1,))] * 2 + [dma((side - 1, side))] * 2 + [dma((side, side))] * 2
+
+
+def reduce_blocks(grid, buffer, rows, refs):
+    from_c, from_u, from_v, from_z, send_c, recv_c, send_u, recv_u, send_v, recv_v, send_z, recv_z = refs
     mine = grid.mine
     side = grid.side
     depth = grid.sizes["z"]
-    here = grid.dp_of(mine["u"], mine["v"], grid.core)
-    chunks = D // COND_CHUNK
-
-    def to_z(k, seat):
+
+    def block(u, v, core):
+        return buffer.at[pl.ds(pl.multiple_of(grid.dp_of(u, v, core) * rows, 8), rows)]
+
+    def copy(source, target, send, recv, device):
         return pltpu.make_async_remote_copy(
-            src_ref=part_ref, dst_ref=arrived.at[seat], send_sem=send_z.at[k], recv_sem=recv_z.at[seat],
-            device_id=grid.device("z", grid.other("z", k)), device_id_type=MESH,
+            src_ref=source, dst_ref=target, send_sem=send, recv_sem=recv, device_id=device, device_id_type=MESH
         )
 
-    def rows_of(dp):
-        return summed.at[dp]
-
-    def one(dp, send, recv, device):
-        return pltpu.make_async_remote_copy(
-            src_ref=rows_of(dp), dst_ref=rows_of(dp), send_sem=send, recv_sem=recv, device_id=device,
-            device_id_type=MESH,
-        )
-
-    def load(i):
-        return pltpu.make_async_copy(
-            weight_ref.at[pl.ds(pl.multiple_of(i * COND_CHUNK, COND_CHUNK), COND_CHUNK)],
-            held.at[i % 2], loads.at[i % 2],
-        )
-
-    def v_copies():
-        return [
-            one(here, send_v.at[k], recv_v.at[grid.seat("v", grid.other("v", k))], grid.device("v", grid.other("v", k)))
-            for k in range(side - 1)
-        ]
-
-    def u_copies():
-        return [
-            one(grid.dp_of(mine["u"], v, grid.core), send_u.at[k, v],
-                recv_u.at[grid.seat("u", grid.other("u", k)), v], grid.device("u", grid.other("u", k)))
-            for k in range(side - 1)
-            for v in range(side)
-        ]
+    def along(axis, k):
+        other = grid.other(axis, k)
+        return other, grid.device(axis, other), grid.seat(axis, other)
 
     def c_copies():
         return [
-            one(grid.dp_of(u, v, grid.core), send_c.at[u, v], recv_c.at[u, v], grid.sibling)
+            copy(block(u, v, 1 - grid.core), from_c.at[u, v], send_c.at[u, v], recv_c.at[u, v], grid.sibling)
             for u in range(side)
             for v in range(side)
         ]
 
+    def u_copies():
+        found = []
+        for k in range(side - 1):
+            other, device, seat = along("u", k)
+            for v in range(side):
+                found.append(
+                    copy(block(other, v, grid.core), from_u.at[seat, v], send_u.at[k, v], recv_u.at[seat, v], device)
+                )
+        return found
+
+    def v_copies():
+        found = []
+        for k in range(side - 1):
+            other, device, seat = along("v", k)
+            found.append(
+                copy(block(mine["u"], other, grid.core), from_v.at[seat], send_v.at[k], recv_v.at[seat], device)
+            )
+        return found
+
+    def z_copies():
+        found = []
+        for k in range(depth - 1):
+            _, device, _ = along("z", k)
+            found.append(
+                copy(block(mine["u"], mine["v"], grid.core), from_z.at[mine["z"]], send_z.at[k],
+                     recv_z.at[mine["z"]], device)
+            )
+        return found
+
+    def start():
+        for one in c_copies():
+            one.start()
+
+    def second():
+        for one in c_copies():
+            one.wait_recv()
+        for one in c_copies():
+            one.wait_send()
+        for u in range(side):
+            for v in range(side):
+                at = block(u, v, grid.core)
+                at[...] = at[...] + from_c[u, v]
+        for one in u_copies():
+            one.start()
+
+    def third():
+        for k in range(side - 1):
+            for v in range(side):
+                copy(from_u.at[k, v], from_u.at[k, v], send_u.at[k, v], recv_u.at[k, v], grid.sibling).wait_recv()
+        for one in u_copies():
+            one.wait_send()
+        for v in range(side):
+            at = block(mine["u"], v, grid.core)
+            total = at[...]
+            for k in range(side - 1):
+                total = total + from_u[k, v]
+            at[...] = total
+        for one in v_copies():
+            one.start()
+
+    def fourth():
+        for k in range(side - 1):
+            copy(from_v.at[k], from_v.at[k], send_v.at[k], recv_v.at[k], grid.sibling).wait_recv()
+        for one in v_copies():
+            one.wait_send()
+        at = block(mine["u"], mine["v"], grid.core)
+        total = at[...]
+        for k in range(side - 1):
+            total = total + from_v[k]
+        at[...] = total
+        from_z[mine["z"]] = total
+        for one in z_copies():
+            one.start()
+
+    def finish():
+        for k in range(depth - 1):
+            other = grid.other("z", k)
+            copy(from_z.at[other], from_z.at[other], send_z.at[k], recv_z.at[other], grid.sibling).wait_recv()
+        for one in z_copies():
+            one.wait_send()
+        total = from_z[0]
+        for z in range(1, depth):
+            total = total + from_z[z]
+        return total
+
+    return start, second, third, fourth, finish
+
+
+def reduce_refs(side, depth, rows):
+    dma = pltpu.SemaphoreType.DMA
+    f32 = jnp.float32
+    return [
+        pltpu.VMEM((side, side, rows, LANES), f32),
+        pltpu.VMEM((side - 1, side, rows, LANES), f32),
+        pltpu.VMEM((side - 1, rows, LANES), f32),
+        pltpu.VMEM((depth, rows, LANES), f32),
+        dma((side, side)),
+        dma((side, side)),
+        dma((side - 1, side)),
+        dma((side - 1, side)),
+        dma((side - 1,)),
+        dma((side - 1,)),
+        dma((depth - 1,)),
+        dma((depth,)),
+    ]
+
+
+def modulation_stages(grid, images, slots, own_ref, info_ref, cond_ref, mod_ref, held_ref, refs):
+    everyone, wide, columns, parts, square = refs[:5]
+    gather = gather_blocks(grid, everyone, COND_ROWS, refs[5:11])
+    reduce = reduce_blocks(grid, parts, IMAGE_ROWS, refs[11:23])
+    here = grid.place
+    depth = held_depth(slots)
+
     def run(s):
+        spread_modulation(s, own_ref, info_ref, wide)
+
         @pl.when(s == 0)
         def _():
-            for k in range(depth - 1):
-                to_z(k, grid.seat("z", grid.other("z", k))).start()
+            everyone[pl.ds(pl.multiple_of(here * COND_ROWS, 8), COND_ROWS), :] = cond_ref[...]
+            gather[0]()
+            square[...] = jnp.zeros_like(square)
+            held_ref[...] = jnp.zeros_like(held_ref)
 
         @pl.when(s == 2)
         def _():
-            for k in range(depth - 1):
-                to_z(k, k).wait_recv()
-            total = part_ref[...].astype(jnp.float32)
-            for k in range(depth - 1):
-                total = total + arrived[k].astype(jnp.float32)
-            total = total.astype(jnp.bfloat16).astype(jnp.float32)
-            summed[here] = total[:IMAGE_ROWS]
-            for k in range(depth - 1):
-                to_z(k, 0).wait_send()
-            for copy in v_copies():
-                copy.start()
-            load(0).start()
-            load(1).start()
-            dense[...] = jnp.zeros_like(dense)
-            for block in range(MOD_BLOCKS):
-                dense[0:SEGS, block * LANES : (block + 1) * LANES] = summed[
-                    here, pl.ds(block, SEGS, stride=MOD_BLOCKS), :
-                ]
+            gather[1]()
 
         @pl.when(s == 4)
         def _():
-            for k in range(side - 1):
-                one(here, send_v.at[k], recv_v.at[k], grid.sibling).wait_recv()
-            for copy in v_copies():
-                copy.wait_send()
-            for copy in u_copies():
-                copy.start()
+            gather[2]()
+
+        @pl.when(s == 7)
+        def _():
+            gather[3]()
+
+        @pl.when(s == 8)
+        def _():
+            for block in range(D // LANES):
+                square[0:images, :] = everyone[pl.ds(block, images, stride=COND_STRIDE), :]
+                held_ref[block * LANES : (block + 1) * LANES, :] = square[...].T
+            held_ref[D : D + 8, :] = (lax.broadcasted_iota(jnp.int32, (8, LANES), 0) == 0).astype(jnp.float32)
+            for part in range(columns.shape[1] // LANES):
+                columns[:, part * LANES : (part + 1) * LANES] = (
+                    held_ref[pl.ds(info_ref[0] + part * LANES, LANES), :].T.astype(jnp.bfloat16)
+                )
+
+        at_product = s - 9
+
+        @pl.when((at_product >= 0) & (at_product < PRODUCT_STEPS))
+        def _():
+            left = columns[0:images, 0:depth]
+            each = MOD_BLOCKS // 2 // PRODUCT_STEPS
+            for pair in range(each):
+                block = (at_product * each + pair) * 2
+                right = jnp.concatenate(
+                    [held_columns(wide, info_ref, depth, block), held_columns(wide, info_ref, depth, block + 1)],
+                    axis=1,
+                )
+                found = jnp.dot(left, right, preferred_element_type=jnp.float32)
+                parts[pl.ds(block, images, stride=MOD_BLOCKS), :] = found[:, :LANES]
+                parts[pl.ds(block + 1, images, stride=MOD_BLOCKS), :] = found[:, LANES:]
+
+        @pl.when(s == 18)
+        def _():
+            reduce[0]()
+
+        for at, stage in ((20, 1), (23, 2), (26, 3)):
+            @pl.when(s == at)
+            def _(stage=stage):
+                reduce[stage]()
+
+        @pl.when(s == 29)
+        def _():
+            mod_ref[...] = reduce[4]()
+
+    return run
+
+
+def modulation_refs(side, depth, images, slots):
+    data_count = side * side * 2
+    lanes = -(-held_depth(slots) // LANES) * LANES
+    f32 = jnp.float32
+    return (
+        [
+            pltpu.VMEM((data_count * COND_ROWS, LANES), f32),
+            pltpu.VMEM((wide_rows(slots), LANES), f32),
+            pltpu.VMEM((LANES, lanes), jnp.bfloat16),
+            pltpu.VMEM((data_count * IMAGE_ROWS, LANES), f32),
+            pltpu.VMEM((LANES, LANES), f32),
+        ]
+        + gather_sems(side)
+        + reduce_refs(side, depth, IMAGE_ROWS)
+    )
+
+
+def modulation_grad_stages(grid, images, slots, own_ref, info_ref, part_ref, all_ref, cond_ref, refs):
+    arrived, summed, wide, around, parts, send_z, recv_z, done_sem = refs[:8]
+    gather = gather_blocks(grid, summed, IMAGE_ROWS, refs[8:14])
+    reduce = reduce_blocks(grid, parts, COND_ROWS, refs[14:26])
+    mine = grid.mine
+    sizes = grid.sizes["z"]
+    here = pl.ds(pl.multiple_of(grid.place * IMAGE_ROWS, 8), IMAGE_ROWS)
+    depth = held_depth(slots)
+
+    def to_z(k):
+        return pltpu.make_async_remote_copy(
+            src_ref=part_ref, dst_ref=arrived.at[mine["z"]], send_sem=send_z.at[k], recv_sem=recv_z.at[mine["z"]],
+            device_id=grid.device("z", grid.other("z", k)), device_id_type=MESH,
+        )
+
+    def run(s):
+        spread_modulation(s, own_ref, info_ref, wide)
+
+        @pl.when(s == 0)
+        def _():
+            for k in range(sizes - 1):
+                to_z(k).start()
+            arrived[mine["z"]] = part_ref[...]
+            around[...] = jnp.zeros_like(around)
+            parts[...] = jnp.zeros_like(parts)
+
+        @pl.when(s == 2)
+        def _():
+            for k in range(sizes - 1):
+                other = grid.other("z", k)
+                pltpu.make_async_remote_copy(
+                    src_ref=part_ref, dst_ref=arrived.at[other], send_sem=send_z.at[k], recv_sem=recv_z.at[other],
+                    device_id=grid.sibling, device_id_type=MESH,
+                ).wait_recv()
+            for k in range(sizes - 1):
+                to_z(k).wait_send()
+            total = arrived[0].astype(jnp.float32)
+            for z in range(1, sizes):
+                total = total + arrived[z].astype(jnp.float32)
+            summed[here, :] = total.astype(jnp.bfloat16).astype(jnp.float32)[:IMAGE_ROWS]
+            gather[0]()
+
+        @pl.when(s == 4)
+        def _():
+            gather[1]()
 
         @pl.when(s == 6)
         def _():
-            for k in range(side - 1):
-                for v in range(side):
-                    one(here, send_u.at[k, v], recv_u.at[k, v], grid.sibling).wait_recv()
-            for copy in u_copies():
-                copy.wait_send()
-            for copy in c_copies():
-                copy.start()
+            gather[2]()
 
         @pl.when(s == 9)
         def _():
-            for copy in c_copies():
-                copy.wait_recv()
-            for copy in c_copies():
-                copy.wait_send()
+            gather[3]()
             pltpu.make_async_copy(summed, all_ref, done_sem).start()
 
-        i = s - 10
-
-        @pl.when((i >= 0) & (i < chunks))
-        def _():
-            load(i).wait()
-            cond_ref[:, pl.ds(pl.multiple_of(i * COND_CHUNK, COND_CHUNK), COND_CHUNK)] = lax.dot_general(
-                dense[...].astype(jnp.bfloat16), held[i % 2], (((1,), (1,)), ((), ())),
-                preferred_element_type=jnp.float32,
-            )
-
-            @pl.when(i + 2 < chunks)
-            def _():
-                load(i + 2).start()
-
-        @pl.when(s == 10 + chunks)
-        def _():
+        at_product = s - 10
+
+        @pl.when((at_product >= 0) & (at_product < PRODUCT_STEPS))
+        def _():
+            total = around[D + 8 : D + 8 + depth, 0:images]
+            each = MOD_BLOCKS // 2 // PRODUCT_STEPS
+            for pair in range(each):
+                block = (at_product * each + pair) * 2
+                left = jnp.concatenate(
+                    [held_columns(wide, info_ref, depth, block), held_columns(wide, info_ref, depth, block + 1)],
+                    axis=1,
+                )
+                right = jnp.concatenate(
+                    [
+                        summed[pl.ds(block + more, images, stride=MOD_BLOCKS), :].astype(jnp.bfloat16)
+                        for more in (0, 1)
+                    ],
+                    axis=1,
+                )
+                total = total + lax.dot_general(
+                    left, right, (((1,), (1,)), ((), ())), preferred_element_type=jnp.float32
+                )
+            around[D + 8 : D + 8 + depth, 0:images] = total
+
+        @pl.when(s == 19)
+        def _():
+            for block in range(D // LANES):
+                piece = around[pl.ds(D + 8 - info_ref[0] + block * LANES, LANES), :].T
+                parts[pl.ds(block, images, stride=COND_STRIDE), :] = piece[0:images, :]
+            reduce[0]()
+
+        for at, stage in ((21, 1), (24, 2), (27, 3)):
+            @pl.when(s == at)
+            def _(stage=stage):
+                reduce[stage]()
+
+        @pl.when(s == 30)
+        def _():
+            cond_ref[...] = reduce[4]()
             pltpu.make_async_copy(summed, all_ref, done_sem).wait()
 
     return run
 
 
-def reduce_body(side, depth, plan, slots, parts_ref, part_ref, weight_ref, out_ref, all_ref, cond_ref, *refs):
+MOD_GRAD_REFS = 26
+
+
+def modulation_grad_refs(side, depth, images, slots):
+    data_count = side * side * 2
+    dma = pltpu.SemaphoreType.DMA
+    f32 = jnp.float32
+    return (
+        [
+            pltpu.VMEM((depth, SENT_ROWS, LANES), jnp.bfloat16),
+            pltpu.VMEM((data_count * IMAGE_ROWS, LANES), f32),
+            pltpu.VMEM((wide_rows(slots), LANES), f32),
+            pltpu.VMEM((2 * (D + 8) + held_depth(slots), LANES), f32),
+            pltpu.VMEM((data_count * COND_ROWS, LANES), f32),
+            dma((depth - 1,)),
+            dma((depth,)),
+            dma,
+        ]
+        + gather_sems(side)
+        + reduce_refs(side, depth, COND_ROWS)
+    )
+
+
+def reduce_body(side, depth, plan, slots, parts_ref, part_ref, own_ref, info_ref, out_ref, all_ref, cond_ref,
+                *refs):
     hosts, share, kept, steps, parts = plan
     grid = Grid(side, depth)
     hosting = Hosting(grid, 2 * side * side * depth, hosts, share, kept, slots - kept) if hosts else None
     grid.greet(hosting)
     passed = refs[-1]
-    modulation_step = modulation_stages(grid, part_ref, weight_ref, all_ref, cond_ref, refs[:MOD_REFS])
-    refs = refs[MOD_REFS:]
+    modulation_step = modulation_grad_stages(
+        grid, 2 * side * side * SEGS, slots, own_ref, info_ref, part_ref, all_ref, cond_ref, refs[:MOD_GRAD_REFS]
+    )
+    refs = refs[MOD_GRAD_REFS:]
     streams = []
     writes = []
     first = 0
@@ -1052,7 +1477,7 @@
             ).wait_recv()
 
 
-def reduce_slots(grads, mod_part, mod_weight, slots, data_count, seq_count):
+def reduce_slots(grads, mod_part, own, info, slots, data_count, seq_count):
     side = math.isqrt(data_count // 2)
     plan = host_plan(slots, data_count * seq_count, seq_count)
     kept, parts = plan[2], plan[4]
@@ -1061,22 +1486,7 @@
     regular = pltpu.SemaphoreType.REGULAR
     bf16 = jnp.bfloat16
     f32 = jnp.float32
-    scratch = [
-        pltpu.VMEM((seq_count - 1, SENT_ROWS, LANES), bf16),
-        pltpu.VMEM((8, 6 * D), f32),
-        pltpu.VMEM((2, COND_CHUNK, 6 * D), bf16),
-        dma((seq_count - 1,)),
-        dma((seq_count - 1,)),
-        dma((side - 1,)),
-        dma((side - 1,)),
-        dma((side - 1, side)),
-        dma((side - 1, side)),
-        dma((side, side)),
-        dma((side, side)),
-        dma((2,)),
-        dma,
-        pltpu.VMEM((data_count, IMAGE_ROWS, LANES), f32),
-    ]
+    scratch = modulation_grad_refs(side, seq_count, data_count * SEGS, slots)
     for order, part in zip(ORDERS, parts):
         span = part * SUBS
         sizes = {"u": side, "v": side, "z": seq_count}
@@ -1104,13 +1514,14 @@
         partial(reduce_body, side, seq_count, plan, slots),
         out_shape=(
             jax.ShapeDtypeStruct((slots * SUBS, LANES), bf16),
-            jax.ShapeDtypeStruct((data_count, IMAGE_ROWS, LANES), f32),
-            jax.ShapeDtypeStruct((8, D), f32),
+            jax.ShapeDtypeStruct((data_count * IMAGE_ROWS, LANES), f32),
+            jax.ShapeDtypeStruct((COND_ROWS, LANES), f32),
         ),
         in_specs=[
             pl.BlockSpec(memory_space=pl.ANY),
             pl.BlockSpec(memory_space=pltpu.VMEM),
-            pl.BlockSpec(memory_space=pl.ANY),
+            pl.BlockSpec(memory_space=pltpu.VMEM),
+            pl.BlockSpec(memory_space=pltpu.SMEM),
         ],
         out_specs=(
             pl.BlockSpec(memory_space=pl.ANY),
@@ -1122,7 +1533,7 @@
             collective_id=1, has_side_effects=True, vmem_limit_bytes=VMEM_LIMIT
         ),
         name="reduce_slots",
-    )(grads.reshape(data_count, seq_count, kept * SUBS, LANES), mod_part, mod_weight)
+    )(grads.reshape(data_count, seq_count, kept * SUBS, LANES), mod_part, own, info)
 
 
 UPDATE_TILES = 72
@@ -1174,18 +1585,11 @@
         )
 
 
-def own_conditions(cond_all, own_first, slots):
-    images = cond_all.shape[0]
+def own_conditions(held, info, images, slots):
     steps = -(-slots // UPDATE_TILES)
     depth = -(-(steps * UPDATE_TILES * SUBS + MOD_BLOCKS) // MOD_BLOCKS)
     depth = -(-depth // 8) * 8
-    extended = jnp.concatenate(
-        [cond_all.T, jnp.ones((1, images), jnp.bfloat16), jnp.zeros((depth, images), jnp.bfloat16)],
-        axis=0,
-    )
-    return lax.dynamic_slice_in_dim(
-        extended, jnp.minimum(own_first[0] * SUBS // MOD_BLOCKS, D + 1), depth, 0
-    )
+    return lax.dynamic_slice(held, (info[0], jnp.int32(0)), (depth, images)).astype(jnp.bfloat16)
 
 
 def update(reduced, cond_own, mod_all, own_first, master, first, second):
@@ -1456,25 +1860,40 @@
     )
     edge_ids = jnp.asarray(EDGE_TILES, jnp.int32)
     edge_owner = jnp.sum((tile_ends[None, :] <= edge_ids[:, None]).astype(jnp.int32), axis=1)
-    edge_slots = edge_owner * slot_count + edge_ids - jnp.take(starts, edge_owner)
+    edge_within = edge_ids - jnp.take(starts, edge_owner)
+    edge_places = edge_owner * plan[2] + edge_within
+    if plan[0]:
+        edge_places = jnp.where(
+            edge_within < plan[2], edge_places, jnp.take(guests, edge_owner) + edge_within - plan[2]
+        )
     own_place = data_place * seq_count + seq_place
     own_start = lax.dynamic_index_in_dim(starts, own_place, 0, False)
     own_count = lax.dynamic_index_in_dim(tile_counts, own_place, 0, False)
     own_low = master.astype(jnp.bfloat16).reshape(own_rows, LANES)
-    packed = gather_slots(own_low, slot_count, data_count, seq_count)
+    info = jnp.stack(
+        [
+            jnp.minimum(own_start * SUBS // MOD_BLOCKS, D + 1),
+            own_start * SUBS % MOD_BLOCKS,
+            jnp.clip(jnp.minimum(own_count * SUBS, MOD_ROWS - own_start * SUBS), 0, own_rows),
+        ]
+    ).astype(jnp.int32)
+    images = data_count * SEGS
 
     own_first = jnp.stack([own_start, own_count])
     cond_f = conditions.astype(jnp.float32)
     cond_act, silu_cond_back = jax.vjp(jax.nn.silu, cond_f)
     cond_low = cond_act.astype(jnp.bfloat16)
+    cond_rows = jnp.pad(cond_low[0].astype(jnp.float32), ((0, 0), (0, LANES))).reshape(COND_ROWS, LANES)
+    packed, modulation, cond_held = gather_slots(own_low, cond_rows, info, slot_count, data_count, seq_count)
+    modulation = modulation.reshape(1, SEGS, 6 * D)
     weights = {
-        index: unpack_weight(index, packed, slot_count, firsts, lasts, starts)
-        for index in (0, 2, 5, 7, 9, 15)
+        index: unpack_weight(index, packed, plan, firsts, lasts, starts, guests)
+        for index in (2, 5, 7, 9, 15)
     }
-    mod_weight, attend_weight, output_weight, hidden_weight, return_weight, proj_three = (
-        weights[index] for index in (0, 2, 5, 7, 9, 15)
-    )
-    edges = edge_read(packed, edge_slots)
+    attend_weight, output_weight, hidden_weight, return_weight, proj_three = (
+        weights[index] for index in (2, 5, 7, 9, 15)
+    )
+    edges = edge_read(packed, edge_places)
     edge_flat = edges.reshape(-1)
 
     def bias(index):
@@ -1482,10 +1901,6 @@
         at = EDGE_TILES.index(row // SUBS) * SUBS + row % SUBS
         return edge_flat[at * LANES : at * LANES + param_shapes()[index][0]]
 
-    mod_bias = bias(1)
-    modulation = (
-        jnp.einsum("rsd,dc->rsc", cond_low, mod_weight, preferred_element_type=jnp.float32) + mod_bias
-    )
     query_bias, value_bias, output_bias, hidden_bias, return_bias = (bias(i) for i in (3, 4, 6, 8, 10))
     proj_bias_one, proj_bias_two, proj_bias_three = (bias(i) for i in (12, 14, 16))
     rows_dev, local_len, model_width = tokens.shape
@@ -1517,7 +1932,7 @@
     head_attended = attention(head_rows, segment_ids[0], padding[0], heads_local)
     head_attended = head_attended.reshape(seq_count, local_len, group_width)
     head_attended, packed = lax.optimization_barrier((head_attended, packed))
-    proj_one, proj_two = (unpack_weight(index, packed, slot_count, firsts, lasts, starts) for index in (11, 13))
+    proj_one, proj_two = (unpack_weight(index, packed, plan, firsts, lasts, starts, guests) for index in (11, 13))
     attended = lax.all_to_all(head_attended, "seq", split_axis=0, concat_axis=0, tiled=True)
     attended, proj_one, proj_two = lax.optimization_barrier((attended, proj_one, proj_two))
     attended = join_groups(attended, 1, group_width)[None]
@@ -1626,17 +2041,15 @@
     grad_triple_heads = attention_grad(
         head_rows, head_grad.reshape(full_len, group_width), segment_ids[0], padding[0], heads_local
     ).reshape(seq_count, local_len, head_rows.shape[-1])
-    grad_triple_heads, grad_buffer, cond_low = lax.optimization_barrier(
-        (grad_triple_heads, grad_buffer, cond_low)
+    grad_triple_heads, grad_buffer, cond_held = lax.optimization_barrier(
+        (grad_triple_heads, grad_buffer, cond_held)
     )
     grad_triple = lax.all_to_all(grad_triple_heads, "seq", split_axis=0, concat_axis=0, tiled=True)
     grad_buffer = put(grad_buffer, 13, first_low, grad_second)
     grad_buffer = put(grad_buffer, 9, activated, grad_branch_two)
     grad_buffer = put(grad_buffer, 7, mlp_in, grad_hidden)
     grad_buffer = put(grad_buffer, 5, attended, grad_branch_one)
-    cond_all = lax.all_gather(cond_low, "dp", axis=0, tiled=True)
-    image_rows = cond_all.shape[0]
-    cond_own = own_conditions(cond_all.reshape(image_rows * SEGS, D), own_first, slot_count)
+    cond_own = own_conditions(cond_held, info, images, slot_count)
     grad_triple, grad_buffer, cond_own = lax.optimization_barrier((grad_triple, grad_buffer, cond_own))
     grad_triple = join_groups(grad_triple, 3, group_width)[None]
     grad_buffer = put(grad_buffer, 2, attend_in, grad_triple)
@@ -1694,19 +2107,11 @@
         tail(15),
         whole(sum_sixteen),
     ]
-    hosts, _, kept = plan[:3]
-    edge_within = edge_ids - jnp.take(starts, edge_owner)
-    edge_places = edge_owner * kept + edge_within
-    if hosts:
-        edge_places = jnp.where(
-            edge_within < kept, edge_places, jnp.take(guests, edge_owner) + edge_within - kept
-        )
     grad_buffer = edge_write(pieces, grad_buffer, edge_places[EDGE_TILES.index(3891) :])
     reduced, mod_all, cond_grad = reduce_slots(
-        grad_buffer, mod_sent, mod_weight, slot_count, data_count, seq_count
-    )
-    (grad_conditions,) = silu_cond_back(cond_grad[None, :SEGS])
-    mod_all = mod_all.reshape(image_rows * IMAGE_ROWS, LANES)
+        grad_buffer, mod_sent, own_low, info, slot_count, data_count, seq_count
+    )
+    (grad_conditions,) = silu_cond_back(cond_grad.reshape(1, SEGS, COND_STRIDE * LANES)[:, :, :D])
     new_master, new_first, new_second = update(
         reduced, cond_own, mod_all, own_first, master, first_moment, second_moment
     )

time: 1040 us -> 989 us (0.951)
  Pallas kernels: 846 us -> 813 us
  blocking collectives: 10.6 us -> 0 us
    pallas_call x1, Pallas kernels: 320 us -> 301 us  [gather_slots(): pl.pallas_call(partial(gather_body, side, seq_count, plan, slots, images)...]
    pallas_call x8 -> x7, Pallas kernels: 86.6 us -> 69.4 us  [unpack_weight(): pl.pallas_call(partial(unpack_body, base, row // SUBS, per_chunk, tiles,...]
    all_gather x1 -> x0, blocking collectives: 10.6 us -> none  [shards(): cond_all = lax.all_gather(cond_low, 'dp', axis=0, tiled=True)]
  transfers between devices with their start and end apart: 4 -> 4, of which waited for: 2 -> 2; matrix products, arithmetic and copies ran while one was open for 1% -> 1% of each run, Pallas kernels for 11% -> 12%
where the time goes in v5:
time: 989 us; the launch traced here: 984 us
  Pallas kernels  813 us (82%)
  matrix products  85.7 us (9%)
  other arithmetic  31.8 us (3%)
  local copies, waits for them, and re-layouts  28.1 us (3%)
  starting transfers between devices  16.5 us (2%)
    pallas_call x1, Pallas kernels, gather_slots(): pl.pallas_call(partial(gather_body, side, seq_count, plan, slots, images)...  301 us
    pallas_call x1, Pallas kernels, reduce_slots(): pl.pallas_call(partial(reduce_body, side, seq_count, plan, slots), out_sh...  295 us
    pallas_call x7, Pallas kernels, unpack_weight(): pl.pallas_call(partial(unpack_body, base, row // SUBS, per_chunk, tiles,...  69.4 us
    pallas_call x7, Pallas kernels, weight_grad(): pl.pallas_call(partial(weight_grad_body, base, row // SUBS, per_chunk, sh...  66 us
    pallas_call x1, Pallas kernels, attention_grad(): pl.pallas_call(partial(attention_grad_body, heads), out_shape=jax.ShapeDt...  28.7 us
  transfers between devices with their start and end apart: 4, of which 2 were waited for; matrix products, arithmetic and copies ran while one was open for 1% of the time, Pallas kernels for 12%

profile of v5, /device:TPU:1, one launch (start us, length us, event | category | flops | bytes accessed | tf_op | source)
XLA Modules:
  0.0 983.7 jit_solution(18099369308615676024)
XLA Ops:
  5.8 1.4 fusion.27
  10.1 2.8 convert_element_type.188
  13.0 2.6 reshape.632.own_ref
  16.2 300.6 %gather_slots.1 = (bf16[8,4,8256,128]{3,2,1,0:T(8,128)(2,1)}, f32[216,128]{1,0:T(8,128)}, f32[1536,128]{1,0:T(8,128)}) custom-call(bf16[9792,128]{1,0:T(8,128)(2,1)} %reshape.632.own_ref, f32[40,128]{1,0:T(8,128)} %reshape.661.cond_ref, s32[3]{0:T(128)} %pad_add_fusion.1.info_ref), custom_call_target="tpu_custom_call" | custom-call | tf_op jit(solution)/shard_map/gather_slots/pallas_call | solution.py:771
  318.9 2.2 edge_read.1
  321.1 1.4 fusion.48
  323.2 3.0 convolution_bitcast_fusion
  326.2 2.9 copy-done.2
  329.5 11.4 %unpack_2.1 = bf16[1152,3456]{1,0:T(8,128)(2,1)} custom-call(s32[43]{0:T(128)} %get-tuple-element.95.first_ref, s32[43]{0:T(128)} %get-tuple-element.94.last_ref, s32[33]{0:T(128)} %copy-done.1, s32[32]{0:T(128)} %constant.152.clone.guests_ref, bf16[264192,128]{1,0:T(8,128)(2,1)} %bitcast.11.packed), custom_call_target="tpu_custom_call" | custom-call | bytes 15925248 | tf_op jit(solution)/shard_map/unpack_2/pallas_call | solution.py:147
  340.9 7.0 fusion.1.x_ref
  347.9 3.4 split_groups_3.1
  351.3 3.8 all-to-all-start
  355.1 5.2 unpack_5.1
  360.3 4.2 unpack_15.1
  364.5 13.3 %unpack_9.1 = bf16[4608,1152]{1,0:T(8,128)(2,1)} custom-call(s32[43]{0:T(128)} %get-tuple-element.95.first_ref, s32[43]{0:T(128)} %get-tuple-element.94.last_ref, s32[33]{0:T(128)} %copy-done.1, s32[32]{0:T(128)} %constant.152.clone.guests_ref, bf16[264192,128]{1,0:T(8,128)(2,1)} %bitcast.11.packed), custom_call_target="tpu_custom_call" | custom-call | bytes 21233664 | tf_op jit(solution)/shard_map/unpack_9/pallas_call | solution.py:147
  377.8 13.3 %unpack_7.1 = bf16[1152,4608]{1,0:T(8,128)(2,1)} custom-call(s32[43]{0:T(128)} %get-tuple-element.95.first_ref, s32[43]{0:T(128)} %get-tuple-element.94.last_ref, s32[33]{0:T(128)} %copy-done.1, s32[32]{0:T(128)} %constant.152.clone.guests_ref, bf16[264192,128]{1,0:T(8,128)(2,1)} %bitcast.11.packed), custom_call_target="tpu_custom_call" | custom-call | bytes 21233664 | tf_op jit(solution)/shard_map/unpack_7/pallas_call | solution.py:147
  393.2 4.4 all-to-all-done
  398.8 18.8 %attention.1 = bf16[1024,288]{1,0:T(8,128)(2,1)} custom-call(bf16[1024,896]{1,0:T(8,128)(2,1)} %bitcast.156, s32[1024,1]{1,0:T(8,128)} %copy.42.seg_col, s32[1024,1]{1,0:T(8,128)} %copy.43.pad_col, s32[1,1024]{1,0:T(1,128)} %seg_row.3), custom_call_target="tpu_custom_call" | custom-call | tf_op jit(solution)/shard_map/attention/pallas_call | solution.py:1748
  417.7 2.2 copy.44
  419.9 3.5 all-to-all-start.1
  425.5 8.5 unpack_11.1
  434.0 13.5 %unpack_13.1 = bf16[2048,2048]{1,0:T(8,128)(2,1)} custom-call(s32[43]{0:T(128)} %get-tuple-element.95.first_ref, s32[43]{0:T(128)} %get-tuple-element.94.last_ref, s32[33]{0:T(128)} %copy-done.1, s32[32]{0:T(128)} %constant.152.clone.guests_ref, bf16[264192,128]{1,0:T(8,128)(2,1)} %bitcast.11.packed), custom_call_target="tpu_custom_call" | custom-call | bytes 16777216 | tf_op jit(solution)/shard_map/unpack_13/pallas_call | solution.py:147
  448.7 2.2 join_groups_1.1.x_ref
  450.9 4.3 fusion.81
  455.5 2.1 fusion.36.x_ref
  457.6 11.2 %multiply_convert_fusion = (bf16[256,4608]{1,0:T(8,128)(2,1)S(1)}, f32[256,4608]{1,0:T(8,128)}) fusion(f32[4608]{0:T(1024)S(1)} %fusion.44, bf16[256,1152]{1,0:T(8,128)(2,1)S(1)} %fusion.36.x_ref, bf16[1152,4608]{1,0:T(8,128)(2,1)} %unpack_7.1), kind=kOutput, calls=%fused_computation.18 | convolution fusion | flops 2729705472 | bytes 18302976 | tf_op jit(solution)/shard_map/rtd,df->rtf/dot_general | solution.py:1947
  468.9 4.3 add_convert_fusion
  473.2 3.1 multiply_convert_fusion.2
  476.3 6.1 convolution_add_fusion.4
  482.5 1.6 fusion.76
  484.7 1.7 multiply_reduce_fusion.2
  487.6 2.0 convert_reduce_fusion.2
  489.6 7.9 convert_reduce_fusion.3
  497.5 2.4 convert_reduce_fusion.5
  499.8 9.1 convert_reduce_fusion
  509.0 8.3 multiply_reduce_fusion
  517.8 1.9 convert_reduce_fusion.6
  520.0 1.9 convolution_convert_fusion.1.x_ref
  521.8 2.2 split_groups_1.1
  524.1 2.2 copy.46
  526.3 4.7 all-to-all-start.2
  531.0 5.5 weight_grad_15.1
  536.5 8.4 weight_grad_11.1
  544.9 1.6 all-to-all-done.2
  546.5 2.2 copy.47
  548.7 28.7 %attention_grad.1 = bf16[1024,896]{1,0:T(8,128)(2,1)} custom-call(bf16[1024,896]{1,0:T(8,128)(2,1)} %bitcast.157, bf16[1024,288]{1,0:T(8,128)(2,1)} %bitcast.161, s32[1024,1]{1,0:T(8,128)} %copy.42.seg_col, s32[1024,1]{1,0:T(8,128)} %copy.43.pad_col, s32[1,1024]{1,0:T(1,128)} %seg_row.3), custom_call_target="tpu_custom_call" | custom-call | tf_op jit(solution)/shard_map/attention_grad/pallas_call | solution.py:1810
  577.4 4.6 all-to-all-start.3
  582.0 1.7 pad_add_fusion.2.own_ref
  583.8 12.2 %weight_grad_13.1 = (bf16[264192,128]{1,0:T(8,128)(2,1)}, f32[32,128]{1,0:T(8,128)}) custom-call(s32[43]{0:T(128)} %get-tuple-element.95.first_ref, s32[43]{0:T(128)} %get-tuple-element.94.last_ref, s32[33]{0:T(128)} %copy-done.1, s32[32]{0:T(128)} %constant.152.clone.guests_ref, bf16[256,2048]{1,0:T(8,128)(2,1)} %copy-done.21, ...), custom_call_target="tpu_custom_call", output_to_operand_aliasing={{0}: (6, {})} | custom-call | flops 2147483648 | bytes 8388608 | tf_op jit(solution)/shard_map/weight_grad_13/pallas_call | solution.py:346
  596.0 11.9 %weight_grad_9.1 = (bf16[264192,128]{1,0:T(8,128)(2,1)}, f32[32,128]{1,0:T(8,128)}) custom-call(s32[43]{0:T(128)} %get-tuple-element.95.first_ref, s32[43]{0:T(128)} %get-tuple-element.94.last_ref, s32[33]{0:T(128)} %copy-done.1, s32[32]{0:T(128)} %constant.152.clone.guests_ref, bf16[256,4608]{1,0:T(8,128)(2,1)} %copy-done.14, ...), custom_call_target="tpu_custom_call", output_to_operand_aliasing={{0}: (6, {})} | custom-call | flops 2717908992 | bytes 10616832 | tf_op jit(solution)/shard_map/weight_grad_9/pallas_call | solution.py:346
  607.9 11.5 %weight_grad_7.1 = (bf16[264192,128]{1,0:T(8,128)(2,1)}, f32[32,128]{1,0:T(8,128)}) custom-call(s32[43]{0:T(128)} %get-tuple-element.95.first_ref, s32[43]{0:T(128)} %get-tuple-element.94.last_ref, s32[33]{0:T(128)} %copy-done.1, s32[32]{0:T(128)} %constant.152.clone.guests_ref, bf16[256,1152]{1,0:T(8,128)(2,1)} %copy-done.16, ...), custom_call_target="tpu_custom_call", output_to_operand_aliasing={{0}: (6, {})} | custom-call | flops 2717908992 | bytes 10616832 | tf_op jit(solution)/shard_map/weight_grad_7/pallas_call | solution.py:346
  619.3 5.9 weight_grad_5.1
  625.2 1.5 dynamic-slice_convert_fusion.cond_ref
  626.8 3.4 join_groups_3.1.dy_ref
  630.2 1.8 convert_reduce_fusion.1
  632.0 8.2 constant_dynamic-update-slice_fusion.1
  640.2 10.6 %weight_grad_2.1 = (bf16[264192,128]{1,0:T(8,128)(2,1)}, f32[32,128]{1,0:T(8,128)}) custom-call(s32[43]{0:T(128)} %get-tuple-element.95.first_ref, s32[43]{0:T(128)} %get-tuple-element.94.last_ref, s32[33]{0:T(128)} %copy-done.1, s32[32]{0:T(128)} %constant.152.clone.guests_ref, bf16[256,1152]{1,0:T(8,128)(2,1)} %copy-done.13, ...), custom_call_target="tpu_custom_call", output_to_operand_aliasing={{0}: (6, {})} | custom-call | flops 2038431744 | bytes 7962624 | tf_op jit(solution)/shard_map/weight_grad_2/pallas_call | solution.py:346
  650.9 3.3 fusion.79
  654.2 1.6 multiply_dynamic-update-slice_fusion.2
  656.9 1.3 multiply_dynamic-update-slice_fusion.1
  659.7 5.3 convolution_convert_fusion
  666.3 2.3 edge_write.1
  668.6 294.5 %reduce_slots.1 = (bf16[9792,128]{1,0:T(8,128)(2,1)}, f32[1728,128]{1,0:T(8,128)}, f32[40,128]{1,0:T(8,128)}) custom-call(bf16[8,4,8256,128]{3,2,1,0:T(8,128)(2,1)} %bitcast.56.parts_ref, bf16[224,128]{1,0:T(8,128)(2,1)} %pad.10.part_ref, bf16[9792,128]{1,0:T(8,128)(2,1)} %reshape.632.own_ref, s32[3]{0:T(128)} %pad_add_fusion.1.info_ref), custom_call_target="tpu_custom_call" | custom-call | tf_op jit(solution)/shard_map/reduce_slots/pallas_call | solution.py:1513
  964.5 18.9 %update.1 = (f32[612,2048]{1,0:T(8,128)}, f32[612,2048]{1,0:T(8,128)}, f32[612,2048]{1,0:T(8,128)}) custom-call(s32[2]{0:T(128)} %pad_add_fusion.2.own_ref, bf16[9792,128]{1,0:T(8,128)(2,1)} %get-tuple-element.86.reduced, bf16[200,32]{1,0:T(8,128)(2,1)} %dynamic-slice_convert_fusion.cond_ref, f32[1728,128]{1,0:T(8,128)} %get-tuple-element.88.mod_ref, ...), custom_call_target="tpu_custom_call" | custom-call | tf_op jit(solution)/shard_map/update/pallas_call | solution.py:1601
  (160 shorter events, 25.4 us)
Async XLA Ops:
  1.6 11.3 %copy-start.1 = (s32[33]{0:T(128)}, s32[33]{0:T(128)S(1)}, u32[]{:S(2)}) copy-start(s32[33]{0:T(128)S(1)} %pad_add_fusion.starts_ref) | copy-start | bytes 400
  5.8 320.3 %copy-start.30 = (f32[256]{0:T(256)}, f32[256]{0:T(256)S(1)}, u32[]{:S(2)}) copy-start(f32[256]{0:T(256)S(1)} %broadcast_multiply_fusion.2) | copy-start | bytes 3076
  7.2 5.7 copy-start.38
  7.2 319.0 %copy-start.36 = (f32[256]{0:T(256)}, f32[256]{0:T(256)S(1)}, u32[]{:S(2)}) copy-start(f32[256]{0:T(256)S(1)} %fusion.60) | copy-start | bytes 3076
  15.6 302.1 %copy-start = (s32[32]{0:T(128)S(1)}, s32[32]{0:T(128)}, u32[]{:S(2)}) copy-start(s32[32]{0:T(128)} %constant.152.clone.guests_ref) | copy-start | bytes 388
  15.6 302.8 %copy-start.44 = (s32[15]{0:T(128)S(1)}, s32[15]{0:T(128)}, u32[]{:S(2)}) copy-start(s32[15]{0:T(128)} %constant.153.clone) | copy-start | bytes 184
  318.9 3.6 copy-start.26
  318.9 3.6 copy-start.42
  318.9 3.6 copy-start.43
  322.5 3.7 copy-start.34
  323.2 5.9 copy-start.4
  326.2 2.9 copy-start.2
  329.5 11.5 %copy-start.13 = (bf16[256,1152]{1,0:T(8,128)(2,1)}, bf16[256,1152]{1,0:T(8,128)(2,1)S(1)}, u32[]{:S(2)}) copy-start(bf16[256,1152]{1,0:T(8,128)(2,1)S(1)} %fusion.37.x_ref) | copy-start | bytes 1769476
  351.3 46.3 %all-to-all-start = ((bf16[4,256,896]{2,1,0:T(8,128)(2,1)}), bf16[4,256,896]{2,1,0:T(8,128)(2,1)S(1)}, u32[]{:S(2)}, u32[]{:S(2)}) async-start(bf16[4,256,896]{2,1,0:T(8,128)(2,1)} %split_groups_3.1), calls=%async_computation | async-start | bytes 3670016 | tf_op jit(solution)/shard_map/all_to_all | solution.py:1927
  377.8 14.4 %copy-start.41 = (s32[1,1024]{1,0:T(1,128)S(1)}, s32[1,1024]{1,0:T(1,128)}, u32[]{:S(2)}) copy-start(s32[1,1024]{1,0:T(1,128)} %param.16) | copy-start | bytes 12292
  397.6 1.2 copy-start.3
  419.9 27.6 %all-to-all-start.1 = ((bf16[4,256,288]{1,2,0:T(8,128)(2,1)}), bf16[4,256,288]{1,2,0:T(8,128)(2,1)S(1)}, u32[]{:S(2)}, u32[]{:S(2)}) async-start(bf16[4,256,288]{1,2,0:T(8,128)(2,1)} %copy.44), calls=%async_computation.1 | async-start | bytes 1179648 | tf_op jit(solution)/shard_map/all_to_all | solution.py:1936
  447.5 3.4 copy-start.5
  447.5 3.4 copy-start.25
  455.2 62.1 %copy-start.28 = (f32[256]{0:T(256)}, f32[256]{0:T(256)S(1)}, u32[]{:S(2)}) copy-start(f32[256]{0:T(256)S(1)} %broadcast_multiply_fusion.1) | copy-start | bytes 3076
  455.2 13.6 %slice-start = ((s8[7077888]{0:T(1024)(128)(4,1)}), s8[4194304]{0:T(1024)(128)(4,1)S(1)}, s32[]{:S(2)}) async-start(s8[7077888]{0:T(1024)(128)(4,1)} %bitcast.152), calls=%async_computation.4 | async-start | bytes 8388608
  455.4 61.9 %copy-start.32 = (f32[256]{0:T(256)}, f32[256]{0:T(256)S(1)}, u32[]{:S(2)}) copy-start(f32[256]{0:T(256)S(1)} %fusion.61) | copy-start | bytes 3076
  455.5 13.4 %slice-start.4 = ((s8[10616832]{0:T(1024)(128)(4,1)}), s8[4194304]{0:T(1024)(128)(4,1)S(1)}, s32[]{:S(2)}) async-start(s8[10616832]{0:T(1024)(128)(4,1)} %bitcast.158), calls=%async_computation.8 | async-start | bytes 8388608
  455.5 17.8 %slice-start.2 = ((s8[4718592]{0:T(1024)(128)(4,1)}), s8[4194304]{0:T(1024)(128)(4,1)S(1)}, s32[]{:S(2)}) async-start(s8[4718592]{0:T(1024)(128)(4,1)} %bitcast.154), calls=%async_computation.6 | async-start | bytes 8388608
  457.6 11.2 %copy-start.16 = (bf16[256,1152]{1,0:T(8,128)(2,1)}, bf16[256,1152]{1,0:T(8,128)(2,1)S(1)}, u32[]{:S(2)}) copy-start(bf16[256,1152]{1,0:T(8,128)(2,1)S(1)} %fusion.36.x_ref) | copy-start | bytes 1769476
  457.6 11.2 %slice-start.1 = ((s8[7077888]{0:T(1024)(128)(4,1)}), s8[2883584]{0:T(1024)(128)(4,1)S(1)}, s32[]{:S(2)}) async-start(s8[7077888]{0:T(1024)(128)(4,1)} %bitcast.152), calls=%async_computation.5 | async-start | bytes 5767168
  457.6 11.2 %slice-start.5 = ((s8[10616832]{0:T(1024)(128)(4,1)}), s8[4194304]{0:T(1024)(128)(4,1)S(1)}, s32[]{:S(2)}) async-start(s8[10616832]{0:T(1024)(128)(4,1)} %bitcast.158), calls=%async_computation.9 | async-start | bytes 8388608
  457.6 11.2 %slice-start.6 = ((s8[10616832]{0:T(1024)(128)(4,1)}), s8[2228224]{0:T(1024)(128)(4,1)S(1)}, s32[]{:S(2)}) async-start(s8[10616832]{0:T(1024)(128)(4,1)} %bitcast.158), calls=%async_computation.10 | async-start | bytes 4456448
  457.6 11.2 %copy-start.40 = (f32[1152]{0:T(1024)S(1)}, f32[1152]{0:T(1024)}, u32[]{:S(2)}) copy-start(f32[1152]{0:T(1024)} %get-tuple-element.118) | copy-start | bytes 13828
  457.6 15.6 %slice-start.3 = ((s8[4718592]{0:T(1024)(128)(4,1)}), s8[524288]{0:T(1024)(128)(4,1)S(1)}, s32[]{:S(2)}) async-start(s8[4718592]{0:T(1024)(128)(4,1)} %bitcast.154), calls=%async_computation.7 | async-start | bytes 1048576
  468.8 4.4 copy-start.14
  473.2 3.1 copy-start.23
  476.3 6.1 copy-start.21
  482.5 2.3 copy-start.11
  484.7 1.7 copy-start.18
  487.6 2.0 copy-start.24
  489.6 7.9 copy-start.22
  489.6 7.9 copy-start.20
  497.4 2.4 copy-start.10
  499.8 9.1 copy-start.17
  509.0 8.3 copy-start.15
  517.8 2.2 copy-start.7
  519.7 2.1 copy-start.12
  526.3 20.2 %all-to-all-start.2 = ((bf16[4,256,288]{1,2,0:T(8,128)(2,1)}), bf16[4,256,288]{1,2,0:T(8,128)(2,1)}, u32[]{:S(2)}, u32[]{:S(2)}) async-start(bf16[4,256,288]{1,2,0:T(8,128)(2,1)} %copy.46), calls=%async_computation.2 | async-start | bytes 1179648 | tf_op jit(solution)/shard_map/all_to_all | solution.py:2037
  577.4 49.4 %all-to-all-start.3 = ((bf16[4,256,896]{2,1,0:T(8,128)(2,1)}), bf16[4,256,896]{2,1,0:T(8,128)(2,1)}, u32[]{:S(2)}, u32[]{:S(2)}) async-start(bf16[4,256,896]{2,1,0:T(8,128)(2,1)} %bitcast.160), calls=%async_computation.3 | async-start | bytes 3670016 | tf_op jit(solution)/shard_map/all_to_all | solution.py:2047
  626.8 5.2 copy-start.6
  626.8 5.2 copy-start.31
  640.2 10.7 %copy-start.39 = (f32[256]{0:T(256)S(1)}, f32[256]{0:T(256)}, u32[]{:S(2)}) copy-start(f32[256]{0:T(256)} %copy-done.38) | copy-start | bytes 3076
  640.2 10.7 %copy-start.37 = (f32[256]{0:T(256)S(1)}, f32[256]{0:T(256)}, u32[]{:S(2)}) copy-start(f32[256]{0:T(256)} %copy-done.36) | copy-start | bytes 3076
  650.9 3.3 copy-start.8
  650.9 3.3 copy-start.9
  655.8 1.1 copy-start.29
  655.8 1.1 copy-start.33
  656.9 1.6 copy-start.19
  658.2 1.4 copy-start.35
  668.6 295.3 %copy-start.27 = (bf16[1,4,1152]{2,1,0:T(4,128)(2,1)S(1)}, bf16[1,4,1152]{2,1,0:T(4,128)(2,1)}, u32[]{:S(2)}) copy-start(bf16[1,4,1152]{2,1,0:T(4,128)(2,1)} %param.14) | copy-start | bytes 27652

commit v6 on v5

--- a/solution.py
+++ b/solution.py
@@ -27,7 +27,6 @@
 learn_rate = 0.02
 weight_decay = 0.01
 adam_eps = 1e-08
-highest = lax.Precision.HIGHEST
 
 
 LANES = 128
@@ -68,7 +67,7 @@
     return starts
 
 
-CHUNK = {2: 128, 5: 384, 7: 128, 9: 512, 11: 384, 13: 256, 15: 1024}
+CHUNK = {2: 384, 5: 384, 7: 384, 9: 1536, 11: 384, 13: 512, 15: 1024}
 EDGE_TILES = [3891, 5835, 5836, 6484, 6485, 9077, 9078, 9079, 11671, 12823, 12824, 14872, 14873, 15641, 15642]
 
 
@@ -1665,13 +1664,13 @@
 def split_groups(x, parts, groups):
     tokens, total = x.shape
     width = total // parts // groups
-    padded = lane_pad(parts * width) if parts > 1 else width
+    padded = lane_pad(parts * width)
     moves = [
         (None, (part * groups + group) * width, group, part * width, width)
         for group in range(groups)
         for part in range(parts)
     ]
-    fill = (parts * width, padded - parts * width) if padded > parts * width and parts > 1 else None
+    fill = (parts * width, padded - parts * width) if padded > parts * width else None
     return pl.pallas_call(
         partial(regroup_body, moves, fill),
         out_shape=jax.ShapeDtypeStruct((groups, tokens, padded), x.dtype),
@@ -1719,8 +1718,8 @@
     scores = lax.dot_general(
         held[1, head], held[0, head, block, :], (((1,), (1,)), ((), ())), preferred_element_type=jnp.float32
     )
-    scores = scores * (HEAD_DIM ** (-0.5)) + bias
-    shifted = jnp.exp(scores - jnp.max(scores, axis=0, keepdims=True))
+    scores = scores + bias
+    shifted = jnp.exp2((scores - jnp.max(scores, axis=0, keepdims=True)) * (HEAD_DIM ** (-0.5) * math.log2(math.e)))
     return shifted * (1.0 / jnp.sum(shifted, axis=0, keepdims=True))
 
 
@@ -1734,6 +1733,9 @@
     first = pl.multiple_of(step * QUERY_BLOCK, QUERY_BLOCK)
     block = pl.ds(first, QUERY_BLOCK)
     bias = key_bias(seg_col[...], pad_col[...], seg_row[...], first)
+    rest = out_ref.shape[1] - heads * HEAD_DIM
+    if rest:
+        out_ref[:, heads * HEAD_DIM :] = jnp.zeros((QUERY_BLOCK, rest), jnp.bfloat16)
     for head in range(heads):
         probs = probabilities(held, head, block, bias).astype(jnp.bfloat16)
         result = lax.dot_general(
@@ -1747,7 +1749,7 @@
     whole = pl.BlockSpec((length, 1), lambda i: (0, 0))
     return pl.pallas_call(
         partial(attention_body, heads),
-        out_shape=jax.ShapeDtypeStruct((length, heads * HEAD_DIM), jnp.bfloat16),
+        out_shape=jax.ShapeDtypeStruct((length, lane_pad(heads * HEAD_DIM)), jnp.bfloat16),
         grid=(length // QUERY_BLOCK,),
         in_specs=[
             pl.BlockSpec(rows.shape, lambda i: (0, 0)),
@@ -1755,7 +1757,7 @@
             whole,
             pl.BlockSpec((1, QUERY_BLOCK), lambda i: (0, i)),
         ],
-        out_specs=pl.BlockSpec((QUERY_BLOCK, heads * HEAD_DIM), lambda i: (i, 0)),
+        out_specs=pl.BlockSpec((QUERY_BLOCK, lane_pad(heads * HEAD_DIM)), lambda i: (i, 0)),
         scratch_shapes=[pltpu.VMEM((3, heads, length, LANES), jnp.bfloat16)],
         compiler_params=pltpu.CompilerParams(vmem_limit_bytes=VMEM_LIMIT),
         name="attention",
@@ -1888,10 +1890,10 @@
     modulation = modulation.reshape(1, SEGS, 6 * D)
     weights = {
         index: unpack_weight(index, packed, plan, firsts, lasts, starts, guests)
-        for index in (2, 5, 7, 9, 15)
+        for index in (2, 5, 7, 9, 11)
     }
-    attend_weight, output_weight, hidden_weight, return_weight, proj_three = (
-        weights[index] for index in (2, 5, 7, 9, 15)
+    attend_weight, output_weight, hidden_weight, return_weight, proj_one = (
+        weights[index] for index in (2, 5, 7, 9, 11)
     )
     edges = edge_read(packed, edge_places)
     edge_flat = edges.reshape(-1)
@@ -1911,7 +1913,7 @@
     local_seg = lax.dynamic_slice_in_dim(segment_ids, token_start, local_len, 1)
     local_pad = lax.dynamic_slice_in_dim(padding, token_start, local_len, 1).astype(jnp.float32)
     onehot = (local_seg[:, :, None] == jnp.arange(SEGS, dtype=jnp.int32)).astype(jnp.float32)
-    per_token = jnp.einsum("rts,rsc->rtc", onehot, modulation, precision=highest)
+    per_token = jnp.einsum("rts,rsc->rtc", onehot, modulation, precision=lax.Precision.HIGH)
     shift_one, scale_one, gate_one, shift_two, scale_two, gate_two = jnp.split(
         per_token, 6, axis=-1
     )
@@ -1925,16 +1927,16 @@
     )
     triple_low = split_groups(triple[0].astype(jnp.bfloat16), 3, seq_count)
     head_rows = lax.all_to_all(triple_low, "seq", split_axis=0, concat_axis=0, tiled=True)
-    (head_rows, output_weight, hidden_weight, return_weight, proj_three) = lax.optimization_barrier(
-        (head_rows, output_weight, hidden_weight, return_weight, proj_three)
+    (head_rows, output_weight, hidden_weight, return_weight, proj_one) = lax.optimization_barrier(
+        (head_rows, output_weight, hidden_weight, return_weight, proj_one)
     )
     head_rows = head_rows.reshape(full_len, head_rows.shape[-1])
     head_attended = attention(head_rows, segment_ids[0], padding[0], heads_local)
-    head_attended = head_attended.reshape(seq_count, local_len, group_width)
+    head_attended = head_attended.reshape(seq_count, local_len, head_attended.shape[-1])
     head_attended, packed = lax.optimization_barrier((head_attended, packed))
-    proj_one, proj_two = (unpack_weight(index, packed, plan, firsts, lasts, starts, guests) for index in (11, 13))
+    proj_two, proj_three = (unpack_weight(index, packed, plan, firsts, lasts, starts, guests) for index in (13, 15))
     attended = lax.all_to_all(head_attended, "seq", split_axis=0, concat_axis=0, tiled=True)
-    attended, proj_one, proj_two = lax.optimization_barrier((attended, proj_one, proj_two))
+    attended, proj_two, proj_three = lax.optimization_barrier((attended, proj_two, proj_three))
     attended = join_groups(attended, 1, group_width)[None]
     branch_one = (
         jnp.einsum("rtd,dc->rtc", attended, output_weight, preferred_element_type=jnp.float32)
@@ -2036,16 +2038,16 @@
     grad_attended, second_low = lax.optimization_barrier((grad_attended, second_low))
     head_grad = lax.all_to_all(grad_attended, "seq", split_axis=0, concat_axis=0, tiled=True)
     grad_buffer = put(None, 15, second_low, grad_projected)
-    grad_buffer = put(grad_buffer, 11, feature, grad_first)
+    grad_buffer = put(grad_buffer, 13, first_low, grad_second)
     head_grad, grad_buffer = lax.optimization_barrier((head_grad, grad_buffer))
     grad_triple_heads = attention_grad(
-        head_rows, head_grad.reshape(full_len, group_width), segment_ids[0], padding[0], heads_local
+        head_rows, head_grad.reshape(full_len, head_grad.shape[-1]), segment_ids[0], padding[0], heads_local
     ).reshape(seq_count, local_len, head_rows.shape[-1])
     grad_triple_heads, grad_buffer, cond_held = lax.optimization_barrier(
         (grad_triple_heads, grad_buffer, cond_held)
     )
     grad_triple = lax.all_to_all(grad_triple_heads, "seq", split_axis=0, concat_axis=0, tiled=True)
-    grad_buffer = put(grad_buffer, 13, first_low, grad_second)
+    grad_buffer = put(grad_buffer, 11, feature, grad_first)
     grad_buffer = put(grad_buffer, 9, activated, grad_branch_two)
     grad_buffer = put(grad_buffer, 7, mlp_in, grad_hidden)
     grad_buffer = put(grad_buffer, 5, attended, grad_branch_one)
@@ -2064,7 +2066,7 @@
         [grad_attend_in, grad_scale_one, grad_gate_one, grad_mlp_in, grad_scale_two, grad_gate_two],
         axis=-1,
     )
-    mod_part = jnp.einsum("rts,rtc->rsc", onehot, token_mod_grad, precision=highest)
+    mod_part = jnp.einsum("rts,rtc->rsc", onehot, token_mod_grad, precision=lax.Precision.HIGH)
     mod_sent = jnp.pad(
         mod_part.astype(jnp.bfloat16).reshape(IMAGE_ROWS, LANES), ((0, SENT_ROWS - IMAGE_ROWS), (0, 0))
     )

time: 989 us -> 972 us (0.983)
  Pallas kernels: 813 us -> 794 us
  transfers between devices with their start and end apart: 4 -> 4, of which waited for: 2 -> 3; matrix products, arithmetic and copies ran while one was open for 1% -> 1% of each run, Pallas kernels for 12% -> 11%
where the time goes in v6:
time: 972 us; the launch traced here: 961 us
  Pallas kernels  794 us (82%)
  matrix products  83.2 us (9%)
  other arithmetic  32.2 us (3%)
  local copies, waits for them, and re-layouts  21.3 us (2%)
  starting transfers between devices  17.3 us (2%)
  waiting for transfers between devices  10.7 us (1%)
    pallas_call x1, Pallas kernels, gather_slots(): pl.pallas_call(partial(gather_body, side, seq_count, plan, slots, images)...  298 us
    pallas_call x1, Pallas kernels, reduce_slots(): pl.pallas_call(partial(reduce_body, side, seq_count, plan, slots), out_sh...  290 us
    pallas_call x7, Pallas kernels, unpack_weight(): pl.pallas_call(partial(unpack_body, base, row // SUBS, per_chunk, tiles,...  63.1 us
    pallas_call x7, Pallas kernels, weight_grad(): pl.pallas_call(partial(weight_grad_body, base, row // SUBS, per_chunk, sh...  60.7 us
    pallas_call x1, Pallas kernels, attention_grad(): pl.pallas_call(partial(attention_grad_body, heads), out_shape=jax.ShapeDt...  28.4 us
  transfers between devices with their start and end apart: 4, of which 3 were waited for; matrix products, arithmetic and copies ran while one was open for 1% of the time, Pallas kernels for 11%

profile of v6, /device:TPU:1, one launch (start us, length us, event | category | flops | bytes accessed | tf_op | source)
XLA Modules:
  0.0 961.5 jit_solution(3330529314146535054)
XLA Ops:
  3.0 1.2 dynamic_slice.22
  6.1 1.4 fusion.27
  10.3 2.8 convert_element_type.188
  13.2 2.6 reshape.632.own_ref
  16.4 298.3 %gather_slots.1 = (bf16[8,4,8256,128]{3,2,1,0:T(8,128)(2,1)}, f32[216,128]{1,0:T(8,128)}, f32[1536,128]{1,0:T(8,128)}) custom-call(bf16[9792,128]{1,0:T(8,128)(2,1)} %reshape.632.own_ref, f32[40,128]{1,0:T(8,128)} %reshape.661.cond_ref, s32[3]{0:T(128)} %pad_add_fusion.1.info_ref), custom_call_target="tpu_custom_call" | custom-call | tf_op jit(solution)/shard_map/gather_slots/pallas_call | solution.py:770
  316.9 2.2 edge_read.1
  319.1 1.4 fusion.48
  321.2 2.1 convolution_bitcast_fusion
  323.3 2.9 copy-done.2
  326.6 9.3 unpack_2.1
  335.9 7.0 fusion.1.x_ref
  342.9 3.4 split_groups_3.1
  346.3 4.4 all-to-all-start
  350.6 5.2 unpack_5.1
  355.9 8.5 unpack_11.1
  364.4 11.2 %unpack_9.1 = bf16[4608,1152]{1,0:T(8,128)(2,1)} custom-call(s32[21]{0:T(128)} %get-tuple-element.95.first_ref, s32[21]{0:T(128)} %get-tuple-element.94.last_ref, s32[33]{0:T(128)} %copy-done.1, s32[32]{0:T(128)} %constant.152.clone.guests_ref, bf16[264192,128]{1,0:T(8,128)(2,1)} %bitcast.11.packed), custom_call_target="tpu_custom_call" | custom-call | bytes 21233664 | tf_op jit(solution)/shard_map/unpack_9/pallas_call | solution.py:146
  375.6 11.3 %unpack_7.1 = bf16[1152,4608]{1,0:T(8,128)(2,1)} custom-call(s32[21]{0:T(128)} %get-tuple-element.95.first_ref, s32[21]{0:T(128)} %get-tuple-element.94.last_ref, s32[33]{0:T(128)} %copy-done.1, s32[32]{0:T(128)} %constant.152.clone.guests_ref, bf16[264192,128]{1,0:T(8,128)(2,1)} %bitcast.11.packed), custom_call_target="tpu_custom_call" | custom-call | bytes 21233664 | tf_op jit(solution)/shard_map/unpack_7/pallas_call | solution.py:146
  388.9 4.0 all-to-all-done
  392.9 1.2 copy-done.3
  394.1 18.4 %attention.1 = bf16[1024,384]{1,0:T(8,128)(2,1)} custom-call(bf16[1024,896]{1,0:T(8,128)(2,1)} %bitcast.156, s32[1024,1]{1,0:T(8,128)} %copy.33.seg_col, s32[1024,1]{1,0:T(8,128)} %copy.34.pad_col, s32[1,1024]{1,0:T(1,128)} %seg_row.3), custom_call_target="tpu_custom_call" | custom-call | tf_op jit(solution)/shard_map/attention/pallas_call | solution.py:1750
  412.5 3.5 all-to-all-start.1
  418.1 4.2 unpack_15.1
  422.4 13.5 %unpack_13.1 = bf16[2048,2048]{1,0:T(8,128)(2,1)} custom-call(s32[21]{0:T(128)} %get-tuple-element.95.first_ref, s32[21]{0:T(128)} %get-tuple-element.94.last_ref, s32[33]{0:T(128)} %copy-done.1, s32[32]{0:T(128)} %constant.152.clone.guests_ref, bf16[264192,128]{1,0:T(8,128)(2,1)} %bitcast.11.packed), custom_call_target="tpu_custom_call" | custom-call | bytes 16777216 | tf_op jit(solution)/shard_map/unpack_13/pallas_call | solution.py:146
  436.8 2.2 join_groups_1.1.x_ref
  439.0 4.3 fusion.81
  443.6 2.1 fusion.36.x_ref
  445.8 11.2 %multiply_convert_fusion = (bf16[256,4608]{1,0:T(8,128)(2,1)S(1)}, f32[256,4608]{1,0:T(8,128)}) fusion(f32[4608]{0:T(1024)S(1)} %fusion.44, bf16[256,1152]{1,0:T(8,128)(2,1)S(1)} %fusion.36.x_ref, bf16[1152,4608]{1,0:T(8,128)(2,1)} %unpack_7.1), kind=kOutput, calls=%fused_computation.18 | convolution fusion | flops 2729705472 | bytes 18302976 | tf_op jit(solution)/shard_map/rtd,df->rtf/dot_general | solution.py:1949
  457.0 4.4 add_convert_fusion
  461.4 3.1 multiply_convert_fusion.2
  464.5 6.1 convolution_add_fusion.4
  470.6 1.6 fusion.76
  472.9 1.3 multiply_reduce_fusion.2
  475.6 2.0 convert_reduce_fusion.2
  477.6 7.9 convert_reduce_fusion.3
  485.5 2.4 convert_reduce_fusion.5
  487.8 9.1 convert_reduce_fusion
  497.0 8.3 multiply_reduce_fusion
  505.8 1.9 convert_reduce_fusion.6
  508.0 1.8 convolution_convert_fusion.1.x_ref
  509.8 2.2 split_groups_1.1
  512.0 4.9 all-to-all-start.2
  516.9 5.5 weight_grad_15.1
  522.5 11.7 %weight_grad_13.1 = (bf16[264192,128]{1,0:T(8,128)(2,1)}, f32[32,128]{1,0:T(8,128)}) custom-call(s32[21]{0:T(128)} %get-tuple-element.95.first_ref, s32[21]{0:T(128)} %get-tuple-element.94.last_ref, s32[33]{0:T(128)} %copy-done.1, s32[32]{0:T(128)} %constant.152.clone.guests_ref, bf16[256,2048]{1,0:T(8,128)(2,1)} %copy-done.22, ...), custom_call_target="tpu_custom_call", output_to_operand_aliasing={{0}: (6, {})} | custom-call | flops 2147483648 | bytes 8388608 | tf_op jit(solution)/shard_map/weight_grad_13/pallas_call | solution.py:345
  534.2 2.5 all-to-all-done.2
  536.7 28.4 %attention_grad.1 = bf16[1024,896]{1,0:T(8,128)(2,1)} custom-call(bf16[1024,896]{1,0:T(8,128)(2,1)} %bitcast.157, bf16[1024,384]{1,0:T(8,128)(2,1)} %bitcast.45.grad_ref, s32[1024,1]{1,0:T(8,128)} %copy.33.seg_col, s32[1024,1]{1,0:T(8,128)} %copy.34.pad_col, s32[1,1024]{1,0:T(1,128)} %seg_row.3), custom_call_target="tpu_custom_call" | custom-call | tf_op jit(solution)/shard_map/attention_grad/pallas_call | solution.py:1812
  565.0 4.5 all-to-all-start.3
  569.6 1.9 pad_add_fusion.2.own_ref
  571.5 8.4 weight_grad_11.1
  579.9 9.8 %weight_grad_9.1 = (bf16[264192,128]{1,0:T(8,128)(2,1)}, f32[32,128]{1,0:T(8,128)}) custom-call(s32[21]{0:T(128)} %get-tuple-element.95.first_ref, s32[21]{0:T(128)} %get-tuple-element.94.last_ref, s32[33]{0:T(128)} %copy-done.1, s32[32]{0:T(128)} %constant.152.clone.guests_ref, bf16[256,4608]{1,0:T(8,128)(2,1)} %copy-done.15, ...), custom_call_target="tpu_custom_call", output_to_operand_aliasing={{0}: (6, {})} | custom-call | flops 2717908992 | bytes 10616832 | tf_op jit(solution)/shard_map/weight_grad_9/pallas_call | solution.py:345
  589.7 10.3 %weight_grad_7.1 = (bf16[264192,128]{1,0:T(8,128)(2,1)}, f32[32,128]{1,0:T(8,128)}) custom-call(s32[21]{0:T(128)} %get-tuple-element.95.first_ref, s32[21]{0:T(128)} %get-tuple-element.94.last_ref, s32[33]{0:T(128)} %copy-done.1, s32[32]{0:T(128)} %constant.152.clone.guests_ref, bf16[256,1152]{1,0:T(8,128)(2,1)} %copy-done.17, ...), custom_call_target="tpu_custom_call", output_to_operand_aliasing={{0}: (6, {})} | custom-call | flops 2717908992 | bytes 10616832 | tf_op jit(solution)/shard_map/weight_grad_7/pallas_call | solution.py:345
  600.0 5.9 weight_grad_5.1
  605.9 1.5 dynamic-slice_convert_fusion.cond_ref
  607.5 4.3 all-to-all-done.3.x_ref
  611.7 3.4 join_groups_3.1.dy_ref
  615.2 1.8 convert_reduce_fusion.1
  616.9 8.1 constant_dynamic-update-slice_fusion.1
  625.0 9.0 weight_grad_2.1
  634.1 3.3 fusion.79
  637.4 1.6 multiply_dynamic-update-slice_fusion.2
  640.1 1.2 multiply_dynamic-update-slice_fusion.1
  642.8 4.2 convolution_convert_fusion
  648.3 2.3 edge_write.1
  650.6 290.4 %reduce_slots.1 = (bf16[9792,128]{1,0:T(8,128)(2,1)}, f32[1728,128]{1,0:T(8,128)}, f32[40,128]{1,0:T(8,128)}) custom-call(bf16[8,4,8256,128]{3,2,1,0:T(8,128)(2,1)} %bitcast.56.parts_ref, bf16[224,128]{1,0:T(8,128)(2,1)} %pad.10.part_ref, bf16[9792,128]{1,0:T(8,128)(2,1)} %reshape.632.own_ref, s32[3]{0:T(128)} %pad_add_fusion.1.info_ref), custom_call_target="tpu_custom_call" | custom-call | tf_op jit(solution)/shard_map/reduce_slots/pallas_call | solution.py:1512
  942.4 18.9 %update.1 = (f32[612,2048]{1,0:T(8,128)}, f32[612,2048]{1,0:T(8,128)}, f32[612,2048]{1,0:T(8,128)}) custom-call(s32[2]{0:T(128)} %pad_add_fusion.2.own_ref, bf16[9792,128]{1,0:T(8,128)(2,1)} %get-tuple-element.86.reduced, bf16[200,32]{1,0:T(8,128)(2,1)} %dynamic-slice_convert_fusion.cond_ref, f32[1728,128]{1,0:T(8,128)} %get-tuple-element.88.mod_ref, ...), custom_call_target="tpu_custom_call" | custom-call | tf_op jit(solution)/shard_map/update/pallas_call | solution.py:1600
  (158 shorter events, 23.0 us)
Async XLA Ops:
  1.6 11.5 %copy-start.1 = (s32[33]{0:T(128)}, s32[33]{0:T(128)S(1)}, u32[]{:S(2)}) copy-start(s32[33]{0:T(128)S(1)} %pad_add_fusion.starts_ref) | copy-start | bytes 400
  6.0 317.3 %copy-start.31 = (f32[256]{0:T(256)}, f32[256]{0:T(256)S(1)}, u32[]{:S(2)}) copy-start(f32[256]{0:T(256)S(1)} %broadcast_multiply_fusion.2) | copy-start | bytes 3076
  7.4 5.7 copy-start.39
  7.4 315.9 %copy-start.37 = (f32[256]{0:T(256)}, f32[256]{0:T(256)S(1)}, u32[]{:S(2)}) copy-start(f32[256]{0:T(256)S(1)} %fusion.60) | copy-start | bytes 3076
  15.8 299.8 %copy-start = (s32[32]{0:T(128)S(1)}, s32[32]{0:T(128)}, u32[]{:S(2)}) copy-start(s32[32]{0:T(128)} %constant.152.clone.guests_ref) | copy-start | bytes 388
  15.8 300.5 %copy-start.45 = (s32[15]{0:T(128)S(1)}, s32[15]{0:T(128)}, u32[]{:S(2)}) copy-start(s32[15]{0:T(128)} %constant.153.clone) | copy-start | bytes 184
  316.9 3.6 copy-start.27
  316.9 3.6 copy-start.43
  316.9 3.6 copy-start.44
  320.5 2.8 copy-start.35
  321.2 5.0 copy-start.4
  323.3 2.9 copy-start.2
  326.6 9.3 copy-start.14
  346.3 46.6 %all-to-all-start = ((bf16[4,256,896]{2,1,0:T(8,128)(2,1)}), bf16[4,256,896]{2,1,0:T(8,128)(2,1)S(1)}, u32[]{:S(2)}, u32[]{:S(2)}) async-start(bf16[4,256,896]{2,1,0:T(8,128)(2,1)} %split_groups_3.1), calls=%async_computation | async-start | bytes 3670016 | tf_op jit(solution)/shard_map/all_to_all | solution.py:1929
  375.5 12.3 %copy-start.42 = (s32[1,1024]{1,0:T(1,128)S(1)}, s32[1,1024]{1,0:T(1,128)}, u32[]{:S(2)}) copy-start(s32[1,1024]{1,0:T(1,128)} %param.16) | copy-start | bytes 12292
  392.9 1.2 copy-start.3
  412.5 23.4 %all-to-all-start.1 = ((bf16[4,256,384]{2,1,0:T(8,128)(2,1)}), bf16[4,256,384]{2,1,0:T(8,128)(2,1)S(1)}, u32[]{:S(2)}, u32[]{:S(2)}) async-start(bf16[4,256,384]{2,1,0:T(8,128)(2,1)} %bitcast.161), calls=%async_computation.1 | async-start | bytes 1572864 | tf_op jit(solution)/shard_map/all_to_all | solution.py:1938
  422.4 16.6 %copy-start.5 = (bf16[1,256,1152]{2,1,0:T(8,128)(2,1)S(1)}, bf16[1,256,1152]{2,1,0:T(8,128)(2,1)}, u32[]{:S(2)}) copy-start(bf16[1,256,1152]{2,1,0:T(8,128)(2,1)} %param.13) | copy-start | bytes 1769476
  422.4 16.6 %copy-start.26 = (f32[1152]{0:T(1024)S(1)}, f32[1152]{0:T(1024)}, u32[]{:S(2)}) copy-start(f32[1152]{0:T(1024)} %get-tuple-element.119) | copy-start | bytes 13828
  435.9 0.9 copy-start.12
  443.3 62.0 %copy-start.29 = (f32[256]{0:T(256)}, f32[256]{0:T(256)S(1)}, u32[]{:S(2)}) copy-start(f32[256]{0:T(256)S(1)} %broadcast_multiply_fusion.1) | copy-start | bytes 3076
  443.3 13.7 %slice-start = ((s8[7077888]{0:T(1024)(128)(4,1)}), s8[4194304]{0:T(1024)(128)(4,1)S(1)}, s32[]{:S(2)}) async-start(s8[7077888]{0:T(1024)(128)(4,1)} %bitcast.152), calls=%async_computation.4 | async-start | bytes 8388608
  443.6 61.7 %copy-start.33 = (f32[256]{0:T(256)}, f32[256]{0:T(256)S(1)}, u32[]{:S(2)}) copy-start(f32[256]{0:T(256)S(1)} %fusion.61) | copy-start | bytes 3076
  443.6 13.4 %slice-start.4 = ((s8[10616832]{0:T(1024)(128)(4,1)}), s8[4194304]{0:T(1024)(128)(4,1)S(1)}, s32[]{:S(2)}) async-start(s8[10616832]{0:T(1024)(128)(4,1)} %bitcast.158), calls=%async_computation.8 | async-start | bytes 8388608
  443.6 17.8 %slice-start.2 = ((s8[4718592]{0:T(1024)(128)(4,1)}), s8[4194304]{0:T(1024)(128)(4,1)S(1)}, s32[]{:S(2)}) async-start(s8[4718592]{0:T(1024)(128)(4,1)} %bitcast.154), calls=%async_computation.6 | async-start | bytes 8388608
  445.7 11.3 %copy-start.17 = (bf16[256,1152]{1,0:T(8,128)(2,1)}, bf16[256,1152]{1,0:T(8,128)(2,1)S(1)}, u32[]{:S(2)}) copy-start(bf16[256,1152]{1,0:T(8,128)(2,1)S(1)} %fusion.36.x_ref) | copy-start | bytes 1769476
  445.7 11.3 %slice-start.1 = ((s8[7077888]{0:T(1024)(128)(4,1)}), s8[2883584]{0:T(1024)(128)(4,1)S(1)}, s32[]{:S(2)}) async-start(s8[7077888]{0:T(1024)(128)(4,1)} %bitcast.152), calls=%async_computation.5 | async-start | bytes 5767168
  445.7 11.3 %slice-start.5 = ((s8[10616832]{0:T(1024)(128)(4,1)}), s8[4194304]{0:T(1024)(128)(4,1)S(1)}, s32[]{:S(2)}) async-start(s8[10616832]{0:T(1024)(128)(4,1)} %bitcast.158), calls=%async_computation.9 | async-start | bytes 8388608
  445.7 11.3 %slice-start.6 = ((s8[10616832]{0:T(1024)(128)(4,1)}), s8[2228224]{0:T(1024)(128)(4,1)S(1)}, s32[]{:S(2)}) async-start(s8[10616832]{0:T(1024)(128)(4,1)} %bitcast.158), calls=%async_computation.10 | async-start | bytes 4456448
  445.7 11.3 %copy-start.41 = (f32[1152]{0:T(1024)S(1)}, f32[1152]{0:T(1024)}, u32[]{:S(2)}) copy-start(f32[1152]{0:T(1024)} %get-tuple-element.118) | copy-start | bytes 13828
  445.8 15.6 %slice-start.3 = ((s8[4718592]{0:T(1024)(128)(4,1)}), s8[524288]{0:T(1024)(128)(4,1)S(1)}, s32[]{:S(2)}) async-start(s8[4718592]{0:T(1024)(128)(4,1)} %bitcast.154), calls=%async_computation.7 | async-start | bytes 1048576
  457.0 4.4 copy-start.15
  461.4 3.1 copy-start.24
  464.5 6.1 copy-start.22
  470.6 2.3 copy-start.11
  472.9 1.3 copy-start.19
  475.6 2.0 copy-start.25
  477.5 7.9 copy-start.23
  477.6 7.9 copy-start.21
  485.5 2.4 copy-start.10
  487.8 9.1 copy-start.18
  497.0 8.3 copy-start.16
  505.8 2.2 copy-start.7
  507.7 2.1 copy-start.13
  512.0 24.6 %all-to-all-start.2 = ((bf16[4,256,384]{2,1,0:T(8,128)(2,1)}), bf16[4,256,384]{2,1,0:T(8,128)(2,1)}, u32[]{:S(2)}, u32[]{:S(2)}) async-start(bf16[4,256,384]{2,1,0:T(8,128)(2,1)} %split_groups_1.1), calls=%async_computation.2 | async-start | bytes 1572864 | tf_op jit(solution)/shard_map/all_to_all | solution.py:2039
  565.0 46.7 %all-to-all-start.3 = ((bf16[4,256,896]{2,1,0:T(8,128)(2,1)}), bf16[4,256,896]{2,1,0:T(8,128)(2,1)}, u32[]{:S(2)}, u32[]{:S(2)}) async-start(bf16[4,256,896]{2,1,0:T(8,128)(2,1)} %bitcast.160), calls=%async_computation.3 | async-start | bytes 3670016 | tf_op jit(solution)/shard_map/all_to_all | solution.py:2049
  611.7 5.2 copy-start.6
  611.7 5.2 copy-start.32
  625.0 9.0 copy-start.40
  625.0 9.1 copy-start.38
  634.1 3.3 copy-start.8
  634.1 3.3 copy-start.9
  639.0 1.1 copy-start.30
  639.0 1.1 copy-start.34
  640.1 1.6 copy-start.20
  641.4 1.4 copy-start.36
  650.6 291.2 %copy-start.28 = (bf16[1,4,1152]{2,1,0:T(4,128)(2,1)S(1)}, bf16[1,4,1152]{2,1,0:T(4,128)(2,1)}, u32[]{:S(2)}) copy-start(bf16[1,4,1152]{2,1,0:T(4,128)(2,1)} %param.14) | copy-start | bytes 27652

commit v7 on v6

--- a/solution.py
+++ b/solution.py
@@ -974,6 +974,7 @@
 COND_STRIDE = D // LANES + 1
 COND_ROWS = SEGS * COND_STRIDE
 FRONT = 56
+SPARE = 64
 MOD_STEPS = 31
 FILL_STEPS = 8
 PRODUCT_STEPS = 9
@@ -1296,7 +1297,7 @@
             pltpu.VMEM((data_count * COND_ROWS, LANES), f32),
             pltpu.VMEM((wide_rows(slots), LANES), f32),
             pltpu.VMEM((LANES, lanes), jnp.bfloat16),
-            pltpu.VMEM((data_count * IMAGE_ROWS, LANES), f32),
+            pltpu.VMEM((data_count * IMAGE_ROWS + SPARE, LANES), f32),
             pltpu.VMEM((LANES, LANES), f32),
         ]
         + gather_sems(side)
@@ -1318,6 +1319,9 @@
             src_ref=part_ref, dst_ref=arrived.at[mine["z"]], send_sem=send_z.at[k], recv_sem=recv_z.at[mine["z"]],
             device_id=grid.device("z", grid.other("z", k)), device_id_type=MESH,
         )
+
+    def done():
+        return pltpu.make_async_copy(summed.at[pl.ds(0, all_ref.shape[0])], all_ref, done_sem)
 
     def run(s):
         spread_modulation(s, own_ref, info_ref, wide)
@@ -1357,7 +1361,7 @@
         @pl.when(s == 9)
         def _():
             gather[3]()
-            pltpu.make_async_copy(summed, all_ref, done_sem).start()
+            done().start()
 
         at_product = s - 10
 
@@ -1398,7 +1402,7 @@
         @pl.when(s == 30)
         def _():
             cond_ref[...] = reduce[4]()
-            pltpu.make_async_copy(summed, all_ref, done_sem).wait()
+            done().wait()
 
     return run
 
@@ -1413,7 +1417,7 @@
     return (
         [
             pltpu.VMEM((depth, SENT_ROWS, LANES), jnp.bfloat16),
-            pltpu.VMEM((data_count * IMAGE_ROWS, LANES), f32),
+            pltpu.VMEM((data_count * IMAGE_ROWS + SPARE, LANES), f32),
             pltpu.VMEM((wide_rows(slots), LANES), f32),
             pltpu.VMEM((2 * (D + 8) + held_depth(slots), LANES), f32),
             pltpu.VMEM((data_count * COND_ROWS, LANES), f32),
@@ -1613,7 +1617,7 @@
             ],
             out_specs=(wide_block,) * 3,
             scratch_shapes=[
-                pltpu.VMEM((mod_depth * MOD_BLOCKS, LANES), jnp.float32),
+                pltpu.VMEM(((mod_depth + 1) * MOD_BLOCKS, LANES), jnp.float32),
                 pltpu.VMEM((tiles * SUBS, LANES), jnp.float32),
             ],
         ),
@@ -1694,7 +1698,7 @@
     )(x)
 
 
-QUERY_BLOCK = 256
+QUERY_BLOCK = 1024
 
 
 def key_bias(seg_col, pad_col, seg_row, first):

time: 972 us -> 964 us (level)
  transfers between devices with their start and end apart: 4 -> 4, of which waited for: 3 -> 3; matrix products, arithmetic and copies ran while one was open for 1% -> 1% of each run, Pallas kernels for 11% -> 12%
where the time goes in v7:
time: 964 us; the launch traced here: 953 us
  Pallas kernels  786 us (82%)
  matrix products  83.2 us (9%)
  other arithmetic  32.4 us (3%)
  local copies, waits for them, and re-layouts  21.3 us (2%)
  starting transfers between devices  16.5 us (2%)
  waiting for transfers between devices  10.6 us (1%)
    pallas_call x1, Pallas kernels, gather_slots(): pl.pallas_call(partial(gather_body, side, seq_count, plan, slots, images)...  298 us
    pallas_call x1, Pallas kernels, reduce_slots(): pl.pallas_call(partial(reduce_body, side, seq_count, plan, slots), out_sh...  290 us
    pallas_call x7, Pallas kernels, unpack_weight(): pl.pallas_call(partial(unpack_body, base, row // SUBS, per_chunk, tiles,...  71.4 us
    pallas_call x7, Pallas kernels, weight_grad(): pl.pallas_call(partial(weight_grad_body, base, row // SUBS, per_chunk, sh...  60.7 us
  transfers between devices with their start and end apart: 4, of which 3 were waited for; matrix products, arithmetic and copies ran while one was open for 1% of the time, Pallas kernels for 12%

profile of v7, /device:TPU:1, one launch (start us, length us, event | category | flops | bytes accessed | tf_op | source)
XLA Modules:
  0.0 952.8 jit_solution(10120643052580432805)
XLA Ops:
  3.0 1.2 dynamic_slice.22
  6.1 1.4 fusion.27
  10.3 2.8 convert_element_type.188
  13.2 2.6 reshape.632.own_ref
  16.4 298.3 %gather_slots.1 = (bf16[8,4,8256,128]{3,2,1,0:T(8,128)(2,1)}, f32[216,128]{1,0:T(8,128)}, f32[1536,128]{1,0:T(8,128)}) custom-call(bf16[9792,128]{1,0:T(8,128)(2,1)} %reshape.632.own_ref, f32[40,128]{1,0:T(8,128)} %reshape.661.cond_ref, s32[3]{0:T(128)} %pad_add_fusion.1.info_ref), custom_call_target="tpu_custom_call" | custom-call | tf_op jit(solution)/shard_map/gather_slots/pallas_call | solution.py:770
  316.9 2.2 edge_read.1
  319.1 1.4 fusion.48
  321.2 2.1 convolution_bitcast_fusion
  323.3 2.9 copy-done.2
  326.6 9.2 unpack_2.1
  335.8 7.0 fusion.1.x_ref
  342.8 3.4 split_groups_3.1
  346.1 4.2 all-to-all-start
  350.3 5.2 unpack_5.1
  355.5 8.5 unpack_11.1
  364.1 11.2 %unpack_9.1 = bf16[4608,1152]{1,0:T(8,128)(2,1)} custom-call(s32[21]{0:T(128)} %get-tuple-element.95.first_ref, s32[21]{0:T(128)} %get-tuple-element.94.last_ref, s32[33]{0:T(128)} %copy-done.1, s32[32]{0:T(128)} %constant.152.clone.guests_ref, bf16[264192,128]{1,0:T(8,128)(2,1)} %bitcast.11.packed), custom_call_target="tpu_custom_call" | custom-call | bytes 21233664 | tf_op jit(solution)/shard_map/unpack_9/pallas_call | solution.py:146
  375.3 11.3 %unpack_7.1 = bf16[1152,4608]{1,0:T(8,128)(2,1)} custom-call(s32[21]{0:T(128)} %get-tuple-element.95.first_ref, s32[21]{0:T(128)} %get-tuple-element.94.last_ref, s32[33]{0:T(128)} %copy-done.1, s32[32]{0:T(128)} %constant.152.clone.guests_ref, bf16[264192,128]{1,0:T(8,128)(2,1)} %bitcast.11.packed), custom_call_target="tpu_custom_call" | custom-call | bytes 21233664 | tf_op jit(solution)/shard_map/unpack_7/pallas_call | solution.py:146
  388.7 3.9 all-to-all-done
  392.6 1.2 copy-done.3
  393.8 11.3 %attention.1 = bf16[1024,384]{1,0:T(8,128)(2,1)} custom-call(bf16[1024,896]{1,0:T(8,128)(2,1)} %bitcast.156, s32[1024,1]{1,0:T(8,128)} %copy.33.seg_col, s32[1024,1]{1,0:T(8,128)} %copy.34.pad_col, s32[1,1024]{1,0:T(1,128)} %seg_row.3), custom_call_target="tpu_custom_call" | custom-call | tf_op jit(solution)/shard_map/attention/pallas_call | solution.py:1754
  405.1 3.5 all-to-all-start.1
  410.7 4.2 unpack_15.1
  415.0 21.8 %unpack_13.1 = bf16[2048,2048]{1,0:T(8,128)(2,1)} custom-call(s32[21]{0:T(128)} %get-tuple-element.95.first_ref, s32[21]{0:T(128)} %get-tuple-element.94.last_ref, s32[33]{0:T(128)} %copy-done.1, s32[32]{0:T(128)} %constant.152.clone.guests_ref, bf16[264192,128]{1,0:T(8,128)(2,1)} %bitcast.11.packed), custom_call_target="tpu_custom_call" | custom-call | bytes 16777216 | tf_op jit(solution)/shard_map/unpack_13/pallas_call | solution.py:146
  437.7 2.2 join_groups_1.1.x_ref
  439.9 4.3 fusion.81
  444.5 2.1 fusion.36.x_ref
  446.7 11.2 %multiply_convert_fusion = (bf16[256,4608]{1,0:T(8,128)(2,1)S(1)}, f32[256,4608]{1,0:T(8,128)}) fusion(f32[4608]{0:T(1024)S(1)} %fusion.44, bf16[256,1152]{1,0:T(8,128)(2,1)S(1)} %fusion.36.x_ref, bf16[1152,4608]{1,0:T(8,128)(2,1)} %unpack_7.1), kind=kOutput, calls=%fused_computation.18 | convolution fusion | flops 2729705472 | bytes 18302976 | tf_op jit(solution)/shard_map/rtd,df->rtf/dot_general | solution.py:1953
  457.9 4.4 add_convert_fusion
  462.3 3.1 multiply_convert_fusion.2
  465.4 6.1 convolution_add_fusion.4
  471.5 1.6 fusion.76
  473.8 1.3 multiply_reduce_fusion.2
  476.6 2.0 convert_reduce_fusion.2
  478.6 7.9 convert_reduce_fusion.3
  486.6 2.4 convert_reduce_fusion.5
  488.9 9.1 convert_reduce_fusion
  498.1 8.3 multiply_reduce_fusion
  506.9 1.9 convert_reduce_fusion.6
  509.1 1.8 convolution_convert_fusion.1.x_ref
  510.9 2.2 split_groups_1.1
  513.1 4.5 all-to-all-start.2
  517.6 5.5 weight_grad_15.1
  523.1 11.8 %weight_grad_13.1 = (bf16[264192,128]{1,0:T(8,128)(2,1)}, f32[32,128]{1,0:T(8,128)}) custom-call(s32[21]{0:T(128)} %get-tuple-element.95.first_ref, s32[21]{0:T(128)} %get-tuple-element.94.last_ref, s32[33]{0:T(128)} %copy-done.1, s32[32]{0:T(128)} %constant.152.clone.guests_ref, bf16[256,2048]{1,0:T(8,128)(2,1)} %copy-done.22, ...), custom_call_target="tpu_custom_call", output_to_operand_aliasing={{0}: (6, {})} | custom-call | flops 2147483648 | bytes 8388608 | tf_op jit(solution)/shard_map/weight_grad_13/pallas_call | solution.py:345
  535.0 2.3 all-to-all-done.2
  537.3 19.0 %attention_grad.1 = bf16[1024,896]{1,0:T(8,128)(2,1)} custom-call(bf16[1024,896]{1,0:T(8,128)(2,1)} %bitcast.157, bf16[1024,384]{1,0:T(8,128)(2,1)} %bitcast.45.grad_ref, s32[1024,1]{1,0:T(8,128)} %copy.33.seg_col, s32[1024,1]{1,0:T(8,128)} %copy.34.pad_col, s32[1,1024]{1,0:T(1,128)} %seg_row.3), custom_call_target="tpu_custom_call" | custom-call | tf_op jit(solution)/shard_map/attention_grad/pallas_call | solution.py:1816
  556.3 4.4 all-to-all-start.3
  560.7 1.9 pad_add_fusion.2.own_ref
  562.6 8.3 weight_grad_11.1
  571.0 9.8 %weight_grad_9.1 = (bf16[264192,128]{1,0:T(8,128)(2,1)}, f32[32,128]{1,0:T(8,128)}) custom-call(s32[21]{0:T(128)} %get-tuple-element.95.first_ref, s32[21]{0:T(128)} %get-tuple-element.94.last_ref, s32[33]{0:T(128)} %copy-done.1, s32[32]{0:T(128)} %constant.152.clone.guests_ref, bf16[256,4608]{1,0:T(8,128)(2,1)} %copy-done.15, ...), custom_call_target="tpu_custom_call", output_to_operand_aliasing={{0}: (6, {})} | custom-call | flops 2717908992 | bytes 10616832 | tf_op jit(solution)/shard_map/weight_grad_9/pallas_call | solution.py:345
  580.8 10.2 %weight_grad_7.1 = (bf16[264192,128]{1,0:T(8,128)(2,1)}, f32[32,128]{1,0:T(8,128)}) custom-call(s32[21]{0:T(128)} %get-tuple-element.95.first_ref, s32[21]{0:T(128)} %get-tuple-element.94.last_ref, s32[33]{0:T(128)} %copy-done.1, s32[32]{0:T(128)} %constant.152.clone.guests_ref, bf16[256,1152]{1,0:T(8,128)(2,1)} %copy-done.17, ...), custom_call_target="tpu_custom_call", output_to_operand_aliasing={{0}: (6, {})} | custom-call | flops 2717908992 | bytes 10616832 | tf_op jit(solution)/shard_map/weight_grad_7/pallas_call | solution.py:345
  591.1 5.9 weight_grad_5.1
  597.0 1.5 dynamic-slice_convert_fusion.cond_ref
  598.5 4.3 all-to-all-done.3.x_ref
  602.9 3.4 join_groups_3.1.dy_ref
  606.3 1.8 convert_reduce_fusion.1
  608.1 8.0 constant_dynamic-update-slice_fusion.1
  616.1 9.1 weight_grad_2.1
  625.3 3.3 fusion.79
  628.6 1.6 multiply_dynamic-update-slice_fusion.2
  631.3 1.2 multiply_dynamic-update-slice_fusion.1
  634.0 4.2 convolution_convert_fusion
  639.5 2.3 edge_write.1
  641.8 290.4 %reduce_slots.1 = (bf16[9792,128]{1,0:T(8,128)(2,1)}, f32[1728,128]{1,0:T(8,128)}, f32[40,128]{1,0:T(8,128)}) custom-call(bf16[8,4,8256,128]{3,2,1,0:T(8,128)(2,1)} %bitcast.56.parts_ref, bf16[224,128]{1,0:T(8,128)(2,1)} %pad.10.part_ref, bf16[9792,128]{1,0:T(8,128)(2,1)} %reshape.632.own_ref, s32[3]{0:T(128)} %pad_add_fusion.1.info_ref), custom_call_target="tpu_custom_call" | custom-call | tf_op jit(solution)/shard_map/reduce_slots/pallas_call | solution.py:1516
  933.6 18.8 %update.1 = (f32[612,2048]{1,0:T(8,128)}, f32[612,2048]{1,0:T(8,128)}, f32[612,2048]{1,0:T(8,128)}) custom-call(s32[2]{0:T(128)} %pad_add_fusion.2.own_ref, bf16[9792,128]{1,0:T(8,128)(2,1)} %get-tuple-element.86.reduced, bf16[200,32]{1,0:T(8,128)(2,1)} %dynamic-slice_convert_fusion.cond_ref, f32[1728,128]{1,0:T(8,128)} %get-tuple-element.88.mod_ref, ...), custom_call_target="tpu_custom_call" | custom-call | tf_op jit(solution)/shard_map/update/pallas_call | solution.py:1604
  (158 shorter events, 23.2 us)
Async XLA Ops:
  1.6 11.5 %copy-start.1 = (s32[33]{0:T(128)}, s32[33]{0:T(128)S(1)}, u32[]{:S(2)}) copy-start(s32[33]{0:T(128)S(1)} %pad_add_fusion.starts_ref) | copy-start | bytes 400
  6.0 317.2 %copy-start.31 = (f32[256]{0:T(256)}, f32[256]{0:T(256)S(1)}, u32[]{:S(2)}) copy-start(f32[256]{0:T(256)S(1)} %broadcast_multiply_fusion.2) | copy-start | bytes 3076
  7.4 5.7 copy-start.39
  7.4 315.9 %copy-start.37 = (f32[256]{0:T(256)}, f32[256]{0:T(256)S(1)}, u32[]{:S(2)}) copy-start(f32[256]{0:T(256)S(1)} %fusion.60) | copy-start | bytes 3076
  15.8 299.8 %copy-start = (s32[32]{0:T(128)S(1)}, s32[32]{0:T(128)}, u32[]{:S(2)}) copy-start(s32[32]{0:T(128)} %constant.152.clone.guests_ref) | copy-start | bytes 388
  15.8 300.5 %copy-start.45 = (s32[15]{0:T(128)S(1)}, s32[15]{0:T(128)}, u32[]{:S(2)}) copy-start(s32[15]{0:T(128)} %constant.153.clone) | copy-start | bytes 184
  316.9 3.6 copy-start.27
  316.9 3.6 copy-start.43
  316.9 3.6 copy-start.44
  320.5 2.8 copy-start.35
  321.2 5.0 copy-start.4
  323.3 2.9 copy-start.2
  326.5 9.2 copy-start.14
  346.1 46.4 %all-to-all-start = ((bf16[4,256,896]{2,1,0:T(8,128)(2,1)}), bf16[4,256,896]{2,1,0:T(8,128)(2,1)S(1)}, u32[]{:S(2)}, u32[]{:S(2)}) async-start(bf16[4,256,896]{2,1,0:T(8,128)(2,1)} %split_groups_3.1), calls=%async_computation | async-start | bytes 3670016 | tf_op jit(solution)/shard_map/all_to_all | solution.py:1933
  375.3 12.4 %copy-start.42 = (s32[1,1024]{1,0:T(1,128)S(1)}, s32[1,1024]{1,0:T(1,128)}, u32[]{:S(2)}) copy-start(s32[1,1024]{1,0:T(1,128)} %param.16) | copy-start | bytes 12292
  392.6 1.2 copy-start.3
  405.1 31.7 %all-to-all-start.1 = ((bf16[4,256,384]{2,1,0:T(8,128)(2,1)}), bf16[4,256,384]{2,1,0:T(8,128)(2,1)S(1)}, u32[]{:S(2)}, u32[]{:S(2)}) async-start(bf16[4,256,384]{2,1,0:T(8,128)(2,1)} %bitcast.161), calls=%async_computation.1 | async-start | bytes 1572864 | tf_op jit(solution)/shard_map/all_to_all | solution.py:1942
  415.0 25.0 %copy-start.5 = (bf16[1,256,1152]{2,1,0:T(8,128)(2,1)S(1)}, bf16[1,256,1152]{2,1,0:T(8,128)(2,1)}, u32[]{:S(2)}) copy-start(bf16[1,256,1152]{2,1,0:T(8,128)(2,1)} %param.13) | copy-start | bytes 1769476
  415.0 25.0 %copy-start.26 = (f32[1152]{0:T(1024)S(1)}, f32[1152]{0:T(1024)}, u32[]{:S(2)}) copy-start(f32[1152]{0:T(1024)} %get-tuple-element.119) | copy-start | bytes 13828
  436.8 0.9 copy-start.12
  444.2 62.2 %copy-start.29 = (f32[256]{0:T(256)}, f32[256]{0:T(256)S(1)}, u32[]{:S(2)}) copy-start(f32[256]{0:T(256)S(1)} %broadcast_multiply_fusion.1) | copy-start | bytes 3076
  444.2 13.6 %slice-start = ((s8[7077888]{0:T(1024)(128)(4,1)}), s8[4194304]{0:T(1024)(128)(4,1)S(1)}, s32[]{:S(2)}) async-start(s8[7077888]{0:T(1024)(128)(4,1)} %bitcast.152), calls=%async_computation.4 | async-start | bytes 8388608
  444.5 61.9 %copy-start.33 = (f32[256]{0:T(256)}, f32[256]{0:T(256)S(1)}, u32[]{:S(2)}) copy-start(f32[256]{0:T(256)S(1)} %fusion.61) | copy-start | bytes 3076
  444.5 13.4 %slice-start.4 = ((s8[10616832]{0:T(1024)(128)(4,1)}), s8[4194304]{0:T(1024)(128)(4,1)S(1)}, s32[]{:S(2)}) async-start(s8[10616832]{0:T(1024)(128)(4,1)} %bitcast.158), calls=%async_computation.8 | async-start | bytes 8388608
  444.5 17.8 %slice-start.2 = ((s8[4718592]{0:T(1024)(128)(4,1)}), s8[4194304]{0:T(1024)(128)(4,1)S(1)}, s32[]{:S(2)}) async-start(s8[4718592]{0:T(1024)(128)(4,1)} %bitcast.154), calls=%async_computation.6 | async-start | bytes 8388608
  446.6 11.2 %copy-start.17 = (bf16[256,1152]{1,0:T(8,128)(2,1)}, bf16[256,1152]{1,0:T(8,128)(2,1)S(1)}, u32[]{:S(2)}) copy-start(bf16[256,1152]{1,0:T(8,128)(2,1)S(1)} %fusion.36.x_ref) | copy-start | bytes 1769476
  446.6 11.2 %slice-start.1 = ((s8[7077888]{0:T(1024)(128)(4,1)}), s8[2883584]{0:T(1024)(128)(4,1)S(1)}, s32[]{:S(2)}) async-start(s8[7077888]{0:T(1024)(128)(4,1)} %bitcast.152), calls=%async_computation.5 | async-start | bytes 5767168
  446.6 11.2 %slice-start.5 = ((s8[10616832]{0:T(1024)(128)(4,1)}), s8[4194304]{0:T(1024)(128)(4,1)S(1)}, s32[]{:S(2)}) async-start(s8[10616832]{0:T(1024)(128)(4,1)} %bitcast.158), calls=%async_computation.9 | async-start | bytes 8388608
  446.6 11.2 %slice-start.6 = ((s8[10616832]{0:T(1024)(128)(4,1)}), s8[2228224]{0:T(1024)(128)(4,1)S(1)}, s32[]{:S(2)}) async-start(s8[10616832]{0:T(1024)(128)(4,1)} %bitcast.158), calls=%async_computation.10 | async-start | bytes 4456448
  446.6 11.2 %copy-start.41 = (f32[1152]{0:T(1024)S(1)}, f32[1152]{0:T(1024)}, u32[]{:S(2)}) copy-start(f32[1152]{0:T(1024)} %get-tuple-element.118) | copy-start | bytes 13828
  446.6 15.6 %slice-start.3 = ((s8[4718592]{0:T(1024)(128)(4,1)}), s8[524288]{0:T(1024)(128)(4,1)S(1)}, s32[]{:S(2)}) async-start(s8[4718592]{0:T(1024)(128)(4,1)} %bitcast.154), calls=%async_computation.7 | async-start | bytes 1048576
  457.8 4.4 copy-start.15
  462.3 3.1 copy-start.24
  465.4 6.1 copy-start.22
  471.5 2.3 copy-start.11
  473.8 1.3 copy-start.19
  476.6 2.0 copy-start.25
  478.6 7.9 copy-start.23
  478.6 7.9 copy-start.21
  486.5 2.4 copy-start.10
  488.9 9.1 copy-start.18
  498.1 8.3 copy-start.16
  506.9 2.2 copy-start.7
  508.8 2.1 copy-start.13
  513.1 24.2 %all-to-all-start.2 = ((bf16[4,256,384]{2,1,0:T(8,128)(2,1)}), bf16[4,256,384]{2,1,0:T(8,128)(2,1)}, u32[]{:S(2)}, u32[]{:S(2)}) async-start(bf16[4,256,384]{2,1,0:T(8,128)(2,1)} %split_groups_1.1), calls=%async_computation.2 | async-start | bytes 1572864 | tf_op jit(solution)/shard_map/all_to_all | solution.py:2043
  556.3 46.5 %all-to-all-start.3 = ((bf16[4,256,896]{2,1,0:T(8,128)(2,1)}), bf16[4,256,896]{2,1,0:T(8,128)(2,1)}, u32[]{:S(2)}, u32[]{:S(2)}) async-start(bf16[4,256,896]{2,1,0:T(8,128)(2,1)} %bitcast.160), calls=%async_computation.3 | async-start | bytes 3670016 | tf_op jit(solution)/shard_map/all_to_all | solution.py:2053
  602.9 5.2 copy-start.6
  602.9 5.2 copy-start.32
  616.1 9.1 copy-start.40
  616.1 9.1 copy-start.38
  625.3 3.3 copy-start.8
  625.3 3.3 copy-start.9
  630.2 1.1 copy-start.30
  630.2 1.1 copy-start.34
  631.3 1.6 copy-start.20
  632.6 1.4 copy-start.36
  641.8 291.2 %copy-start.28 = (bf16[1,4,1152]{2,1,0:T(4,128)(2,1)S(1)}, bf16[1,4,1152]{2,1,0:T(4,128)(2,1)}, u32[]{:S(2)}) copy-start(bf16[1,4,1152]{2,1,0:T(4,128)(2,1)} %param.14) | copy-start | bytes 27652

commit v8 on v7

--- a/solution.py
+++ b/solution.py
@@ -1539,7 +1539,7 @@
     )(grads.reshape(data_count, seq_count, kept * SUBS, LANES), mod_part, own, info)
 
 
-UPDATE_TILES = 72
+UPDATE_TILES = 104
 
 
 def update_body(mod_depth, own_ref, reduced, cond_ref, mod_ref, master, first, second,

time: 964 us -> 962 us (level)
  no operation moved by 1% of the time
where the time goes in v8:
time: 962 us; the launch traced here: 952 us
  Pallas kernels  785 us (82%)
  matrix products  83.2 us (9%)
  other arithmetic  32.3 us (3%)
  local copies, waits for them, and re-layouts  21.3 us (2%)
  starting transfers between devices  16.5 us (2%)
  waiting for transfers between devices  10.5 us (1%)
    pallas_call x1, Pallas kernels, gather_slots(): pl.pallas_call(partial(gather_body, side, seq_count, plan, slots, images)...  298 us
    pallas_call x1, Pallas kernels, reduce_slots(): pl.pallas_call(partial(reduce_body, side, seq_count, plan, slots), out_sh...  290 us
    pallas_call x7, Pallas kernels, unpack_weight(): pl.pallas_call(partial(unpack_body, base, row // SUBS, per_chunk, tiles,...  71.5 us
    pallas_call x7, Pallas kernels, weight_grad(): pl.pallas_call(partial(weight_grad_body, base, row // SUBS, per_chunk, sh...  60.8 us
  transfers between devices with their start and end apart: 4, of which 3 were waited for; matrix products, arithmetic and copies ran while one was open for 1% of the time, Pallas kernels for 12%

profile of v8, /device:TPU:1, one launch (start us, length us, event | category | flops | bytes accessed | tf_op | source)
XLA Modules:
  0.0 951.6 jit_solution(10205602209391348317)
XLA Ops:
  3.0 1.2 dynamic_slice.22
  6.1 1.4 fusion.27
  10.3 2.8 convert_element_type.188
  13.2 2.6 reshape.632.own_ref
  16.4 298.3 %gather_slots.1 = (bf16[8,4,8256,128]{3,2,1,0:T(8,128)(2,1)}, f32[216,128]{1,0:T(8,128)}, f32[1536,128]{1,0:T(8,128)}) custom-call(bf16[9792,128]{1,0:T(8,128)(2,1)} %reshape.632.own_ref, f32[40,128]{1,0:T(8,128)} %reshape.661.cond_ref, s32[3]{0:T(128)} %pad_add_fusion.1.info_ref), custom_call_target="tpu_custom_call" | custom-call | tf_op jit(solution)/shard_map/gather_slots/pallas_call | solution.py:770
  316.9 2.2 edge_read.1
  319.1 1.4 fusion.48
  321.2 2.1 convolution_bitcast_fusion
  323.3 2.9 copy-done.2
  326.6 9.2 unpack_2.1
  335.8 7.0 fusion.1.x_ref
  342.8 3.4 split_groups_3.1
  346.2 4.2 all-to-all-start
  350.4 5.2 unpack_5.1
  355.6 8.5 unpack_11.1
  364.1 11.3 %unpack_9.1 = bf16[4608,1152]{1,0:T(8,128)(2,1)} custom-call(s32[21]{0:T(128)} %get-tuple-element.95.first_ref, s32[21]{0:T(128)} %get-tuple-element.94.last_ref, s32[33]{0:T(128)} %copy-done.1, s32[32]{0:T(128)} %constant.152.clone.guests_ref, bf16[264192,128]{1,0:T(8,128)(2,1)} %bitcast.11.packed), custom_call_target="tpu_custom_call" | custom-call | bytes 21233664 | tf_op jit(solution)/shard_map/unpack_9/pallas_call | solution.py:146
  375.3 11.4 %unpack_7.1 = bf16[1152,4608]{1,0:T(8,128)(2,1)} custom-call(s32[21]{0:T(128)} %get-tuple-element.95.first_ref, s32[21]{0:T(128)} %get-tuple-element.94.last_ref, s32[33]{0:T(128)} %copy-done.1, s32[32]{0:T(128)} %constant.152.clone.guests_ref, bf16[264192,128]{1,0:T(8,128)(2,1)} %bitcast.11.packed), custom_call_target="tpu_custom_call" | custom-call | bytes 21233664 | tf_op jit(solution)/shard_map/unpack_7/pallas_call | solution.py:146
  388.8 3.8 all-to-all-done
  392.6 1.2 copy-done.3
  393.9 11.3 %attention.1 = bf16[1024,384]{1,0:T(8,128)(2,1)} custom-call(bf16[1024,896]{1,0:T(8,128)(2,1)} %bitcast.156, s32[1024,1]{1,0:T(8,128)} %copy.33.seg_col, s32[1024,1]{1,0:T(8,128)} %copy.34.pad_col, s32[1,1024]{1,0:T(1,128)} %seg_row.3), custom_call_target="tpu_custom_call" | custom-call | tf_op jit(solution)/shard_map/attention/pallas_call | solution.py:1754
  405.1 3.5 all-to-all-start.1
  410.8 4.2 unpack_15.1
  415.0 21.8 %unpack_13.1 = bf16[2048,2048]{1,0:T(8,128)(2,1)} custom-call(s32[21]{0:T(128)} %get-tuple-element.95.first_ref, s32[21]{0:T(128)} %get-tuple-element.94.last_ref, s32[33]{0:T(128)} %copy-done.1, s32[32]{0:T(128)} %constant.152.clone.guests_ref, bf16[264192,128]{1,0:T(8,128)(2,1)} %bitcast.11.packed), custom_call_target="tpu_custom_call" | custom-call | bytes 16777216 | tf_op jit(solution)/shard_map/unpack_13/pallas_call | solution.py:146
  437.7 2.2 join_groups_1.1.x_ref
  439.9 4.3 fusion.81
  444.5 2.1 fusion.36.x_ref
  446.7 11.2 %multiply_convert_fusion = (bf16[256,4608]{1,0:T(8,128)(2,1)S(1)}, f32[256,4608]{1,0:T(8,128)}) fusion(f32[4608]{0:T(1024)S(1)} %fusion.44, bf16[256,1152]{1,0:T(8,128)(2,1)S(1)} %fusion.36.x_ref, bf16[1152,4608]{1,0:T(8,128)(2,1)} %unpack_7.1), kind=kOutput, calls=%fused_computation.18 | convolution fusion | flops 2729705472 | bytes 18302976 | tf_op jit(solution)/shard_map/rtd,df->rtf/dot_general | solution.py:1953
  457.9 4.4 add_convert_fusion
  462.3 3.1 multiply_convert_fusion.2
  465.4 6.1 convolution_add_fusion.4
  471.6 1.6 fusion.76
  473.8 1.3 multiply_reduce_fusion.2
  476.7 2.0 convert_reduce_fusion.2
  478.7 7.9 convert_reduce_fusion.3
  486.6 2.4 convert_reduce_fusion.5
  489.0 9.1 convert_reduce_fusion
  498.1 8.3 multiply_reduce_fusion
  506.9 1.9 convert_reduce_fusion.6
  509.1 1.8 convolution_convert_fusion.1.x_ref
  510.9 2.2 split_groups_1.1
  513.2 4.5 all-to-all-start.2
  517.6 5.5 weight_grad_15.1
  523.2 11.8 %weight_grad_13.1 = (bf16[264192,128]{1,0:T(8,128)(2,1)}, f32[32,128]{1,0:T(8,128)}) custom-call(s32[21]{0:T(128)} %get-tuple-element.95.first_ref, s32[21]{0:T(128)} %get-tuple-element.94.last_ref, s32[33]{0:T(128)} %copy-done.1, s32[32]{0:T(128)} %constant.152.clone.guests_ref, bf16[256,2048]{1,0:T(8,128)(2,1)} %copy-done.22, ...), custom_call_target="tpu_custom_call", output_to_operand_aliasing={{0}: (6, {})} | custom-call | flops 2147483648 | bytes 8388608 | tf_op jit(solution)/shard_map/weight_grad_13/pallas_call | solution.py:345
  535.0 2.4 all-to-all-done.2
  537.4 19.0 %attention_grad.1 = bf16[1024,896]{1,0:T(8,128)(2,1)} custom-call(bf16[1024,896]{1,0:T(8,128)(2,1)} %bitcast.157, bf16[1024,384]{1,0:T(8,128)(2,1)} %bitcast.45.grad_ref, s32[1024,1]{1,0:T(8,128)} %copy.33.seg_col, s32[1024,1]{1,0:T(8,128)} %copy.34.pad_col, s32[1,1024]{1,0:T(1,128)} %seg_row.3), custom_call_target="tpu_custom_call" | custom-call | tf_op jit(solution)/shard_map/attention_grad/pallas_call | solution.py:1816
  556.4 4.4 all-to-all-start.3
  560.8 1.8 pad_add_fusion.2.own_ref
  562.6 8.4 weight_grad_11.1
  571.0 9.8 %weight_grad_9.1 = (bf16[264192,128]{1,0:T(8,128)(2,1)}, f32[32,128]{1,0:T(8,128)}) custom-call(s32[21]{0:T(128)} %get-tuple-element.95.first_ref, s32[21]{0:T(128)} %get-tuple-element.94.last_ref, s32[33]{0:T(128)} %copy-done.1, s32[32]{0:T(128)} %constant.152.clone.guests_ref, bf16[256,4608]{1,0:T(8,128)(2,1)} %copy-done.15, ...), custom_call_target="tpu_custom_call", output_to_operand_aliasing={{0}: (6, {})} | custom-call | flops 2717908992 | bytes 10616832 | tf_op jit(solution)/shard_map/weight_grad_9/pallas_call | solution.py:345
  580.8 10.3 %weight_grad_7.1 = (bf16[264192,128]{1,0:T(8,128)(2,1)}, f32[32,128]{1,0:T(8,128)}) custom-call(s32[21]{0:T(128)} %get-tuple-element.95.first_ref, s32[21]{0:T(128)} %get-tuple-element.94.last_ref, s32[33]{0:T(128)} %copy-done.1, s32[32]{0:T(128)} %constant.152.clone.guests_ref, bf16[256,1152]{1,0:T(8,128)(2,1)} %copy-done.17, ...), custom_call_target="tpu_custom_call", output_to_operand_aliasing={{0}: (6, {})} | custom-call | flops 2717908992 | bytes 10616832 | tf_op jit(solution)/shard_map/weight_grad_7/pallas_call | solution.py:345
  591.2 5.9 weight_grad_5.1
  597.1 1.5 dynamic-slice_convert_fusion.cond_ref
  598.6 4.2 all-to-all-done.3.x_ref
  602.9 3.4 join_groups_3.1.dy_ref
  606.3 1.8 convert_reduce_fusion.1
  608.1 8.0 constant_dynamic-update-slice_fusion.1
  616.2 9.0 weight_grad_2.1
  625.3 3.3 fusion.79
  628.6 1.6 multiply_dynamic-update-slice_fusion.2
  631.3 1.2 multiply_dynamic-update-slice_fusion.1
  634.0 4.2 convolution_convert_fusion
  639.4 2.3 edge_write.1
  641.8 290.4 %reduce_slots.1 = (bf16[9792,128]{1,0:T(8,128)(2,1)}, f32[1728,128]{1,0:T(8,128)}, f32[40,128]{1,0:T(8,128)}) custom-call(bf16[8,4,8256,128]{3,2,1,0:T(8,128)(2,1)} %bitcast.56.parts_ref, bf16[224,128]{1,0:T(8,128)(2,1)} %pad.10.part_ref, bf16[9792,128]{1,0:T(8,128)(2,1)} %reshape.632.own_ref, s32[3]{0:T(128)} %pad_add_fusion.1.info_ref), custom_call_target="tpu_custom_call" | custom-call | tf_op jit(solution)/shard_map/reduce_slots/pallas_call | solution.py:1516
  933.5 17.6 %update.1 = (f32[612,2048]{1,0:T(8,128)}, f32[612,2048]{1,0:T(8,128)}, f32[612,2048]{1,0:T(8,128)}) custom-call(s32[2]{0:T(128)} %pad_add_fusion.2.own_ref, bf16[9792,128]{1,0:T(8,128)(2,1)} %get-tuple-element.86.reduced, bf16[192,32]{1,0:T(8,128)(2,1)} %dynamic-slice_convert_fusion.cond_ref, f32[1728,128]{1,0:T(8,128)} %get-tuple-element.88.mod_ref, ...), custom_call_target="tpu_custom_call" | custom-call | tf_op jit(solution)/shard_map/update/pallas_call | solution.py:1604
  (158 shorter events, 23.2 us)
Async XLA Ops:
  1.6 11.5 %copy-start.1 = (s32[33]{0:T(128)}, s32[33]{0:T(128)S(1)}, u32[]{:S(2)}) copy-start(s32[33]{0:T(128)S(1)} %pad_add_fusion.starts_ref) | copy-start | bytes 400
  6.0 317.2 %copy-start.31 = (f32[256]{0:T(256)}, f32[256]{0:T(256)S(1)}, u32[]{:S(2)}) copy-start(f32[256]{0:T(256)S(1)} %broadcast_multiply_fusion.2) | copy-start | bytes 3076
  7.4 5.7 copy-start.39
  7.4 315.9 %copy-start.37 = (f32[256]{0:T(256)}, f32[256]{0:T(256)S(1)}, u32[]{:S(2)}) copy-start(f32[256]{0:T(256)S(1)} %fusion.60) | copy-start | bytes 3076
  15.8 299.8 %copy-start = (s32[32]{0:T(128)S(1)}, s32[32]{0:T(128)}, u32[]{:S(2)}) copy-start(s32[32]{0:T(128)} %constant.152.clone.guests_ref) | copy-start | bytes 388
  15.8 300.5 %copy-start.45 = (s32[15]{0:T(128)S(1)}, s32[15]{0:T(128)}, u32[]{:S(2)}) copy-start(s32[15]{0:T(128)} %constant.153.clone) | copy-start | bytes 184
  316.9 3.6 copy-start.27
  316.9 3.6 copy-start.43
  316.9 3.6 copy-start.44
  320.5 2.8 copy-start.35
  321.2 5.0 copy-start.4
  323.3 2.9 copy-start.2
  326.6 9.3 copy-start.14
  346.2 46.4 %all-to-all-start = ((bf16[4,256,896]{2,1,0:T(8,128)(2,1)}), bf16[4,256,896]{2,1,0:T(8,128)(2,1)S(1)}, u32[]{:S(2)}, u32[]{:S(2)}) async-start(bf16[4,256,896]{2,1,0:T(8,128)(2,1)} %split_groups_3.1), calls=%async_computation | async-start | bytes 3670016 | tf_op jit(solution)/shard_map/all_to_all | solution.py:1933
  375.3 12.4 %copy-start.42 = (s32[1,1024]{1,0:T(1,128)S(1)}, s32[1,1024]{1,0:T(1,128)}, u32[]{:S(2)}) copy-start(s32[1,1024]{1,0:T(1,128)} %param.16) | copy-start | bytes 12292
  392.6 1.2 copy-start.3
  405.1 31.7 %all-to-all-start.1 = ((bf16[4,256,384]{2,1,0:T(8,128)(2,1)}), bf16[4,256,384]{2,1,0:T(8,128)(2,1)S(1)}, u32[]{:S(2)}, u32[]{:S(2)}) async-start(bf16[4,256,384]{2,1,0:T(8,128)(2,1)} %bitcast.161), calls=%async_computation.1 | async-start | bytes 1572864 | tf_op jit(solution)/shard_map/all_to_all | solution.py:1942
  415.0 24.9 %copy-start.5 = (bf16[1,256,1152]{2,1,0:T(8,128)(2,1)S(1)}, bf16[1,256,1152]{2,1,0:T(8,128)(2,1)}, u32[]{:S(2)}) copy-start(bf16[1,256,1152]{2,1,0:T(8,128)(2,1)} %param.13) | copy-start | bytes 1769476
  415.0 24.9 %copy-start.26 = (f32[1152]{0:T(1024)S(1)}, f32[1152]{0:T(1024)}, u32[]{:S(2)}) copy-start(f32[1152]{0:T(1024)} %get-tuple-element.119) | copy-start | bytes 13828
  436.8 0.9 copy-start.12
  444.2 62.2 %copy-start.29 = (f32[256]{0:T(256)}, f32[256]{0:T(256)S(1)}, u32[]{:S(2)}) copy-start(f32[256]{0:T(256)S(1)} %broadcast_multiply_fusion.1) | copy-start | bytes 3076
  444.2 13.7 %slice-start = ((s8[7077888]{0:T(1024)(128)(4,1)}), s8[4194304]{0:T(1024)(128)(4,1)S(1)}, s32[]{:S(2)}) async-start(s8[7077888]{0:T(1024)(128)(4,1)} %bitcast.152), calls=%async_computation.4 | async-start | bytes 8388608
  444.5 61.9 %copy-start.33 = (f32[256]{0:T(256)}, f32[256]{0:T(256)S(1)}, u32[]{:S(2)}) copy-start(f32[256]{0:T(256)S(1)} %fusion.61) | copy-start | bytes 3076
  444.5 13.4 %slice-start.4 = ((s8[10616832]{0:T(1024)(128)(4,1)}), s8[4194304]{0:T(1024)(128)(4,1)S(1)}, s32[]{:S(2)}) async-start(s8[10616832]{0:T(1024)(128)(4,1)} %bitcast.158), calls=%async_computation.8 | async-start | bytes 8388608
  444.5 17.8 %slice-start.2 = ((s8[4718592]{0:T(1024)(128)(4,1)}), s8[4194304]{0:T(1024)(128)(4,1)S(1)}, s32[]{:S(2)}) async-start(s8[4718592]{0:T(1024)(128)(4,1)} %bitcast.154), calls=%async_computation.6 | async-start | bytes 8388608
  446.6 11.3 %copy-start.17 = (bf16[256,1152]{1,0:T(8,128)(2,1)}, bf16[256,1152]{1,0:T(8,128)(2,1)S(1)}, u32[]{:S(2)}) copy-start(bf16[256,1152]{1,0:T(8,128)(2,1)S(1)} %fusion.36.x_ref) | copy-start | bytes 1769476
  446.6 11.3 %slice-start.1 = ((s8[7077888]{0:T(1024)(128)(4,1)}), s8[2883584]{0:T(1024)(128)(4,1)S(1)}, s32[]{:S(2)}) async-start(s8[7077888]{0:T(1024)(128)(4,1)} %bitcast.152), calls=%async_computation.5 | async-start | bytes 5767168
  446.6 11.3 %slice-start.5 = ((s8[10616832]{0:T(1024)(128)(4,1)}), s8[4194304]{0:T(1024)(128)(4,1)S(1)}, s32[]{:S(2)}) async-start(s8[10616832]{0:T(1024)(128)(4,1)} %bitcast.158), calls=%async_computation.9 | async-start | bytes 8388608
  446.6 11.3 %slice-start.6 = ((s8[10616832]{0:T(1024)(128)(4,1)}), s8[2228224]{0:T(1024)(128)(4,1)S(1)}, s32[]{:S(2)}) async-start(s8[10616832]{0:T(1024)(128)(4,1)} %bitcast.158), calls=%async_computation.10 | async-start | bytes 4456448
  446.7 11.3 %copy-start.41 = (f32[1152]{0:T(1024)S(1)}, f32[1152]{0:T(1024)}, u32[]{:S(2)}) copy-start(f32[1152]{0:T(1024)} %get-tuple-element.118) | copy-start | bytes 13828
  446.7 15.6 %slice-start.3 = ((s8[4718592]{0:T(1024)(128)(4,1)}), s8[524288]{0:T(1024)(128)(4,1)S(1)}, s32[]{:S(2)}) async-start(s8[4718592]{0:T(1024)(128)(4,1)} %bitcast.154), calls=%async_computation.7 | async-start | bytes 1048576
  457.9 4.4 copy-start.15
  462.3 3.1 copy-start.24
  465.4 6.1 copy-start.22
  471.5 2.3 copy-start.11
  473.8 1.3 copy-start.19
  476.7 2.0 copy-start.25
  478.7 7.9 copy-start.23
  478.7 7.9 copy-start.21
  486.6 2.4 copy-start.10
  489.0 9.1 copy-start.18
  498.1 8.3 copy-start.16
  506.9 2.2 copy-start.7
  508.8 2.1 copy-start.13
  513.2 24.2 %all-to-all-start.2 = ((bf16[4,256,384]{2,1,0:T(8,128)(2,1)}), bf16[4,256,384]{2,1,0:T(8,128)(2,1)}, u32[]{:S(2)}, u32[]{:S(2)}) async-start(bf16[4,256,384]{2,1,0:T(8,128)(2,1)} %split_groups_1.1), calls=%async_computation.2 | async-start | bytes 1572864 | tf_op jit(solution)/shard_map/all_to_all | solution.py:2043
  556.4 46.5 %all-to-all-start.3 = ((bf16[4,256,896]{2,1,0:T(8,128)(2,1)}), bf16[4,256,896]{2,1,0:T(8,128)(2,1)}, u32[]{:S(2)}, u32[]{:S(2)}) async-start(bf16[4,256,896]{2,1,0:T(8,128)(2,1)} %bitcast.160), calls=%async_computation.3 | async-start | bytes 3670016 | tf_op jit(solution)/shard_map/all_to_all | solution.py:2053
  602.9 5.2 copy-start.6
  602.9 5.2 copy-start.32
  616.2 9.0 copy-start.40
  616.2 9.1 copy-start.38
  625.2 3.3 copy-start.8
  625.2 3.3 copy-start.9
  630.2 1.1 copy-start.30
  630.2 1.1 copy-start.34
  631.3 1.6 copy-start.20
  632.5 1.4 copy-start.36
  641.7 291.2 %copy-start.28 = (bf16[1,4,1152]{2,1,0:T(4,128)(2,1)S(1)}, bf16[1,4,1152]{2,1,0:T(4,128)(2,1)}, u32[]{:S(2)}) copy-start(bf16[1,4,1152]{2,1,0:T(4,128)(2,1)} %param.14) | copy-start | bytes 27652
